TPU v7x, 256 devices: a whole 4x4x8 slice. The times are simulated.
256 devices in a mesh: seq: 32 (over z_hi, y, x), chan: 8 (over z_lo, core).
Axes of the slice: x: 4, y: 4, z: 8 (z_hi: 2, z_lo: 4; z = z_hi * 4 + z_lo), core: 2. Of those that a mesh axis runs over, the one named last changes fastest.
Arguments:
- query_branch: bfloat16 [4096, 8192], P('seq', 'chan'), may hold values from -6 to 6
- key_branch: bfloat16 [4096, 8192], P('seq', 'chan'), may hold values from -6 to 6
- value_branch: bfloat16 [4096, 8192], P('seq', 'chan'), may hold values from -6 to 6
- short_filter: float32 [3, 3, 8192], P(None, None, 'chan'), may hold values from -1 to 1
- long_filter: float32 [8192, 4096], P(('chan', 'seq')), may hold values from -1.1 to 1.1
- out_weight: bfloat16 [8192, 8192], P('chan', 'seq'), may hold values from -0.0625 to 0.0625
- cotangent: bfloat16 [4096, 8192], P('seq', 'chan'), may hold values from -6 to 6
Outputs:
- block_output: bfloat16 [4096, 8192], P('seq', 'chan')
- query_grad: bfloat16 [4096, 8192], P('seq', 'chan')
- key_grad: bfloat16 [4096, 8192], P('seq', 'chan')
- value_grad: bfloat16 [4096, 8192], P('seq', 'chan')
- filter_grad: float32 [8192, 4096], P(('chan', 'seq'))
All inputs are finite; a program needn't handle non-finite values.
Results may differ from a plain program's by a relative error of at most 0.017.
Values may be sent and summed in bfloat16 or wider, within the bound.
No kernel may reach another device: no remote copies, remote signals or barrier semaphores. Data moves between devices by JAX's collectives and lax.ppermute only.
A program may use at most 128 MiB of HBM per device.

v0:
```python
import math

import jax
import jax.numpy as jnp
from jax import lax
from jax.sharding import PartitionSpec as P

exact_mode = lax.Precision.HIGHEST


def rounded(value):
    return lax.optimization_barrier(value.astype(jnp.bfloat16)).astype(jnp.float32)


def angle_table(first_count, second_count, period):
    first = jnp.arange(first_count, dtype=jnp.int32)[:, None]
    second = jnp.arange(second_count, dtype=jnp.int32)[None, :]
    turns = first * second % period
    angle = turns.astype(jnp.float32) * (2.0 * math.pi / period)
    return (jnp.cos(angle), jnp.sin(angle))


def make_plan(length):
    total = 2 * length
    order = total.bit_length() - 1
    rows_count = 2 ** (order // 2)
    cols_count = total // rows_count
    cosine_rows, sine_rows = angle_table(rows_count, rows_count // 2, rows_count)
    cosine_cols, sine_cols = angle_table(cols_count, cols_count, cols_count)
    twist_cos, twist_sin = angle_table(rows_count, cols_count, total)
    return (cosine_rows, sine_rows, cosine_cols, sine_cols, twist_cos, twist_sin)


def forward_dft(signal, transform_plan):
    cosine_rows, sine_rows, cosine_cols, sine_cols, twist_cos, twist_sin = transform_plan
    shaped = signal.reshape(signal.shape[0], cosine_rows.shape[1], cosine_cols.shape[0])
    first_re = jnp.einsum("kn,bnm->bkm", cosine_rows, shaped, precision=exact_mode)
    first_im = -jnp.einsum("kn,bnm->bkm", sine_rows, shaped, precision=exact_mode)
    turned_re = first_re * twist_cos + first_im * twist_sin
    turned_im = first_im * twist_cos - first_re * twist_sin
    real_part = jnp.einsum(
        "bkn,nm->bkm", turned_re, cosine_cols, precision=exact_mode
    ) + jnp.einsum("bkn,nm->bkm", turned_im, sine_cols, precision=exact_mode)
    imag_part = jnp.einsum(
        "bkn,nm->bkm", turned_im, cosine_cols, precision=exact_mode
    ) - jnp.einsum("bkn,nm->bkm", turned_re, sine_cols, precision=exact_mode)
    return (real_part, imag_part)


def inverse_dft(spectrum, transform_plan):
    cosine_rows, sine_rows, cosine_cols, sine_cols, twist_cos, twist_sin = transform_plan
    real_part, imag_part = spectrum
    up_re = jnp.einsum("bkn,nm->bkm", real_part, cosine_cols, precision=exact_mode) - jnp.einsum(
        "bkn,nm->bkm", imag_part, sine_cols, precision=exact_mode
    )
    up_im = jnp.einsum("bkn,nm->bkm", real_part, sine_cols, precision=exact_mode) + jnp.einsum(
        "bkn,nm->bkm", imag_part, cosine_cols, precision=exact_mode
    )
    back_re = up_re * twist_cos - up_im * twist_sin
    back_im = up_re * twist_sin + up_im * twist_cos
    result = jnp.einsum("kn,bkm->bnm", cosine_rows, back_re, precision=exact_mode) - jnp.einsum(
        "kn,bkm->bnm", sine_rows, back_im, precision=exact_mode
    )
    total = 2 * cosine_rows.shape[1] * cosine_cols.shape[0]
    return result.reshape(result.shape[0], -1) / total


def multiply(first, second, conjugate):
    first_re, first_im = first
    second_re, second_im = second
    if conjugate:
        return (
            first_re * second_re + first_im * second_im,
            first_im * second_re - first_re * second_im,
        )
    return (
        first_re * second_re - first_im * second_im,
        first_re * second_im + first_im * second_re,
    )


def causal_along(signal, weights):
    extent = signal.shape[1]
    joined = jnp.pad(signal, ((0, 0), (2, 0)))
    return (
        weights[0][:, None] * joined[:, 2:]
        + weights[1][:, None] * joined[:, 1 : extent + 1]
        + weights[2][:, None] * joined[:, :extent]
    )


def adjoint_along(signal, weights):
    extent = signal.shape[1]
    joined = jnp.pad(signal, ((0, 0), (0, 2)))
    return (
        weights[0][:, None] * joined[:, :extent]
        + weights[1][:, None] * joined[:, 1 : extent + 1]
        + weights[2][:, None] * joined[:, 2:]
    )


def shards(
    query_branch, key_branch, value_branch, short_filter, long_filter, out_weight, cotangent
):
    tokens_here, local_width = query_branch.shape
    seq_count = lax.axis_size("seq")
    length = tokens_here * seq_count
    chan_width = local_width // seq_count
    transform_plan = make_plan(length)
    weight_rows = lax.all_gather(out_weight, "seq", axis=1, tiled=True)
    filter_spec = forward_dft(long_filter, transform_plan)
    stacked = jnp.stack([query_branch.T, key_branch.T, value_branch.T])
    columns = lax.all_to_all(stacked, "seq", split_axis=1, concat_axis=2, tiled=True).astype(
        jnp.float32
    )
    local_taps = lax.dynamic_slice_in_dim(
        short_filter, lax.axis_index("seq") * chan_width, chan_width, 2
    )
    query_conv = causal_along(columns[0], local_taps[:, 0])
    key_conv = causal_along(columns[1], local_taps[:, 1])
    value_conv = causal_along(columns[2], local_taps[:, 2])
    gated_cols = rounded(key_conv * value_conv)
    gated_spec = forward_dft(gated_cols, transform_plan)
    mixed = rounded(inverse_dft(multiply(gated_spec, filter_spec, False), transform_plan))
    product_cols = (query_conv * mixed).astype(jnp.bfloat16)
    product = lax.all_to_all(product_cols, "seq", split_axis=1, concat_axis=0, tiled=True).T
    partial_terms = jnp.dot(product, weight_rows, preferred_element_type=jnp.float32)
    block_output = lax.psum_scatter(
        partial_terms.astype(jnp.bfloat16), "chan", scatter_dimension=1, tiled=True
    )
    full_cotangent = lax.all_gather(cotangent, "chan", axis=1, tiled=True)
    scale = length ** (-0.5)
    out_grad_local = jnp.einsum(
        "cd,td->ct", weight_rows, full_cotangent, preferred_element_type=jnp.float32
    )
    out_grad_cols = lax.all_to_all(
        out_grad_local.astype(jnp.bfloat16), "seq", split_axis=0, concat_axis=1, tiled=True
    ).astype(out_grad_local.dtype)
    mixed_grad = rounded(out_grad_cols * query_conv)
    mixed_spec = forward_dft(mixed_grad, transform_plan)
    gated_grad = rounded(inverse_dft(multiply(mixed_spec, filter_spec, True), transform_plan))
    filter_grad = inverse_dft(multiply(mixed_spec, gated_spec, True), transform_plan) * scale
    query_cols = adjoint_along(out_grad_cols * mixed, local_taps[:, 0])
    key_cols = adjoint_along(gated_grad * value_conv, local_taps[:, 1])
    value_cols = adjoint_along(gated_grad * key_conv, local_taps[:, 2])
    grads_cols = jnp.stack([query_cols, key_cols, value_cols]).astype(jnp.bfloat16)
    returned = lax.all_to_all(grads_cols, "seq", split_axis=2, concat_axis=1, tiled=True)
    query_grad = returned[0].T
    key_grad = returned[1].T
    value_grad = returned[2].T
    return (block_output, query_grad, key_grad, value_grad, filter_grad)


def solution(mesh):
    return jax.shard_map(
        shards,
        mesh=mesh,
        in_specs=(
            P("seq", "chan"),
            P("seq", "chan"),
            P("seq", "chan"),
            P(None, None, "chan"),
            P(("chan", "seq"), None),
            P("chan", "seq"),
            P("seq", "chan"),
        ),
        out_specs=(
            P("seq", "chan"),
            P("seq", "chan"),
            P("seq", "chan"),
            P("seq", "chan"),
            P(("chan", "seq"), None),
        ),
        check_vma=False,
    )
```

profile of v0, /device:TPU:2, one launch (start us, length us, event | category | flops | bytes accessed | tf_op | source)
XLA Modules:
  0.0 534.4 jit_solution(2318840804369858780)
XLA Ops:
  8.7 1.1 copy.55
  9.8 1.1 copy.56
  10.9 1.1 copy.57
  12.1 1.6 copy.58
  13.8 14.3 %all-to-all-start = ((bf16[3,1024,128]{2,0,1:T(4,128)(2,1)}), bf16[3,1024,128]{2,0,1:T(4,128)(2,1)}, u32[]{:S(2)}, u32[]{:S(2)}) async-start(bf16[3,1024,128]{2,0,1:T(4,128)(2,1)} %copy.58), calls=%async_computation | async-start | bytes 2097152 | tf_op jit(solution)/shard_map/all_to_all | solution.py:113
  29.3 1.1 convolution_negate_fusion
  31.5 1.2 fusion.7
  32.7 1.2 fusion.11
  34.0 1.2 convolution_subtract_fusion.4
  35.2 1.2 convolution_add_fusion.4
  36.4 32.2 %all-to-all-done = bf16[3,1024,128]{2,0,1:T(4,128)(2,1)} async-done(((bf16[3,1024,128]{2,0,1:T(4,128)(2,1)}), bf16[3,1024,128]{2,0,1:T(4,128)(2,1)}, u32[]{:S(2)}, u32[]{:S(2)}) %all-to-all-start) | async-done | bytes 786464 | tf_op jit(solution)/shard_map/all_to_all | solution.py:113
  68.7 1.3 copy.59
  70.7 1.1 copy.61
  72.4 311.1 %all-gather.3.cloned.1.call-done = bf16[1024,8192]{1,0:T(8,128)(2,1)} async-done(((bf16[1024,256]{1,0:T(8,128)(2,1)}), bf16[1024,8192]{1,0:T(8,128)(2,1)}) %all-gather.3.cloned.1.call-update) | async-done | bytes 16777232 | tf_op jit(solution)/shard_map/all_gather | solution.py:110
  383.6 11.9 %convolution_convert_fusion.1 = bf16[1024,128]{1,0:T(8,128)(2,1)} fusion(bf16[1024,8192]{1,0:T(8,128)(2,1)} %all-gather.3.cloned.1.call-done, bf16[128,8192]{1,0:T(8,128)(2,1)} %all-gather.5.cloned.1.call-done), kind=kOutput, calls=%fused_computation.27 | convolution fusion | flops 2147614720 | bytes 19136512 | tf_op jit(solution)/shard_map/cd,td->ct/dot_general | solution.py:133
  395.5 6.2 %all-to-all-start.2 = ((bf16[32,32,128]{2,1,0:T(8,128)(2,1)}), bf16[32,32,128]{2,1,0:T(8,128)(2,1)S(1)}, u32[]{:S(2)}, u32[]{:S(2)}) async-start(bf16[32,32,128]{2,1,0:T(8,128)(2,1)} %bitcast.253), calls=%async_computation.3 | async-start | bytes 524288 | tf_op jit(solution)/shard_map/all_to_all | solution.py:136
  401.7 2.6 copy_bitcast_fusion.1
  404.3 8.9 %all-to-all-done.2 = bf16[32,32,128]{2,1,0:T(8,128)(2,1)S(1)} async-done(((bf16[32,32,128]{2,1,0:T(8,128)(2,1)}), bf16[32,32,128]{2,1,0:T(8,128)(2,1)S(1)}, u32[]{:S(2)}, u32[]{:S(2)}) %all-to-all-start.2) | async-done | bytes 262176 | tf_op jit(solution)/shard_map/all_to_all | solution.py:136
  415.0 1.3 fusion.51
  416.3 1.3 fusion.50
  417.5 1.3 convolution_subtract_fusion.2
  418.8 1.5 multiply_subtract_fusion.1
  420.3 1.2 fusion.62
  421.5 1.2 fusion.78
  422.7 1.2 convolution_add_fusion.1
  424.0 1.4 convolution_subtract_fusion.1
  427.4 1.6 convert_multiply_fusion.1
  430.5 1.2 fusion.49
  431.8 1.2 fusion.48
  433.0 1.3 convolution_add_fusion.5
  434.3 2.8 multiply_subtract_fusion
  437.1 1.2 fusion.67
  438.3 1.2 fusion.83
  439.6 1.5 convolution_add_fusion.3
  441.0 1.2 convolution_subtract_fusion.3
  445.1 5.3 all-to-all-start.1
  450.8 11.1 %all-to-all-done.1 = bf16[32,32,128]{2,0,1:T(8,128)(2,1)S(1)} async-done(((bf16[32,32,128]{2,0,1:T(8,128)(2,1)}), bf16[32,32,128]{2,0,1:T(8,128)(2,1)S(1)}, u32[]{:S(2)}, u32[]{:S(2)}) %all-to-all-start.1) | async-done | bytes 262176 | tf_op jit(solution)/shard_map/all_to_all | solution.py:126
  461.9 9.6 %convolution_convert_fusion = bf16[128,8192]{1,0:T(8,128)(2,1)} fusion(bf16[1024,128]{1,0:T(8,128)(2,1)S(1)} %bitcast.238, bf16[1024,8192]{1,0:T(8,128)(2,1)} %all-gather.3.cloned.1.call-done), kind=kOutput, calls=%fused_computation | convolution fusion | flops 2148532224 | bytes 19136512 | tf_op jit(solution)/shard_map/dot_general | solution.py:127
  472.4 4.7 copy.65
  477.1 7.3 %reshape.125 = bf16[32,2,6144]{2,1,0:T(2,128)(2,1)} reshape(bf16[4096,3,32]{2,1,0:T(4,128)(2,1)} %bitcast.223) | data formatting | bytes 1572864
  484.3 5.7 %all-to-all-start.3 = ((bf16[32,2,6144]{2,1,0:T(2,128)(2,1)}), bf16[32,2,6144]{2,1,0:T(2,128)(2,1)S(1)}, u32[]{:S(2)}, u32[]{:S(2)}) async-start(bf16[32,2,6144]{2,1,0:T(2,128)(2,1)} %reshape.125), calls=%async_computation.4 | async-start | bytes 1572864 | tf_op jit(solution)/shard_map/all_to_all | solution.py:147
  490.0 1.2 fusion.59
  491.3 1.2 fusion.75
  492.5 1.2 convolution_add_fusion
  493.7 1.2 convolution_subtract_fusion
  497.8 17.6 %all-to-all-done.3 = bf16[32,2,6144]{2,1,0:T(2,128)(2,1)S(1)} async-done(((bf16[32,2,6144]{2,1,0:T(2,128)(2,1)}), bf16[32,2,6144]{2,1,0:T(2,128)(2,1)S(1)}, u32[]{:S(2)}, u32[]{:S(2)}) %all-to-all-start.3) | async-done | bytes 786464 | tf_op jit(solution)/shard_map/all_to_all | solution.py:147
  515.4 4.9 reshape.126
  520.3 4.2 copy.73
  (60 shorter events, 20.0 us)
Async XLA Ops:
  7.2 20.9 %copy-start.5 = (f32[32,4096]{1,0:T(8,128)S(1)}, f32[32,4096]{1,0:T(8,128)}, u32[]{:S(2)}) copy-start(f32[32,4096]{1,0:T(8,128)} %param.11) | copy-start | bytes 1572868
  7.2 65.2 %all-gather.5.cloned.1.call-start = ((), (), s32[]{:S(2)}) async-start(), calls=%async_computation.7 | async-start | bytes 2359296 | tf_op jit(solution)/shard_map/all_gather | solution.py:131
  7.9 375.7 %all-gather.3.cloned.1.call-start = ((), (), s32[]{:S(2)}) async-start(), calls=%async_computation.5 | async-start | bytes 17301504 | tf_op jit(solution)/shard_map/all_gather | solution.py:110
  13.8 54.9 %all-to-all-start = ((bf16[3,1024,128]{2,0,1:T(4,128)(2,1)}), bf16[3,1024,128]{2,0,1:T(4,128)(2,1)}, u32[]{:S(2)}, u32[]{:S(2)}) async-start(bf16[3,1024,128]{2,0,1:T(4,128)(2,1)} %copy.58), calls=%async_computation | async-start | bytes 2097152 | tf_op jit(solution)/shard_map/all_to_all | solution.py:113
  395.5 17.7 %all-to-all-start.2 = ((bf16[32,32,128]{2,1,0:T(8,128)(2,1)}), bf16[32,32,128]{2,1,0:T(8,128)(2,1)S(1)}, u32[]{:S(2)}, u32[]{:S(2)}) async-start(bf16[32,32,128]{2,1,0:T(8,128)(2,1)} %bitcast.253), calls=%async_computation.3 | async-start | bytes 524288 | tf_op jit(solution)/shard_map/all_to_all | solution.py:136
  424.0 3.4 copy-start.3
  424.0 3.4 copy-start.4
  442.3 8.2 %copy-start.2 = (f32[32,4096]{1,0:T(8,128)S(1)}, f32[32,4096]{1,0:T(8,128)}, u32[]{:S(2)}) copy-start(f32[32,4096]{1,0:T(8,128)} %get-tuple-element.25) | copy-start | bytes 1572868
  445.1 16.8 %all-to-all-start.1 = ((bf16[32,32,128]{2,0,1:T(8,128)(2,1)}), bf16[32,32,128]{2,0,1:T(8,128)(2,1)S(1)}, u32[]{:S(2)}, u32[]{:S(2)}) async-start(bf16[32,32,128]{2,0,1:T(8,128)(2,1)} %bitcast.222), calls=%async_computation.1 | async-start | bytes 524288 | tf_op jit(solution)/shard_map/all_to_all | solution.py:126
  450.4 77.1 %reduce-scatter.2.cloned.1.call-start = ((), (), s32[]{:S(2)}) async-start(), calls=%async_computation.6 | async-start | bytes 2359296 | tf_op jit(solution)/shard_map/reduce_scatter | solution.py:128
  461.9 9.7 %copy-start.1 = (f32[32,4096]{1,0:T(8,128)S(1)}, f32[32,4096]{1,0:T(8,128)}, u32[]{:S(2)}) copy-start(f32[32,4096]{1,0:T(8,128)} %get-tuple-element.47) | copy-start | bytes 1572868
  477.1 13.0 %copy-start = (f32[32,64,128]{2,1,0:T(8,128)S(1)}, f32[32,64,128]{2,1,0:T(8,128)}, u32[]{:S(2)}) copy-start(f32[32,64,128]{2,1,0:T(8,128)} %get-tuple-element.32) | copy-start | bytes 3145732
  484.3 31.1 %all-to-all-start.3 = ((bf16[32,2,6144]{2,1,0:T(2,128)(2,1)}), bf16[32,2,6144]{2,1,0:T(2,128)(2,1)S(1)}, u32[]{:S(2)}, u32[]{:S(2)}) async-start(bf16[32,2,6144]{2,1,0:T(2,128)(2,1)} %reshape.125), calls=%async_computation.4 | async-start | bytes 1572864 | tf_op jit(solution)/shard_map/all_to_all | solution.py:147
Sparse Core Ops, SparseCore 0:
  9.8 59.9 all-gather.4
  73.0 310.5 all-gather.2
  471.7 46.8 reduce-scatter.1
where the time goes:
time: 545 us; the launch traced here: 534 us
  waiting for transfers between devices  382 us (70%)
  matrix products  63.8 us (12%)
  local copies, waits for them, and re-layouts  38.3 us (7%)
  starting transfers between devices  31.6 us (6%)
  between operations  14.8 us (3%)
    all_gather x1, waiting for transfers between devices, shards(): weight_rows = lax.all_gather(out_weight, 'seq', axis=1, tiled=True)  311 us
    all_to_all x1, waiting for transfers between devices, shards(): lax.all_to_all(stacked, 'seq', split_axis=1, concat_axis=2, tiled=True)  32.2 us
    unnamed x27, local copies, waits for them, and re-layouts  19.9 us
    all_to_all x1, waiting for transfers between devices, shards(): lax.all_to_all(grads_cols, 'seq', split_axis=2, concat_axis=1, tiled=True)  17.6 us
    all_to_all x1, starting transfers between devices, shards(): lax.all_to_all(stacked, 'seq', split_axis=1, concat_axis=2, tiled=True)  14.3 us
    dot_general x1, matrix products, shards(): jnp.einsum('cd,td->ct', weight_rows, full_cotangent, preferred_element_ty...  11.9 us
    all_to_all x1, waiting for transfers between devices, shards(): lax.all_to_all(product_cols, 'seq', split_axis=1, concat_axis=0, tiled=True)  11.1 us
  transfers between devices with their start and end apart: 7, of which 5 were waited for; matrix products, arithmetic and copies ran while one was open for 10% of the time, Pallas kernels for 0%

commit v1 on v0

v1 whole, which is shorter than its diff:
```python
import math

import jax
import jax.numpy as jnp
import numpy as np
from jax import lax
from jax.experimental import pallas as pl
from jax.experimental.pallas import tpu as pltpu
from jax.sharding import Mesh
from jax.sharding import PartitionSpec as P

SEQ = ("zh", "y", "x")
CHAN = ("zl", "core")
BF = jnp.bfloat16
F32 = jnp.float32
FAST = 128
GROUP = 8
VMEM = 40 * 1024 * 1024


def halves(value):
    high = np.asarray(value, np.float64).astype(jnp.bfloat16)
    low = (np.asarray(value, np.float64) - high.astype(np.float64)).astype(jnp.bfloat16)
    return high, low


def tables(length):
    rows = length // FAST
    slow = np.arange(rows)
    fast = np.arange(FAST)
    angle = 2 * math.pi * np.outer(slow + 0.25, slow) / rows
    first = np.concatenate([np.cos(angle), -np.sin(angle)], axis=0)
    high, low = halves(first)
    first_in = np.concatenate([high, low, high], axis=1)
    back = np.concatenate([np.cos(angle.T), -np.sin(angle.T)], axis=1) / length
    high, low = halves(back)
    first_out = np.concatenate([high, low, high], axis=1)
    twist = 2 * math.pi * np.outer(slow + 0.25, fast) / length
    twist = np.stack([np.cos(twist), np.sin(twist)]).astype(np.float32)
    turn = 2 * math.pi * np.outer(fast, fast) / FAST
    cos, sin = np.cos(turn), np.sin(turn)
    second_in = np.stack(halves(np.block([[cos, -sin], [sin, cos]])))
    second_out = np.stack(halves(np.block([[cos, sin], [-sin, cos]])))
    return first_in, first_out, twist, second_in, second_out


def split(value):
    high = value.astype(BF)
    return high, (value - high.astype(F32)).astype(BF)


def dot(first, second):
    return jnp.dot(first, second, preferred_element_type=F32)


def dot_wide(value, table):
    high, low = split(value)
    return dot(high, table[0]) + (dot(low, table[0]) + dot(high, table[1]))


def group_forward(held, group, first_in, twist, second_in):
    rows = twist.shape[1]
    channels = held.shape[0] // rows
    signal = jnp.concatenate(
        [held[pl.ds(group * GROUP + i, rows, stride=channels), :] for i in range(GROUP)], axis=1
    )
    high, low = split(signal)
    first = dot(first_in[...], jnp.concatenate([high, high, low], axis=0))
    cos, sin = twist[0], twist[1]
    parts = []
    for i in range(GROUP):
        real = first[:rows, i * FAST : (i + 1) * FAST]
        imag = first[rows:, i * FAST : (i + 1) * FAST]
        parts.append(jnp.concatenate([real * cos + imag * sin, imag * cos - real * sin], axis=1))
    return dot_wide(jnp.concatenate(parts, axis=0), second_in)


def group_inverse(spectrum, group, first_out, twist, second_out, held):
    rows = twist.shape[1]
    channels = held.shape[0] // rows
    back = dot_wide(spectrum, second_out)
    cos, sin = twist[0], twist[1]
    real_parts, imag_parts = [], []
    for i in range(GROUP):
        real = back[i * rows : (i + 1) * rows, :FAST]
        imag = back[i * rows : (i + 1) * rows, FAST:]
        real_parts.append(real * cos - imag * sin)
        imag_parts.append(real * sin + imag * cos)
    turned = jnp.concatenate(
        [jnp.concatenate(real_parts, axis=1), jnp.concatenate(imag_parts, axis=1)], axis=0
    )
    high, low = split(turned)
    result = dot(first_out[...], jnp.concatenate([high, high, low], axis=0))
    for i in range(GROUP):
        held[pl.ds(group * GROUP + i, rows, stride=channels), :] = result[:, i * FAST : (i + 1) * FAST]


def product_of(first, second, conjugate):
    first_re, first_im = first[:, :FAST], first[:, FAST:]
    second_re, second_im = second[:, :FAST], second[:, FAST:]
    if conjugate:
        return jnp.concatenate(
            [
                first_re * second_re + first_im * second_im,
                first_im * second_re - first_re * second_im,
            ],
            axis=1,
        )
    return jnp.concatenate(
        [
            first_re * second_re - first_im * second_im,
            first_re * second_im + first_im * second_re,
        ],
        axis=1,
    )


def filter_kernel(signal, first_in, twist, second_in, spectrum, held):
    rows = twist.shape[1]
    channels = signal.shape[0]
    for n1 in range(rows):
        held[n1 * channels : (n1 + 1) * channels, :] = signal[:, n1 * FAST : (n1 + 1) * FAST]
    step = GROUP * rows
    for group in range(channels // GROUP):
        spectrum[group * step : (group + 1) * step, :] = group_forward(
            held, group, first_in, twist, second_in
        )


def convolve_kernel(
    conjugate, signal, filter_spec, first_in, first_out, twist, second_in, second_out,
    result, spectrum, held, out,
):
    rows = twist.shape[1]
    channels = signal.shape[0] // rows
    held[...] = signal[...].astype(F32)
    step = GROUP * rows
    for group in range(channels // GROUP):
        here = slice(group * step, (group + 1) * step)
        spec = group_forward(held, group, first_in, twist, second_in)
        spectrum[here, :] = spec
        both = product_of(spec, filter_spec[here, :], conjugate)
        group_inverse(both, group, first_out, twist, second_out, out)
    result[...] = out[...].astype(result.dtype)


def filter_grad_kernel(first_spec, second_spec, first_out, twist, second_out, result, out):
    rows = twist.shape[1]
    channels = result.shape[0]
    scale = result.shape[1] ** -0.5
    step = GROUP * rows
    for group in range(channels // GROUP):
        here = slice(group * step, (group + 1) * step)
        both = product_of(first_spec[here, :], second_spec[here, :], True) * scale
        group_inverse(both, group, first_out, twist, second_out, out)
    for n1 in range(rows):
        result[:, n1 * FAST : (n1 + 1) * FAST] = out[n1 * channels : (n1 + 1) * channels, :]


def call(kernel, out_shape, scratch, *args):
    flops = 2 * 3 * 2 * 1024 * 256 * 256
    return pl.pallas_call(
        kernel,
        out_shape=out_shape,
        in_specs=[pl.BlockSpec(memory_space=pltpu.VMEM)] * len(args),
        out_specs=jax.tree.map(lambda _: pl.BlockSpec(memory_space=pltpu.VMEM), out_shape),
        scratch_shapes=scratch,
        compiler_params=pltpu.CompilerParams(vmem_limit_bytes=VMEM),
        cost_estimate=pl.CostEstimate(flops=flops, bytes_accessed=4 << 20, transcendentals=0),
    )(*args)


def causal(signal, before, weights):
    extent = signal.shape[0]
    joined = jnp.concatenate([before, signal], axis=0).astype(F32)
    return weights[0] * joined[2:] + weights[1] * joined[1 : extent + 1] + weights[2] * joined[:extent]


def adjoint(signal, after, weights):
    extent = signal.shape[0]
    joined = jnp.concatenate([signal, after], axis=0)
    return (
        weights[0] * joined[:extent] + weights[1] * joined[1 : extent + 1] + weights[2] * joined[2:]
    )


def swap(value, axis):
    return lax.ppermute(value, axis, [(0, 1), (1, 0)])


def to_channels(value):
    return lax.all_to_all(value.T, SEQ, split_axis=0, concat_axis=0, tiled=True)


def to_tokens(value):
    return lax.all_to_all(value, SEQ, split_axis=0, concat_axis=0, tiled=True).T


def shards(query, key, value, short_filter, long_filter, out_weight, cotangent):
    tokens, width = query.shape
    seq_count = lax.axis_size(SEQ)
    length = tokens * seq_count
    channels = width // seq_count
    zh, zl, core = lax.axis_index("zh"), lax.axis_index("zl"), lax.axis_index("core")
    upper, lower = zl // 2, zl % 2
    first_in, first_out, twist, second_in, second_out = (jnp.asarray(t) for t in tables(length))
    spec_type = jax.ShapeDtypeStruct((channels * length // FAST, 2 * FAST), F32)
    rows_type = jax.ShapeDtypeStruct((length // FAST * channels, FAST), BF)
    held = pltpu.VMEM(rows_type.shape, F32)

    weight = lax.all_gather(out_weight, ("y", "x"), axis=1, tiled=True)

    rows = jnp.concatenate([query[-2:], key[-2:], value[-2:]], axis=0)
    rows = lax.ppermute(rows, SEQ, [(i, i + 1) for i in range(seq_count - 1)])
    query_conv = causal(query, rows[0:2], short_filter[:, 0])
    key_conv = causal(key, rows[2:4], short_filter[:, 1])
    value_conv = causal(value, rows[4:6], short_filter[:, 2])
    gated = (key_conv * value_conv).astype(BF)
    gated_rows = to_channels(gated)

    filter_spec = call(filter_kernel, spec_type, [held], long_filter, first_in, twist, second_in)

    def links(k1, k2, back):
        pairs = []
        for a in range(2):
            for u in range(2):
                for v in range(2):
                    chip, owner = a * 4 + u * 2 + v, (u ^ k2) * 4 + a * 2 + (v ^ k1)
                    pairs.append((chip, owner) if back else (owner, chip))
        return pairs

    got = [[lax.ppermute(cotangent, ("zh", "zl"), links(k1, k2, False)) for k1 in range(2)] for k2 in range(2)]
    other_row = upper != zh
    mine = [jnp.where(other_row, got[1][k1], got[0][k1]) for k1 in range(2)]
    theirs = [jnp.where(other_row, got[0][k1], got[1][k1]) for k1 in range(2)]
    swapped = lower == 1
    ordered = jnp.stack(
        [
            jnp.stack([jnp.where(swapped, r[1], r[0]), jnp.where(swapped, r[0], r[1])], axis=1)
            for r in (mine, theirs)
        ]
    )
    beside = swap(ordered, "core")
    first_core = core == 0
    whole = jnp.stack(
        [jnp.where(first_core, ordered, beside), jnp.where(first_core, beside, ordered)], axis=3
    ).reshape(2 * tokens, 4 * width)

    mixed_rows, gated_spec = call(
        lambda *refs: convolve_kernel(False, *refs), (rows_type, spec_type), [held, held],
        gated_rows, filter_spec, first_in, first_out, twist, second_in, second_out,
    )
    mixed = to_tokens(mixed_rows).astype(F32)
    product = (query_conv * mixed).astype(BF)

    both = jnp.concatenate([product, swap(product, "zh")], axis=0)
    partial = jnp.dot(both, weight, preferred_element_type=F32).astype(BF)
    partial = partial.reshape(2, tokens, 2, 2, width)
    keep = lax.dynamic_index_in_dim(partial, core, 3, keepdims=False)
    give = lax.dynamic_index_in_dim(partial, 1 - core, 3, keepdims=False)
    chip = (keep.astype(F32) + swap(give, "core").astype(F32)).astype(BF)
    total = jnp.zeros((tokens, width), F32)
    for k2 in range(2):
        row = lax.dynamic_index_in_dim(chip, (upper ^ k2) ^ zh, 0, keepdims=False)
        for k1 in range(2):
            block = lax.dynamic_index_in_dim(row, lower ^ k1, 1, keepdims=False)
            total = total + lax.ppermute(block, ("zh", "zl"), links(k1, k2, True)).astype(F32)
    block_output = total.astype(BF)

    grads = lax.dot_general(whole, weight, (((1,), (1,)), ((), ())), preferred_element_type=F32)
    out_grad = grads[:tokens] + swap(grads[tokens:].astype(BF), "zh").astype(F32)
    mixed_grad = (out_grad * query_conv).astype(BF)
    mixed_grad_rows = to_channels(mixed_grad)
    gated_grad_rows, mixed_spec = call(
        lambda *refs: convolve_kernel(True, *refs), (rows_type, spec_type), [held, held],
        mixed_grad_rows, filter_spec, first_in, first_out, twist, second_in, second_out,
    )
    gated_grad = to_tokens(gated_grad_rows).astype(F32)
    filter_grad = call(
        filter_grad_kernel, jax.ShapeDtypeStruct((channels, length), F32), [held],
        mixed_spec, gated_spec, first_out, twist, second_out,
    )
    back = [(i + 1, i) for i in range(seq_count - 1)]
    query_conv_grad = out_grad * mixed
    query_after = lax.ppermute(query_conv_grad[:2], SEQ, back)
    query_grad = adjoint(query_conv_grad, query_after, short_filter[:, 0]).astype(BF)
    key_conv_grad = gated_grad * value_conv
    value_conv_grad = gated_grad * key_conv
    after = lax.ppermute(jnp.concatenate([key_conv_grad[:2], value_conv_grad[:2]], axis=0), SEQ, back)
    key_grad = adjoint(key_conv_grad, after[:2], short_filter[:, 1]).astype(BF)
    value_grad = adjoint(value_conv_grad, after[2:], short_filter[:, 2]).astype(BF)
    return (block_output, query_grad, key_grad, value_grad, filter_grad)


def solution(mesh):
    fine = Mesh(mesh.devices.reshape(2, 4, 4, 4, 2), SEQ + CHAN)
    return jax.shard_map(
        shards,
        mesh=fine,
        in_specs=(
            P(SEQ, CHAN),
            P(SEQ, CHAN),
            P(SEQ, CHAN),
            P(None, None, CHAN),
            P(CHAN + SEQ, None),
            P(CHAN, SEQ),
            P(SEQ, CHAN),
        ),
        out_specs=(
            P(SEQ, CHAN),
            P(SEQ, CHAN),
            P(SEQ, CHAN),
            P(SEQ, CHAN),
            P(CHAN + SEQ, None),
        ),
        check_vma=False,
    )
```

time: 545 us -> 340 us (0.62)
  the two profiles are of different devices: /device:TPU:2 before, /device:TPU:96 now
where the time goes in v1:
time: 340 us; the launch traced here: 339 us
  waiting for transfers between devices  146 us (43%)
  starting transfers between devices  68.8 us (20%)
  blocking collectives  33.8 us (10%)
  local copies, waits for them, and re-layouts  31.2 us (9%)
  other arithmetic  20.4 us (6%)
  between operations  14.5 us (4%)
  matrix products  13.5 us (4%)
  Pallas kernels  10.6 us (3%)
    all_gather x1, waiting for transfers between devices, shards(): weight = lax.all_gather(out_weight, ('y', 'x'), axis=1, tiled=True)  36.8 us
    ppermute x4, starting transfers between devices, shards(): lax.ppermute(block, ('zh', 'zl'), links(k1, k2, True)).astype(F32)  36.2 us
    ppermute x4, waiting for transfers between devices, shards(): lax.ppermute(cotangent, ('zh', 'zl'), links(k1, k2, False))  30.6 us
    ppermute x4, waiting for transfers between devices, swap(): return lax.ppermute(value, axis, [(0, 1), (1, 0)])  22.5 us
    ppermute x4, waiting for transfers between devices, shards(): lax.ppermute(block, ('zh', 'zl'), links(k1, k2, True)).astype(F32)  18.8 us
    all_to_all x1, blocking collectives, to_channels(): return lax.all_to_all(value.T, SEQ, split_axis=0, concat_axis=0, tiled=True)  17 us
    all_to_all x1, blocking collectives, to_tokens(): return lax.all_to_all(value, SEQ, split_axis=0, concat_axis=0, tiled=True).T  16.8 us
    ppermute x1, waiting for transfers between devices, shards(): lax.ppermute(jnp.concatenate([key_conv_grad[:2], value_conv_grad[:2]], ax...  15.2 us
  transfers between devices with their start and end apart: 18, of which 11 were waited for; matrix products, arithmetic and copies ran while one was open for 10% of the time, Pallas kernels for 1%

profile of v1, /device:TPU:96, one launch (start us, length us, event | category | flops | bytes accessed | tf_op | source)
XLA Modules:
  0.0 338.6 jit_solution(12492497943717860859)
XLA Ops:
  7.9 5.5 %collective-permute-start.10 = (bf16[128,1024]{1,0:T(8,128)(2,1)}, bf16[128,1024]{1,0:T(8,128)(2,1)S(1)}, u32[]{:S(2)}, u32[]{:S(2)}) collective-permute-start(bf16[128,1024]{1,0:T(8,128)(2,1)} %param.18), channel_id=1, source_target_pairs={{0,0},{2,2},{128,4},{130,6},{4,128},{6,130},{132,132},{134,134},{1... | collective-permute-start | bytes 786440 | tf_op jit(solution)/shard_map/ppermute | solution.py:232
  13.6 3.4 collective-permute-start.9
  17.0 10.8 %collective-permute-done.10 = bf16[128,1024]{1,0:T(8,128)(2,1)S(1)} collective-permute-done((bf16[128,1024]{1,0:T(8,128)(2,1)}, bf16[128,1024]{1,0:T(8,128)(2,1)S(1)}, u32[]{:S(2)}, u32[]{:S(2)}) %collective-permute-start.10) | collective-permute-done | bytes 262176 | tf_op jit(solution)/shard_map/ppermute | solution.py:232
  27.8 10.4 %collective-permute-done.7 = bf16[128,1024]{1,0:T(8,128)(2,1)S(1)} collective-permute-done((bf16[128,1024]{1,0:T(8,128)(2,1)}, bf16[128,1024]{1,0:T(8,128)(2,1)S(1)}, u32[]{:S(2)}, u32[]{:S(2)}) %collective-permute-start.7) | collective-permute-done | bytes 262176 | tf_op jit(solution)/shard_map/ppermute | solution.py:232
  38.1 9.4 %collective-permute-done.8 = bf16[128,1024]{1,0:T(8,128)(2,1)S(1)} collective-permute-done((bf16[128,1024]{1,0:T(8,128)(2,1)}, bf16[128,1024]{1,0:T(8,128)(2,1)S(1)}, u32[]{:S(2)}, u32[]{:S(2)}) %collective-permute-start.8) | collective-permute-done | bytes 262176 | tf_op jit(solution)/shard_map/ppermute | solution.py:232
  50.1 3.4 %collective-permute-start = (bf16[6,1024]{1,0:T(8,128)(2,1)S(1)}, bf16[6,1024]{1,0:T(8,128)(2,1)S(1)}, u32[]{:S(2)}, u32[]{:S(2)}) collective-permute-start(bf16[6,1024]{1,0:T(8,128)(2,1)S(1)} %pad_maximum_fusion.6), channel_id=1, source_target_pairs={{0,8},{8,16},{16,24},{24,32},{32,40},{40,48},{48,56},{56,64},{64,7... | collective-permute-start | bytes 36872 | tf_op jit(solution)/shard_map/ppermute | solution.py:214
  53.9 2.2 copy.53
  56.1 2.8 reshape.57
  58.9 36.8 %all-gather.2.cloned.1.call-done = bf16[1024,4096]{1,0:T(8,128)(2,1)} async-done(((bf16[1024,256]{1,0:T(8,128)(2,1)}), bf16[1024,4096]{1,0:T(8,128)(2,1)}) %all-gather.2.cloned.1.call-update) | async-done | bytes 8388624 | tf_op jit(solution)/shard_map/all_gather | solution.py:211
  95.7 6.4 %fusion.39 = f32[256,1024]{1,0:T(8,128)S(1)} fusion(bf16[256,4096]{1,0:T(8,128)(2,1)} %reshape.57, bf16[1024,4096]{1,0:T(8,128)(2,1)} %all-gather.2.cloned.1.call-done), kind=kOutput, calls=%fused_computation.92 | convolution fusion | flops 2147483648 | bytes 11534336 | tf_op jit(solution)/shard_map/dot_general | solution.py:270
  102.1 3.1 collective-permute-start.12
  105.3 12.6 %collective-permute-done.12 = bf16[128,1024]{1,0:T(8,128)(2,1)S(1)} collective-permute-done((bf16[128,1024]{1,0:T(8,128)(2,1)S(1)}, bf16[128,1024]{1,0:T(8,128)(2,1)S(1)}, u32[]{:S(2)}, u32[]{:S(2)}) %collective-permute-start.12) | collective-permute-done | bytes 262176 | tf_op jit(solution)/shard_map/ppermute | solution.py:188
  118.0 1.0 fusion.31
  119.9 9.1 %all-to-all-start.2 = ((bf16[32,32,128]{2,1,0:T(8,128)(2,1)}), bf16[32,32,128]{2,1,0:T(8,128)(2,1)S(1)}, u32[]{:S(2)}, u32[]{:S(2)}) async-start(bf16[32,32,128]{2,1,0:T(8,128)(2,1)} %bitcast.30), calls=%async_computation.2 | async-start | bytes 524288 | tf_op jit(solution)/shard_map/all_to_all | solution.py:192
  129.0 0.9 shard_map.155.refs_1_
  129.9 13.1 %all-to-all-done.2 = bf16[32,32,128]{2,1,0:T(8,128)(2,1)S(1)} async-done(((bf16[32,32,128]{2,1,0:T(8,128)(2,1)}), bf16[32,32,128]{2,1,0:T(8,128)(2,1)S(1)}, u32[]{:S(2)}, u32[]{:S(2)}) %all-to-all-start.2) | async-done | bytes 262176 | tf_op jit(solution)/shard_map/all_to_all | solution.py:192
  143.0 4.0 %shard_map.157 = (bf16[1024,128]{1,0:T(8,128)(2,1)}, f32[1024,256]{1,0:T(8,128)S(1)}) custom-call(bf16[1024,128]{1,0:T(8,128)(2,1)S(1)} %bitcast.74, f32[1024,256]{1,0:T(8,128)S(1)} %shard_map.155.refs_1_, bf16[64,96]{1,0:T(8,128)(2,1)S(1)} %copy-done.5, bf16[32,192]{1,0:T(8,128)(2,1)S(1)} %copy-done.4, f32[2,32,128]{2,1,0:T(8,128)S(1)} %copy-done.3, ...), custom_call_target="tpu_custom_call" | custom-call | flops 805306368 | bytes 4194304 | tf_op jit(solution)/shard_map/pallas_call | solution.py:162
  147.0 4.6 %all-to-all-start.3 = ((bf16[32,32,128]{2,1,0:T(8,128)(2,1)}), bf16[32,32,128]{2,1,0:T(8,128)(2,1)}, u32[]{:S(2)}, u32[]{:S(2)}) async-start(bf16[32,32,128]{2,1,0:T(8,128)(2,1)} %bitcast.32), calls=%async_computation.3 | async-start | bytes 524288 | tf_op jit(solution)/shard_map/all_to_all | solution.py:196
  151.8 1.1 copy.49
  153.1 0.9 copy.48
  154.0 2.3 maximum_convert_fusion
  156.4 8.2 %all-to-all-done.3 = bf16[32,32,128]{2,1,0:T(8,128)(2,1)} async-done(((bf16[32,32,128]{2,1,0:T(8,128)(2,1)}), bf16[32,32,128]{2,1,0:T(8,128)(2,1)}, u32[]{:S(2)}, u32[]{:S(2)}) %all-to-all-start.3) | async-done | bytes 262176 | tf_op jit(solution)/shard_map/all_to_all | solution.py:196
  164.6 3.8 %fusion.29 = (f32[128,1024]{0,1:T(8,128)S(1)}, f32[128,1024]{0,1:T(8,128)S(1)}, f32[128,1024]{0,1:T(8,128)}, f32[128,1024]{0,1:T(8,128)S(1)}) fusion(bf16[32,32,128]{2,1,0:T(8,128)(2,1)} %all-to-all-done.3, f32[130,1024]{0,1:T(8,128)} %get-tuple-element.67, f32[1024]{0:T(1024)S(1)} %bitcast.94, f32[1024]{0:T(1024)S(1)} %bitcast.96, f32[1024]{0:T(1024)S(1)} %bitcast.92, ...), kind=kLoop, calls=%fused_computation.63 | loop fusion | flops 1703936 | bytes 5529600 | tf_op jit(solution)/shard_map/mul | solution.py:287
  168.4 17.0 %all_to_all.40 = bf16[32,32,128]{2,1,0:T(8,128)(2,1)S(1)} all-to-all(bf16[32,32,128]{2,1,0:T(8,128)(2,1)S(1)} %bitcast.79), channel_id=1, replica_groups=mesh['zh'=2,'y'=4,'x'=4,'zl'=4,'core'=2] {'zh','y','x'}, dimensions={0} | all-to-all | bytes 524288 | tf_op jit(solution)/shard_map/all_to_all | solution.py:192
  185.4 3.3 shard_map.156
  188.7 16.8 %all_to_all.41 = bf16[32,32,128]{2,1,0:T(8,128)(2,1)S(1)} all-to-all(bf16[32,32,128]{2,1,0:T(8,128)(2,1)S(1)} %bitcast.76), channel_id=1, replica_groups=mesh['zh'=2,'y'=4,'x'=4,'zl'=4,'core'=2] {'zh','y','x'}, dimensions={0} | all-to-all | bytes 524288 | tf_op jit(solution)/shard_map/all_to_all | solution.py:196
  206.3 1.2 copy.50
  207.5 2.3 bitcast_multiply_fusion
  210.6 9.8 %collective-permute-done.1 = bf16[128,1024]{1,0:T(8,128)(2,1)S(1)} collective-permute-done((bf16[128,1024]{1,0:T(8,128)(2,1)}, bf16[128,1024]{1,0:T(8,128)(2,1)S(1)}, u32[]{:S(2)}, u32[]{:S(2)}) %collective-permute-start.1) | collective-permute-done | bytes 262176 | tf_op jit(solution)/shard_map/ppermute | solution.py:188
  220.5 7.1 %convolution_convert_fusion = bf16[256,4096]{1,0:T(8,128)(2,1)} fusion(bf16[1024,4096]{1,0:T(8,128)(2,1)} %all-gather.2.cloned.1.call-done, bf16[128,1024]{1,0:T(8,128)(2,1)S(1)} %collective-permute-done.1, bf16[128,1024]{1,0:T(8,128)(2,1)} %get-tuple-element.49), kind=kOutput, calls=%fused_computation | convolution fusion | flops 2149580800 | bytes 11010048 | tf_op jit(solution)/shard_map/dot_general | solution.py:257
  227.6 4.5 %reshape.56 = bf16[2,128,2,2,1024]{4,3,2,1,0:T(2,128)(2,1)} reshape(bf16[256,4096]{1,0:T(8,128)(2,1)} %convolution_convert_fusion) | data formatting | bytes 4194304 | tf_op jit(solution)/shard_map/reshape | solution.py:258
  232.1 7.9 %constant_dynamic-slice_fusion.1 = (bf16[2,128,2,1,1024]{4,3,2,1,0:T(2,128)(2,1)}, bf16[2,128,2,1,1024]{4,3,2,1,0:T(2,128)(2,1)S(1)}) fusion(bf16[2,128,2,2,1024]{4,3,2,1,0:T(2,128)(2,1)} %reshape.56, s32[]{:T(128)S(6)} %select_n.92, s32[]{:T(128)S(6)} %select_n.93), kind=kLoop, calls=%fused_computation.87 | loop fusion | bytes 4194312 | tf_op jit(solution)/shard_map/jit(dynamic_index_in_dim)/dynamic_slice | solution.py:259
  240.0 1.6 copy.63
  241.6 1.0 pad_maximum_fusion.5
  242.6 1.3 collective-permute-start.14
  243.9 15.2 %collective-permute-done.14 = f32[4,1024]{0,1:T(8,128)} collective-permute-done((f32[4,1024]{0,1:T(8,128)}, f32[4,1024]{0,1:T(8,128)}, u32[]{:S(2)}, u32[]{:S(2)}) %collective-permute-start.14) | collective-permute-done | bytes 16416 | tf_op jit(solution)/shard_map/ppermute | solution.py:289
  259.1 2.1 fusion.36
  261.2 1.7 fusion.10
  262.9 1.8 copy.56
  264.7 2.2 fusion.15
  268.6 1.3 collective-permute-start.13
  269.9 2.6 fusion
  272.6 29.6 %collective-permute-start.3 = (bf16[128,1024]{1,0:T(8,128)(2,1)S(1)}, bf16[128,1024]{1,0:T(8,128)(2,1)S(1)}, u32[]{:S(2)}, u32[]{:S(2)}) collective-permute-start(bf16[128,1024]{1,0:T(8,128)(2,1)S(1)} %get-tuple-element.38), channel_id=1, source_target_pairs={{0,0},{2,2},{4,128},{6,130},{128,4},{130,6},{132,132},{134,134},{1... | collective-permute-start | bytes 786440 | tf_op jit(solution)/shard_map/ppermute | solution.py:267
  302.6 6.1 %collective-permute-start.6 = (bf16[128,1024]{1,0:T(8,128)(2,1)S(1)}, bf16[128,1024]{1,0:T(8,128)(2,1)S(1)}, u32[]{:S(2)}, u32[]{:S(2)}) collective-permute-start(bf16[128,1024]{1,0:T(8,128)(2,1)S(1)} %get-tuple-element.39), channel_id=1, source_target_pairs={{0,130},{2,128},{4,2},{6,0},{128,134},{130,132},{132,6},{134,4},{1... | collective-permute-start | bytes 786440 | tf_op jit(solution)/shard_map/ppermute | solution.py:267
  308.8 2.5 shard_map.158
  311.3 0.9 fusion.5
  312.1 3.5 %collective-permute-done.3 = bf16[128,1024]{1,0:T(8,128)(2,1)S(1)} collective-permute-done((bf16[128,1024]{1,0:T(8,128)(2,1)S(1)}, bf16[128,1024]{1,0:T(8,128)(2,1)S(1)}, u32[]{:S(2)}, u32[]{:S(2)}) %collective-permute-start.3) | collective-permute-done | bytes 262176 | tf_op jit(solution)/shard_map/ppermute | solution.py:267
  315.7 15.2 %collective-permute-done.4 = bf16[128,1024]{1,0:T(8,128)(2,1)S(1)} collective-permute-done((bf16[128,1024]{1,0:T(8,128)(2,1)S(1)}, bf16[128,1024]{1,0:T(8,128)(2,1)S(1)}, u32[]{:S(2)}, u32[]{:S(2)}) %collective-permute-start.4) | collective-permute-done | bytes 262176 | tf_op jit(solution)/shard_map/ppermute | solution.py:267
  (68 shorter events, 9.8 us)
Async XLA Ops:
  7.2 88.5 %all-gather.2.cloned.1.call-start = ((), (), s32[]{:S(2)}) async-start(), calls=%async_computation.4 | async-start | bytes 8912896 | tf_op jit(solution)/shard_map/all_gather | solution.py:211
  7.9 19.9 %collective-permute-start.10 = (bf16[128,1024]{1,0:T(8,128)(2,1)}, bf16[128,1024]{1,0:T(8,128)(2,1)S(1)}, u32[]{:S(2)}, u32[]{:S(2)}) collective-permute-start(bf16[128,1024]{1,0:T(8,128)(2,1)} %param.18), channel_id=1, source_target_pairs={{0,0},{2,2},{128,4},{130,6},{4,128},{6,130},{132,132},{134,134},{1... | collective-permute-start | bytes 786440 | tf_op jit(solution)/shard_map/ppermute | solution.py:232
  13.4 24.7 %collective-permute-start.7 = (bf16[128,1024]{1,0:T(8,128)(2,1)}, bf16[128,1024]{1,0:T(8,128)(2,1)S(1)}, u32[]{:S(2)}, u32[]{:S(2)}) collective-permute-start(bf16[128,1024]{1,0:T(8,128)(2,1)} %param.18), channel_id=1, source_target_pairs={{130,0},{128,2},{2,4},{0,6},{134,128},{132,130},{6,132},{4,134},{1... | collective-permute-start | bytes 786440 | tf_op jit(solution)/shard_map/ppermute | solution.py:232
  13.5 34.0 %collective-permute-start.8 = (bf16[128,1024]{1,0:T(8,128)(2,1)}, bf16[128,1024]{1,0:T(8,128)(2,1)S(1)}, u32[]{:S(2)}, u32[]{:S(2)}) collective-permute-start(bf16[128,1024]{1,0:T(8,128)(2,1)} %param.18), channel_id=1, source_target_pairs={{2,0},{0,2},{130,4},{128,6},{6,128},{4,130},{134,132},{132,134},{3... | collective-permute-start | bytes 786440 | tf_op jit(solution)/shard_map/ppermute | solution.py:232
  13.6 34.0 %collective-permute-start.9 = (bf16[128,1024]{1,0:T(8,128)(2,1)}, bf16[128,1024]{1,0:T(8,128)(2,1)S(1)}, u32[]{:S(2)}, u32[]{:S(2)}) collective-permute-start(bf16[128,1024]{1,0:T(8,128)(2,1)} %param.18), channel_id=1, source_target_pairs={{128,0},{130,2},{0,4},{2,6},{132,128},{134,130},{4,132},{6,134},{1... | collective-permute-start | bytes 786440 | tf_op jit(solution)/shard_map/ppermute | solution.py:232
  47.7 1.0 copy-start.12
  47.7 5.8 %copy-start.14 = (f32[3,3,1024]{2,1,0:T(4,128)S(1)}, f32[3,3,1024]{2,1,0:T(4,128)}, u32[]{:S(2)}) copy-start(f32[3,3,1024]{2,1,0:T(4,128)} %param.15) | copy-start | bytes 110596
  47.9 5.7 %collective-permute-start.11 = (bf16[2,128,2,1024]{3,1,2,0:T(8,128)(2,1)S(1)}, bf16[2,128,2,1024]{3,1,2,0:T(8,128)(2,1)S(1)}, u32[]{:S(2)}, u32[]{:S(2)}) collective-permute-start(bf16[2,128,2,1024]{3,1,2,0:T(8,128)(2,1)S(1)} %pad_maximum_fusion.1), channel_id=1, source_target_pairs={{0,1},{1,0},{2,3},{3,2},{4,5},{5,4},{6,7},{7,6},{8,9},{9,8},{10,11... | collective-permute-start | bytes 3145736 | tf_op jit(solution)/shard_map/ppermute | solution.py:188
  50.1 55.1 %collective-permute-start = (bf16[6,1024]{1,0:T(8,128)(2,1)S(1)}, bf16[6,1024]{1,0:T(8,128)(2,1)S(1)}, u32[]{:S(2)}, u32[]{:S(2)}) collective-permute-start(bf16[6,1024]{1,0:T(8,128)(2,1)S(1)} %pad_maximum_fusion.6), channel_id=1, source_target_pairs={{0,8},{8,16},{16,24},{24,32},{32,40},{40,48},{48,56},{56,64},{64,7... | collective-permute-start | bytes 36872 | tf_op jit(solution)/shard_map/ppermute | solution.py:214
  102.1 16.9 %copy-start.10 = (f32[256,1024]{1,0:T(8,128)}, f32[256,1024]{1,0:T(8,128)S(1)}, u32[]{:S(2)}) copy-start(f32[256,1024]{1,0:T(8,128)S(1)} %fusion.39) | copy-start | bytes 3145732
  102.1 15.8 %collective-permute-start.12 = (bf16[128,1024]{1,0:T(8,128)(2,1)S(1)}, bf16[128,1024]{1,0:T(8,128)(2,1)S(1)}, u32[]{:S(2)}, u32[]{:S(2)}) collective-permute-start(bf16[128,1024]{1,0:T(8,128)(2,1)S(1)} %slice.290), channel_id=1, source_target_pairs={{0,128},{128,0},{1,129},{129,1},{2,130},{130,2},{3,131},{131,3},{4... | collective-permute-start | bytes 786440 | tf_op jit(solution)/shard_map/ppermute | solution.py:188
  118.0 1.9 copy-start.11
  118.0 11.0 %copy-start = (f32[32,4096]{1,0:T(8,128)S(1)}, f32[32,4096]{1,0:T(8,128)}, u32[]{:S(2)}) copy-start(f32[32,4096]{1,0:T(8,128)} %signal.1) | copy-start | bytes 1572868
  118.0 11.0 %copy-start.2 = (bf16[2,256,256]{2,1,0:T(8,128)(2,1)S(1)}, bf16[2,256,256]{2,1,0:T(8,128)(2,1)}, u32[]{:S(2)}) copy-start(bf16[2,256,256]{2,1,0:T(8,128)(2,1)} %constant.155.clone.second_in.refs_5_) | copy-start | bytes 786436
  118.0 11.0 %copy-start.3 = (f32[2,32,128]{2,1,0:T(8,128)S(1)}, f32[2,32,128]{2,1,0:T(8,128)}, u32[]{:S(2)}) copy-start(f32[2,32,128]{2,1,0:T(8,128)} %constant.154.clone.twist.refs_4_) | copy-start | bytes 98308
  118.0 11.0 %copy-start.5 = (bf16[64,96]{1,0:T(8,128)(2,1)S(1)}, bf16[64,96]{1,0:T(8,128)(2,1)}, u32[]{:S(2)}) copy-start(bf16[64,96]{1,0:T(8,128)(2,1)} %constant.152.clone.first_in.refs_2_) | copy-start | bytes 36868
  119.0 24.0 %copy-start.1 = (bf16[2,256,256]{2,1,0:T(8,128)(2,1)S(1)}, bf16[2,256,256]{2,1,0:T(8,128)(2,1)}, u32[]{:S(2)}) copy-start(bf16[2,256,256]{2,1,0:T(8,128)(2,1)} %constant.156.clone.refs_6_.second_out) | copy-start | bytes 786436
  119.0 24.0 %copy-start.4 = (bf16[32,192]{1,0:T(8,128)(2,1)S(1)}, bf16[32,192]{1,0:T(8,128)(2,1)}, u32[]{:S(2)}) copy-start(bf16[32,192]{1,0:T(8,128)(2,1)} %constant.153.clone.refs_3_.first_out) | copy-start | bytes 36868
  119.9 23.2 %all-to-all-start.2 = ((bf16[32,32,128]{2,1,0:T(8,128)(2,1)}), bf16[32,32,128]{2,1,0:T(8,128)(2,1)S(1)}, u32[]{:S(2)}, u32[]{:S(2)}) async-start(bf16[32,32,128]{2,1,0:T(8,128)(2,1)} %bitcast.30), calls=%async_computation.2 | async-start | bytes 524288 | tf_op jit(solution)/shard_map/all_to_all | solution.py:192
  129.9 23.0 %copy-start.6 = (f32[1024,256]{1,0:T(8,128)}, f32[1024,256]{1,0:T(8,128)S(1)}, u32[]{:S(2)}) copy-start(f32[1024,256]{1,0:T(8,128)S(1)} %shard_map.155.refs_1_) | copy-start | bytes 3145732
  129.9 21.7 %copy-start.13 = (bf16[128,1024]{1,0:T(8,128)(2,1)S(1)}, bf16[128,1024]{1,0:T(8,128)(2,1)}, u32[]{:S(2)}) copy-start(bf16[128,1024]{1,0:T(8,128)(2,1)} %param.13) | copy-start | bytes 786436
  147.0 17.6 %all-to-all-start.3 = ((bf16[32,32,128]{2,1,0:T(8,128)(2,1)}), bf16[32,32,128]{2,1,0:T(8,128)(2,1)}, u32[]{:S(2)}, u32[]{:S(2)}) async-start(bf16[32,32,128]{2,1,0:T(8,128)(2,1)} %bitcast.32), calls=%async_computation.3 | async-start | bytes 524288 | tf_op jit(solution)/shard_map/all_to_all | solution.py:196
  164.6 20.9 %copy-start.7 = (f32[1024,256]{1,0:T(8,128)S(1)}, f32[1024,256]{1,0:T(8,128)}, u32[]{:S(2)}) copy-start(f32[1024,256]{1,0:T(8,128)} %copy-done.6) | copy-start | bytes 3145732
  209.9 10.6 %collective-permute-start.1 = (bf16[128,1024]{1,0:T(8,128)(2,1)}, bf16[128,1024]{1,0:T(8,128)(2,1)S(1)}, u32[]{:S(2)}, u32[]{:S(2)}) collective-permute-start(bf16[128,1024]{1,0:T(8,128)(2,1)} %get-tuple-element.49), channel_id=1, source_target_pairs={{0,128},{128,0},{1,129},{129,1},{2,130},{130,2},{3,131},{131,3},{4... | collective-permute-start | bytes 786440 | tf_op jit(solution)/shard_map/ppermute | solution.py:188
  240.0 1.6 copy-start.8
  241.5 28.3 %collective-permute-start.2 = (bf16[2,128,2,1024]{3,1,2,0:T(8,128)(2,1)}, bf16[2,128,2,1024]{3,1,2,0:T(8,128)(2,1)}, u32[]{:S(2)}, u32[]{:S(2)}) collective-permute-start(bf16[2,128,2,1024]{3,1,2,0:T(8,128)(2,1)} %bitcast.71), channel_id=1, source_target_pairs={{0,1},{1,0},{2,3},{3,2},{4,5},{5,4},{6,7},{7,6},{8,9},{9,8},{10,11... | collective-permute-start | bytes 3145736 | tf_op jit(solution)/shard_map/ppermute | solution.py:188
  242.6 16.5 %collective-permute-start.14 = (f32[4,1024]{0,1:T(8,128)}, f32[4,1024]{0,1:T(8,128)}, u32[]{:S(2)}, u32[]{:S(2)}) collective-permute-start(f32[4,1024]{0,1:T(8,128)} %pad_maximum_fusion.5), channel_id=1, source_target_pairs={{8,0},{16,8},{24,16},{32,24},{40,32},{48,40},{56,48},{64,56},{72,6... | collective-permute-start | bytes 49160 | tf_op jit(solution)/shard_map/ppermute | solution.py:289
  268.6 42.7 %collective-permute-start.13 = (f32[2,1024]{1,0:T(2,128)S(1)}, f32[2,1024]{1,0:T(2,128)S(1)}, u32[]{:S(2)}, u32[]{:S(2)}) collective-permute-start(f32[2,1024]{1,0:T(2,128)S(1)} %slice.196), channel_id=1, source_target_pairs={{8,0},{16,8},{24,16},{32,24},{40,32},{48,40},{56,48},{64,56},{72,6... | collective-permute-start | bytes 24584 | tf_op jit(solution)/shard_map/ppermute | solution.py:285
  272.5 38.8 %copy-start.9 = (f32[128,1024]{1,0:T(8,128)S(1)}, f32[128,1024]{1,0:T(8,128)}, u32[]{:S(2)}) copy-start(f32[128,1024]{1,0:T(8,128)} %get-tuple-element.48) | copy-start | bytes 1572868
  272.6 43.1 %collective-permute-start.3 = (bf16[128,1024]{1,0:T(8,128)(2,1)S(1)}, bf16[128,1024]{1,0:T(8,128)(2,1)S(1)}, u32[]{:S(2)}, u32[]{:S(2)}) collective-permute-start(bf16[128,1024]{1,0:T(8,128)(2,1)S(1)} %get-tuple-element.38), channel_id=1, source_target_pairs={{0,0},{2,2},{4,128},{6,130},{128,4},{130,6},{132,132},{134,134},{1... | collective-permute-start | bytes 786440 | tf_op jit(solution)/shard_map/ppermute | solution.py:267
  302.2 28.7 %collective-permute-start.4 = (bf16[128,1024]{1,0:T(8,128)(2,1)S(1)}, bf16[128,1024]{1,0:T(8,128)(2,1)S(1)}, u32[]{:S(2)}, u32[]{:S(2)}) collective-permute-start(bf16[128,1024]{1,0:T(8,128)(2,1)S(1)} %get-tuple-element.41), channel_id=1, source_target_pairs={{0,2},{2,0},{4,130},{6,128},{128,6},{130,4},{132,134},{134,132},{1... | collective-permute-start | bytes 786440 | tf_op jit(solution)/shard_map/ppermute | solution.py:267
  302.3 28.6 %collective-permute-start.5 = (bf16[128,1024]{1,0:T(8,128)(2,1)S(1)}, bf16[128,1024]{1,0:T(8,128)(2,1)S(1)}, u32[]{:S(2)}, u32[]{:S(2)}) collective-permute-start(bf16[128,1024]{1,0:T(8,128)(2,1)S(1)} %get-tuple-element.40), channel_id=1, source_target_pairs={{0,128},{2,130},{4,0},{6,2},{128,132},{130,134},{132,4},{134,6},{1... | collective-permute-start | bytes 786440 | tf_op jit(solution)/shard_map/ppermute | solution.py:267
  302.6 28.3 %collective-permute-start.6 = (bf16[128,1024]{1,0:T(8,128)(2,1)S(1)}, bf16[128,1024]{1,0:T(8,128)(2,1)S(1)}, u32[]{:S(2)}, u32[]{:S(2)}) collective-permute-start(bf16[128,1024]{1,0:T(8,128)(2,1)S(1)} %get-tuple-element.39), channel_id=1, source_target_pairs={{0,130},{2,128},{4,2},{6,0},{128,134},{130,132},{132,6},{134,4},{1... | collective-permute-start | bytes 786440 | tf_op jit(solution)/shard_map/ppermute | solution.py:267
Sparse Core Ops, SparseCore 0:
  10.4 85.2 all-gather.1

commit v2 on v1

v2 whole, which is shorter than its diff:
```python
import functools
import math

import jax
import jax.numpy as jnp
import numpy as np
from jax import lax
from jax.experimental import pallas as pl
from jax.experimental.pallas import tpu as pltpu
from jax.sharding import Mesh
from jax.sharding import PartitionSpec as P

SEQ = ("zh", "y", "x")
CHAN = ("zl", "core")
BF = jnp.bfloat16
F32 = jnp.float32
FAST = 128
GROUP = 8
VMEM = 60 * 1024 * 1024


def halves(value):
    high = np.asarray(value, np.float64).astype(jnp.bfloat16)
    low = (np.asarray(value, np.float64) - high.astype(np.float64)).astype(jnp.bfloat16)
    return high, low


def tables(length):
    rows = length // FAST
    slow = np.arange(rows)
    fast = np.arange(FAST)
    angle = 2 * math.pi * np.outer(slow + 0.25, slow) / rows
    first = np.concatenate([np.cos(angle), -np.sin(angle)], axis=0)
    high, low = halves(first)
    first_in = np.concatenate([high, low, high], axis=1)
    back = np.concatenate([np.cos(angle.T), -np.sin(angle.T)], axis=1) / length
    high, low = halves(back)
    first_out = np.concatenate([high, low, high], axis=1)
    twist = 2 * math.pi * np.outer(slow + 0.25, fast) / length
    twist = np.stack([np.cos(twist), np.sin(twist)]).astype(np.float32)
    turn = 2 * math.pi * np.outer(fast, fast) / FAST
    cos, sin = np.cos(turn), np.sin(turn)
    second_in = np.stack(halves(np.block([[cos, -sin], [sin, cos]])))
    second_out = np.stack(halves(np.block([[cos, sin], [-sin, cos]])))
    return first_in, first_out, twist, second_in, second_out


def split(value):
    high = value.astype(BF)
    return high, (value - high.astype(F32)).astype(BF)


def dot(first, second):
    return jnp.dot(first, second, preferred_element_type=F32)


def dot_wide(value, table):
    high, low = split(value)
    return dot(high, table[0]) + (dot(low, table[0]) + dot(high, table[1]))


def group_forward(held, group, first_in, twist, second_in):
    rows = twist.shape[1]
    channels = held.shape[0] // rows
    signal = jnp.concatenate(
        [held[pl.ds(group * GROUP + i, rows, stride=channels), :] for i in range(GROUP)], axis=1
    )
    high, low = split(signal)
    first = dot(first_in[...], jnp.concatenate([high, high, low], axis=0))
    cos, sin = twist[0], twist[1]
    parts = []
    for i in range(GROUP):
        real = first[:rows, i * FAST : (i + 1) * FAST]
        imag = first[rows:, i * FAST : (i + 1) * FAST]
        parts.append(jnp.concatenate([real * cos + imag * sin, imag * cos - real * sin], axis=1))
    return dot_wide(jnp.concatenate(parts, axis=0), second_in)


def group_inverse(spectrum, group, first_out, twist, second_out, held):
    rows = twist.shape[1]
    channels = held.shape[0] // rows
    back = dot_wide(spectrum, second_out)
    cos, sin = twist[0], twist[1]
    real_parts, imag_parts = [], []
    for i in range(GROUP):
        real = back[i * rows : (i + 1) * rows, :FAST]
        imag = back[i * rows : (i + 1) * rows, FAST:]
        real_parts.append(real * cos - imag * sin)
        imag_parts.append(real * sin + imag * cos)
    turned = jnp.concatenate(
        [jnp.concatenate(real_parts, axis=1), jnp.concatenate(imag_parts, axis=1)], axis=0
    )
    high, low = split(turned)
    result = dot(first_out[...], jnp.concatenate([high, high, low], axis=0))
    for i in range(GROUP):
        held[pl.ds(group * GROUP + i, rows, stride=channels), :] = result[:, i * FAST : (i + 1) * FAST]


def product_of(first, second, conjugate):
    first_re, first_im = first[:, :FAST], first[:, FAST:]
    second_re, second_im = second[:, :FAST], second[:, FAST:]
    if conjugate:
        return jnp.concatenate(
            [
                first_re * second_re + first_im * second_im,
                first_im * second_re - first_re * second_im,
            ],
            axis=1,
        )
    return jnp.concatenate(
        [
            first_re * second_re - first_im * second_im,
            first_re * second_im + first_im * second_re,
        ],
        axis=1,
    )


def filter_kernel(signal, first_in, twist, second_in, spectrum, held):
    rows = twist.shape[1]
    channels = signal.shape[0]
    for n1 in range(rows):
        held[n1 * channels : (n1 + 1) * channels, :] = signal[:, n1 * FAST : (n1 + 1) * FAST]
    step = GROUP * rows
    for group in range(channels // GROUP):
        spectrum[group * step : (group + 1) * step, :] = group_forward(
            held, group, first_in, twist, second_in
        )


def convolve_kernel(
    conjugate, signal, filter_spec, first_in, first_out, twist, second_in, second_out,
    result, spectrum, held, out,
):
    rows = twist.shape[1]
    channels = held.shape[0] // rows
    step = GROUP * rows

    def line(n1):
        return slice(n1 * channels, (n1 + 1) * channels)

    if len(signal.shape) == 2:
        held[...] = signal[...].astype(F32)
    else:
        for n1 in range(rows):
            held[line(n1), :] = signal[n1 % signal.shape[0], n1 // signal.shape[0]].astype(F32)
    for group in range(channels // GROUP):
        here = slice(group * step, (group + 1) * step)
        spec = group_forward(held, group, first_in, twist, second_in)
        spectrum[here, :] = spec
        both = product_of(spec, filter_spec[here, :], conjugate)
        group_inverse(both, group, first_out, twist, second_out, out)
    if len(result.shape) == 2:
        result[...] = out[...].astype(result.dtype)
    else:
        for n1 in range(rows):
            result[n1 % result.shape[0], n1 // result.shape[0]] = out[line(n1), :].astype(result.dtype)


def filter_grad_kernel(first_spec, second_spec, first_out, twist, second_out, result, out):
    rows = twist.shape[1]
    channels = result.shape[0]
    scale = result.shape[1] ** -0.5
    step = GROUP * rows
    for group in range(channels // GROUP):
        here = slice(group * step, (group + 1) * step)
        both = product_of(first_spec[here, :], second_spec[here, :], True) * scale
        group_inverse(both, group, first_out, twist, second_out, out)
    for n1 in range(rows):
        result[:, n1 * FAST : (n1 + 1) * FAST] = out[n1 * channels : (n1 + 1) * channels, :]


def whole(array):
    return pl.BlockSpec(array.shape, lambda *_: (0,) * len(array.shape))


def call(kernel, out_shape, scratch, *args, grid=(), specs=None, out_specs=None, flops=1024):
    specs = specs or {}
    return pl.pallas_call(
        kernel,
        out_shape=out_shape,
        grid=grid,
        in_specs=[specs.get(i, whole(arg)) for i, arg in enumerate(args)],
        out_specs=out_specs or jax.tree.map(whole, out_shape),
        scratch_shapes=scratch,
        compiler_params=pltpu.CompilerParams(vmem_limit_bytes=VMEM),
        cost_estimate=pl.CostEstimate(flops=flops, bytes_accessed=1024, transcendentals=0),
    )(*args)


def position(*names):
    return tuple(lax.axis_index(name) for name in names)


def shape_of(dims, dtype):
    return jax.ShapeDtypeStruct(dims, dtype)


PAD = 16


def taps_of(short_filter, branch, columns=slice(None)):
    return [short_filter[tap, branch : branch + 1, columns] for tap in range(3)]


def causal_rows(joined, taps):
    extent = joined.shape[0] - 8
    return (
        taps[0] * joined[8:] + taps[1] * joined[7 : 7 + extent] + taps[2] * joined[6 : 6 + extent]
    )


def causal(signal, halo, short_filter, branch):
    before = halo[branch * PAD : (branch + 1) * PAD, :].astype(F32)[PAD - 8 :]
    joined = jnp.concatenate([before, signal[...].astype(F32)], axis=0)
    return causal_rows(joined, taps_of(short_filter, branch))


def adjoint(signal, after, taps):
    extent = signal.shape[0]
    joined = jnp.concatenate([signal, after], axis=0)
    return (
        taps[0] * joined[:extent]
        + taps[1] * joined[1 : extent + 1]
        + taps[2] * joined[2 : extent + 2]
    )


def turned(value):
    return jnp.concatenate(
        [value[:, i : i + 128].T for i in range(0, value.shape[1], 128)], axis=0
    )


def turned_back(rows):
    rows = rows.astype(F32)
    return jnp.concatenate(
        [rows[i : i + 128].T for i in range(0, rows.shape[0], 128)], axis=1
    )


def gated_kernel(key, value, halo, short_filter, result):
    gated = causal(key, halo, short_filter, 1) * causal(value, halo, short_filter, 2)
    result[...] = turned(gated).astype(BF)


def columns_of(which, width):
    return pl.ds(pl.multiple_of((lax.axis_index("zh") ^ which) * width, width), width)


def halo_kernel(query, key, value, result):
    for branch, ref in enumerate((query, key, value)):
        result[branch * PAD : (branch + 1) * PAD, :] = ref[...]


def query_split_kernel(query, halo, keep, give):
    for which, result in ((0, keep), (1, give)):
        columns = columns_of(which, result.shape[1])
        result[:PAD, :] = halo[:PAD, columns]
        result[PAD:, :] = query[:, columns]


def query_conv(query, short_filter):
    taps = taps_of(short_filter, 0, columns_of(0, query.shape[1]))
    return causal_rows(query[...].astype(F32)[PAD - 8 :], taps)


def product_kernel(own, other, short_filter, mixed_rows, product, mixed):
    for half, query in enumerate((own, other)):
        there = lax.axis_index("zh") ^ half
        sources, _, channels, _ = mixed_rows.shape
        blocks = []
        for first in range(0, sources * channels, 128):
            rows = [
                mixed_rows[s, there] for s in range(first // channels, (first + 128) // channels)
            ]
            blocks.append(jnp.concatenate(rows, axis=0).astype(F32).T)
        here = jnp.concatenate(blocks, axis=1)
        mixed[half] = here.astype(BF)
        product[half] = (query_conv(query, short_filter) * here).astype(BF)


def mixed_grad_kernel(
    keep, beside, own, other, short_filter, mixed, result, conv_grad, edge
):
    channels = result.shape[2]
    for half, query in enumerate((own, other)):
        out_grad = keep[half] + beside[1 - half].astype(F32)
        rows = turned(out_grad * query_conv(query, short_filter)).astype(BF)
        for s in range(result.shape[0]):
            result[s, lax.axis_index("zh") ^ half] = rows[s * channels : (s + 1) * channels]
        query_grad = out_grad * mixed[half].astype(F32)
        conv_grad[half] = query_grad
        edge[half] = query_grad[:8]


def query_grad_kernel(conv_grad, after, short_filter, keep, give):
    taps = taps_of(short_filter, 0, columns_of(0, keep.shape[1]))
    zh, y, x = position("zh", "y", "x")
    last = (y == 3) & (x == 3)
    for half, result in ((0, keep), (1, give)):
        beyond = jnp.where((zh ^ half) == 0, after[1 - half], 0.0)
        rows = jnp.where(last, beyond, after[half])
        result[...] = adjoint(conv_grad[half], rows, taps).astype(BF)


def query_join_kernel(keep, beside, result):
    width = keep.shape[1]
    result[:, columns_of(0, width)] = keep[...]
    result[:, columns_of(1, width)] = beside[...]


def edge_kernel(key, value, halo, short_filter, gated_grad_rows, key_grad, value_grad, edge):
    gated_grad = turned_back(gated_grad_rows[...])
    key_here = gated_grad * causal(value, halo, short_filter, 2)
    value_here = gated_grad * causal(key, halo, short_filter, 1)
    key_grad[...] = key_here
    value_grad[...] = value_here
    edge[:8] = key_here[:8]
    edge[8:] = value_here[:8]


def last_kernel(key_conv_grad, value_conv_grad, after, short_filter, key_grad, value_grad):
    key_grad[...] = adjoint(key_conv_grad[...], after[:8], taps_of(short_filter, 1)).astype(BF)
    value_grad[...] = adjoint(value_conv_grad[...], after[8:], taps_of(short_filter, 2)).astype(BF)


def backward_kernel(cot, beside, weight, keep, give, both, total):
    row = pl.program_id(0)
    zh, zl, core = position("zh", "zl", "core")
    tokens, half_width = keep.shape[1:]

    @pl.when(row == 0)
    def _():
        both[0] = cot[...]
        both[1] = beside[...]
        total[...] = jnp.zeros_like(total)

    which, k1 = (row % 2) ^ core, (row // 2) ^ (zl % 2)
    lines = jnp.concatenate(
        [both[which, (half ^ zh ^ (zl // 2)) * 2 + k1] for half in range(2)], axis=0
    )
    across = (((1,), (1,)), ((), ()))
    for part in range(2):
        here = slice(part * half_width, (part + 1) * half_width)
        rows = jnp.concatenate([weight[i, here, :] for i in range(4)], axis=1)
        total[part] += lax.dot_general(lines, rows, across, preferred_element_type=F32)

    @pl.when(row == 3)
    def _():
        for half in range(2):
            here = slice(half * tokens, (half + 1) * tokens)
            keep[half] = total[zh, here, :]
            give[half] = total[1 - zh, here, :].astype(BF)


def forward_kernel(product, beside, weight, result):
    zh = lax.axis_index("zh")
    tokens = product.shape[1]
    own = jnp.concatenate([product[0], product[1]], axis=0)
    other = jnp.concatenate([beside[1], beside[0]], axis=0)
    left = jnp.concatenate(
        [jnp.where(zh == 0, own, other), jnp.where(zh == 0, other, own)], axis=1
    )
    rows = jnp.concatenate([weight[i] for i in range(4)], axis=1)
    term = jnp.dot(left, rows, preferred_element_type=F32).astype(BF)
    for half in range(2):
        result[half ^ zh, 0] = term[half * tokens : (half + 1) * tokens]


def swap(value, axis):
    return lax.ppermute(value, axis, [(0, 1), (1, 0)])


def exchange(value):
    return lax.all_to_all(value, ("y", "x"), split_axis=0, concat_axis=0, tiled=True)


def once(value, *others):
    return lax.optimization_barrier((value,) + others)[0]


def shards(query, key, value, short_filter, long_filter, out_weight, cotangent):
    tokens, width = query.shape
    seq_count = lax.axis_size(SEQ)
    length = tokens * seq_count
    channels = width // seq_count
    first_in, first_out, twist, second_in, second_out = (jnp.asarray(t) for t in tables(length))
    spec_type = shape_of((channels * length // FAST, 2 * FAST), F32)
    rows_type = shape_of((length // FAST * channels, FAST), BF)
    tokens_bf, tokens_f32 = shape_of((tokens, width), BF), shape_of((tokens, width), F32)
    held = pltpu.VMEM(rows_type.shape, F32)

    half = width // 2
    split_type = shape_of((16, 2, channels, FAST), BF)
    halves_bf = shape_of((2, tokens, half), BF)
    halves_f32 = shape_of((2, tokens, half), F32)

    weight = lax.all_gather(out_weight, ("y", "x"))

    def links(k1, k2, back):
        result = []
        for a in range(2):
            for u in range(2):
                for v in range(2):
                    chip, owner = a * 4 + u * 2 + v, (u ^ k2) * 4 + a * 2 + (v ^ k1)
                    result.append((chip, owner) if back else (owner, chip))
        return result


    last_rows = pl.BlockSpec((PAD, width), lambda *_: (tokens // PAD - 1, 0))
    halo = call(
        halo_kernel, shape_of((3 * PAD, width), BF), [], query, key, value,
        grid=(1,), specs={i: last_rows for i in range(3)},
    )
    halo = lax.ppermute(halo, SEQ, [(i, i + 1) for i in range(seq_count - 1)])
    filter_spec = call(filter_kernel, spec_type, [held], long_filter, first_in, twist, second_in)
    halo = once(halo, filter_spec)
    gated_rows = call(gated_kernel, rows_type, [], key, value, halo, short_filter)
    gated_rows = lax.all_to_all(gated_rows, SEQ, split_axis=0, concat_axis=0, tiled=True)

    query_type = shape_of((PAD + tokens, half), BF)
    query_own, query_other = call(
        query_split_kernel, (query_type, query_type), [], query, halo
    )
    query_other = swap(query_other, "zh")

    cot_there = once(cotangent, gated_rows)
    blocks = [
        lax.ppermute(cot_there, ("zh", "zl"), links(k1, k2, False)) for k2 in range(2) for k1 in range(2)
    ]
    gated_rows = once(gated_rows, query_other)
    mixed_rows, gated_spec = call(
        functools.partial(convolve_kernel, False), (split_type, spec_type), [held, held],
        gated_rows, filter_spec, first_in, first_out, twist, second_in, second_out,
    )
    mixed_rows = exchange(mixed_rows)
    product, mixed = call(
        product_kernel, (halves_bf, halves_bf), [],
        query_own, query_other, short_filter, mixed_rows,
    )
    product_beside = swap(product, "zh")
    got = jnp.stack(once(tuple(blocks), product))
    got_beside = swap(got, "core")

    four = pl.BlockSpec((4,) + out_weight.shape, lambda row: (row, 0, 0))
    grads, grads_beside = call(
        backward_kernel, (halves_f32, halves_bf),
        [pltpu.VMEM((2, 4, tokens, width), BF), pltpu.VMEM((2, 2 * tokens, half), F32)],
        got, got_beside, weight, grid=(4,), specs={2: four},
    )
    product_beside = once(product_beside, grads_beside)
    grads_beside = swap(grads_beside, "zh")

    partial = call(
        forward_kernel, shape_of((2, 4, tokens, width), BF), [],
        product, product_beside, weight, grid=(4,), specs={2: four}, flops=1 << 34,
        out_specs=pl.BlockSpec((2, 1, tokens, width), lambda row: (0, row, 0, 0)),
    )
    summed = lax.psum_scatter(partial.reshape(8, tokens, width), CHAN, scatter_dimension=0)
    block_output = lax.ppermute(summed, ("zh", "zl"), links(0, 0, True))

    mixed_grad_rows, query_conv_grad, query_edge = call(
        mixed_grad_kernel, (split_type, halves_f32, shape_of((2, 8, half), F32)), [],
        grads, once(grads_beside, partial), query_own, query_other, short_filter, mixed, flops=1 << 33,
    )
    query_after = lax.ppermute(query_edge, ("y", "x"), [((i + 1) % 16, i) for i in range(16)])
    mixed_grad_rows = exchange(mixed_grad_rows)
    half_type = shape_of((tokens, half), BF)
    query_grad, query_grad_other = call(
        query_grad_kernel, (half_type, half_type), [],
        query_conv_grad, query_after, short_filter,
    )
    gated_grad_rows, mixed_spec = call(
        functools.partial(convolve_kernel, True), (rows_type, spec_type), [held, held],
        once(mixed_grad_rows, query_grad_other), filter_spec, first_in, first_out, twist, second_in, second_out,
        flops=1 << 35,
    )
    gated_grad_rows = lax.all_to_all(gated_grad_rows, SEQ, split_axis=0, concat_axis=0, tiled=True)
    filter_grad = call(
        filter_grad_kernel, shape_of((channels, length), F32), [held],
        mixed_spec, gated_spec, first_out, twist, second_out,
    )
    back = [(i + 1, i) for i in range(seq_count - 1)]
    query_grad_other = swap(query_grad_other, "zh")
    query_grad = call(
        query_join_kernel, tokens_bf, [], query_grad, query_grad_other
    )
    key_conv_grad, value_conv_grad, edge = call(
        edge_kernel, (tokens_f32, tokens_f32, shape_of((16, width), F32)), [],
        key, value, halo, short_filter, gated_grad_rows, flops=1 << 33,
    )
    after = lax.ppermute(edge, SEQ, back)
    key_grad, value_grad = call(
        last_kernel, (tokens_bf, tokens_bf), [], key_conv_grad, value_conv_grad, once(after, filter_grad), short_filter
    )
    return (block_output, query_grad, key_grad, value_grad, filter_grad)


def solution(mesh):
    fine = Mesh(mesh.devices.reshape(2, 4, 4, 4, 2), SEQ + CHAN)
    return jax.shard_map(
        shards,
        mesh=fine,
        in_specs=(
            P(SEQ, CHAN),
            P(SEQ, CHAN),
            P(SEQ, CHAN),
            P(None, None, CHAN),
            P(CHAN + SEQ, None),
            P(CHAN, SEQ),
            P(SEQ, CHAN),
        ),
        out_specs=(
            P(SEQ, CHAN),
            P(SEQ, CHAN),
            P(SEQ, CHAN),
            P(SEQ, CHAN),
            P(CHAN + SEQ, None),
        ),
        check_vma=False,
    )
```

time: 340 us -> 197 us (0.58)
  the two profiles are of different devices: /device:TPU:96 before, /device:TPU:2 now
where the time goes in v2:
time: 197 us; the launch traced here: 193 us
  starting transfers between devices  85 us (43%)
  Pallas kernels  50.7 us (26%)
  waiting for transfers between devices  21.6 us (11%)
  blocking collectives  15.7 us (8%)
  between operations  14.2 us (7%)
  local copies, waits for them, and re-layouts  6.06 us (3%)
    pallas_call x15, Pallas kernels, call(): pl.pallas_call(kernel, out_shape=out_shape, grid=grid, in_specs=[specs.ge...  50.7 us
    ppermute x5, starting transfers between devices, swap(): return lax.ppermute(value, axis, [(0, 1), (1, 0)])  26.7 us
    all_to_all x1, starting transfers between devices, shards(): lax.all_to_all(gated_grad_rows, SEQ, split_axis=0, concat_axis=0, tiled=T...  18.3 us
    all_to_all x1, starting transfers between devices, shards(): lax.all_to_all(gated_rows, SEQ, split_axis=0, concat_axis=0, tiled=True)  17.3 us
    all_to_all x1, blocking collectives, exchange(): lax.all_to_all(value, ('y', 'x'), split_axis=0, concat_axis=0, tiled=True)  15.7 us
    ppermute x4, starting transfers between devices, shards(): lax.ppermute(cot_there, ('zh', 'zl'), links(k1, k2, False))  7.73 us
    all_to_all x1, waiting for transfers between devices, shards(): lax.all_to_all(gated_rows, SEQ, split_axis=0, concat_axis=0, tiled=True)  7.52 us
    all_to_all x1, waiting for transfers between devices, shards(): lax.all_to_all(gated_grad_rows, SEQ, split_axis=0, concat_axis=0, tiled=T...  6.08 us
  transfers between devices with their start and end apart: 18, of which 6 were waited for; matrix products, arithmetic and copies ran while one was open for 0% of the time, Pallas kernels for 26%

profile of v2, /device:TPU:2, one launch (start us, length us, event | category | flops | bytes accessed | tf_op | source)
XLA Modules:
  0.0 193.3 jit_solution(14200071435078434072)
XLA Ops:
  7.2 0.7 all-gather.3.cloned.1.call-update
  7.9 1.4 shard_map.155
  9.3 3.4 %collective-permute-start = (bf16[48,1024]{1,0:T(8,128)(2,1)}, bf16[48,1024]{1,0:T(8,128)(2,1)S(1)}, u32[]{:S(2)}, u32[]{:S(2)}) collective-permute-start(bf16[48,1024]{1,0:T(8,128)(2,1)} %shard_map.155), channel_id=1, source_target_pairs={{0,8},{8,16},{16,24},{24,32},{32,40},{40,48},{48,56},{56,64},{64,7... | collective-permute-start | bytes 294920 | tf_op jit(solution)/shard_map/ppermute | solution.py:416
  12.7 3.1 %shard_map.156.filter_spec = f32[1024,256]{1,0:T(8,128)} custom-call(f32[32,4096]{1,0:T(8,128)} %signal.1, bf16[64,96]{1,0:T(8,128)(2,1)} %constant.10.clone.first_in, f32[2,32,128]{2,1,0:T(8,128)} %constant.12.clone.twist, bf16[2,256,256]{2,1,0:T(8,128)(2,1)} %constant.13.clone.second_in), custom_call_target="tpu_custom_call" | custom-call | flops 1024 | bytes 1024 | tf_op jit(solution)/shard_map/pallas_call | solution.py:179
  15.8 0.2 collective-permute-done.halo
  16.1 0.6 copy-done.3
  16.7 2.3 %shard_map.158 = bf16[1024,128]{1,0:T(8,128)(2,1)} custom-call(bf16[128,1024]{1,0:T(8,128)(2,1)} %key.5, bf16[128,1024]{1,0:T(8,128)(2,1)} %value.5, bf16[48,1024]{1,0:T(8,128)(2,1)} %copy-done.3, f32[3,3,1024]{2,1,0:T(4,128)} %short_filter.11), custom_call_target="tpu_custom_call" | custom-call | flops 1024 | bytes 1024 | tf_op jit(solution)/shard_map/pallas_call | solution.py:179
  18.9 17.3 %all-to-all-start = ((bf16[32,32,128]{2,1,0:T(8,128)(2,1)}), bf16[32,32,128]{2,1,0:T(8,128)(2,1)S(1)}, u32[]{:S(2)}, u32[]{:S(2)}) async-start(bf16[32,32,128]{2,1,0:T(8,128)(2,1)} %bitcast.14), calls=%async_computation | async-start | bytes 524288 | tf_op jit(solution)/shard_map/all_to_all | solution.py:420
  36.3 1.7 shard_map.157
  38.0 5.4 %collective-permute-start.1 = (bf16[144,512]{1,0:T(8,128)(2,1)}, bf16[144,512]{1,0:T(8,128)(2,1)S(1)}, u32[]{:S(2)}, u32[]{:S(2)}) collective-permute-start(bf16[144,512]{1,0:T(8,128)(2,1)} %get-tuple-element.38), channel_id=1, source_target_pairs={{0,128},{128,0},{1,129},{129,1},{2,130},{130,2},{3,131},{131,3},{4... | collective-permute-start | bytes 442376 | tf_op jit(solution)/shard_map/ppermute | solution.py:372
  43.4 7.5 %all-to-all-done = bf16[32,32,128]{2,1,0:T(8,128)(2,1)S(1)} async-done(((bf16[32,32,128]{2,1,0:T(8,128)(2,1)}), bf16[32,32,128]{2,1,0:T(8,128)(2,1)S(1)}, u32[]{:S(2)}, u32[]{:S(2)}) %all-to-all-start) | async-done | bytes 262176 | tf_op jit(solution)/shard_map/all_to_all | solution.py:420
  50.9 1.9 collective-permute-start.6
  52.8 3.7 %collective-permute-start.5 = (bf16[128,1024]{1,0:T(8,128)(2,1)}, bf16[128,1024]{1,0:T(8,128)(2,1)S(1)}, u32[]{:S(2)}, u32[]{:S(2)}) collective-permute-start(bf16[128,1024]{1,0:T(8,128)(2,1)} %param.18), channel_id=1, source_target_pairs={{128,0},{130,2},{0,4},{2,6},{132,128},{134,130},{4,132},{6,134},{1... | collective-permute-start | bytes 786440 | tf_op jit(solution)/shard_map/ppermute | solution.py:430
  56.5 0.6 collective-permute-start.4
  57.1 1.6 collective-permute-start.3
  58.7 5.5 %shard_map.159 = (bf16[16,2,32,128]{3,2,1,0:T(8,128)(2,1)}, f32[1024,256]{1,0:T(8,128)}) custom-call(bf16[1024,128]{1,0:T(8,128)(2,1)} %bitcast.15, f32[1024,256]{1,0:T(8,128)} %shard_map.156.filter_spec, bf16[64,96]{1,0:T(8,128)(2,1)} %constant.10.clone.first_in, bf16[32,192]{1,0:T(8,128)(2,1)} %constant.11.clone.first_out, ...), custom_call_target="tpu_custom_call" | custom-call | flops 1024 | bytes 1024 | tf_op jit(solution)/shard_map/pallas_call | solution.py:179
  64.2 15.7 %all_to_all.33.mixed_rows = bf16[16,2,32,128]{3,2,1,0:T(8,128)(2,1)} all-to-all(bf16[16,2,32,128]{3,2,1,0:T(8,128)(2,1)} %get-tuple-element.40), channel_id=1, replica_groups=mesh['zh'=2,'y'=4,'x'=4,'zl'=4,'core'=2] {'y','x'}, dimensions={0} | all-to-all | bytes 524288 | tf_op jit(solution)/shard_map/all_to_all | solution.py:376
  79.9 2.2 %shard_map.160 = (bf16[2,128,512]{2,1,0:T(8,128)(2,1)}, bf16[2,128,512]{2,1,0:T(8,128)(2,1)}) custom-call(bf16[144,512]{1,0:T(8,128)(2,1)} %get-tuple-element.37.own, bf16[144,512]{1,0:T(8,128)(2,1)} %copy-done.6, f32[3,3,1024]{2,1,0:T(4,128)} %short_filter.11, bf16[16,2,32,128]{3,2,1,0:T(8,128)(2,1)} %all_to_all.33.mixed_rows), custom_call_target="tpu_custom_call" | custom-call | flops 1024 | bytes 1024 | tf_op jit(solution)/shard_map/pallas_call | solution.py:179
  82.1 0.1 pad_maximum_fusion.cot
  82.3 10.0 %collective-permute-start.2 = (bf16[2,128,512]{2,1,0:T(8,128)(2,1)}, bf16[2,128,512]{2,1,0:T(8,128)(2,1)S(1)}, u32[]{:S(2)}, u32[]{:S(2)}) collective-permute-start(bf16[2,128,512]{2,1,0:T(8,128)(2,1)} %get-tuple-element.41.product), channel_id=1, source_target_pairs={{0,128},{128,0},{1,129},{129,1},{2,130},{130,2},{3,131},{131,3},{4... | collective-permute-start | bytes 786440 | tf_op jit(solution)/shard_map/ppermute | solution.py:372
  92.4 1.6 all-gather.3.cloned.1.call-done
  94.0 7.3 %shard_map.161 = (f32[2,128,512]{2,1,0:T(8,128)}, bf16[2,128,512]{2,1,0:T(8,128)(2,1)}) custom-call(bf16[4,128,1024]{2,1,0:T(8,128)(2,1)} %copy-done, bf16[4,128,1024]{2,1,0:T(8,128)(2,1)} %copy-done.1, bf16[16,1024,256]{2,1,0:T(8,128)(2,1)} %bitcast.11), custom_call_target="tpu_custom_call" | custom-call | flops 1024 | bytes 1024 | tf_op jit(solution)/shard_map/pallas_call | solution.py:179
  101.3 5.7 %collective-permute-start.9 = (bf16[2,128,512]{2,1,0:T(8,128)(2,1)}, bf16[2,128,512]{2,1,0:T(8,128)(2,1)S(1)}, u32[]{:S(2)}, u32[]{:S(2)}) collective-permute-start(bf16[2,128,512]{2,1,0:T(8,128)(2,1)} %get-tuple-element.47), channel_id=1, source_target_pairs={{0,128},{128,0},{1,129},{129,1},{2,130},{130,2},{3,131},{131,3},{4... | collective-permute-start | bytes 786440 | tf_op jit(solution)/shard_map/ppermute | solution.py:372
  107.0 0.7 copy-done.11
  107.7 6.6 %shard_map.162 = bf16[2,4,128,1024]{3,2,1,0:T(8,128)(2,1)} custom-call(bf16[2,128,512]{2,1,0:T(8,128)(2,1)} %get-tuple-element.41.product, bf16[2,128,512]{2,1,0:T(8,128)(2,1)} %copy-done.11, bf16[16,1024,256]{2,1,0:T(8,128)(2,1)} %bitcast.12), custom_call_target="tpu_custom_call" | custom-call | flops 17179869184 | bytes 1024 | tf_op jit(solution)/shard_map/pallas_call | solution.py:179
  114.4 0.9 collective-permute-done.9.beside
  115.3 0.7 copy-done.10
  116.0 2.5 %shard_map.163 = (bf16[16,2,32,128]{3,2,1,0:T(8,128)(2,1)}, f32[2,128,512]{2,1,0:T(8,128)}, f32[2,8,512]{2,1,0:T(8,128)}) custom-call(f32[2,128,512]{2,1,0:T(8,128)} %get-tuple-element.49.keep, bf16[2,128,512]{2,1,0:T(8,128)(2,1)} %copy-done.10, bf16[144,512]{1,0:T(8,128)(2,1)} %get-tuple-element.37.own, bf16[144,512]{1,0:T(8,128)(2,1)} %copy-done.6, ...), custom_call_target="tpu_custom_call" | custom-call | flops 8589934592 | bytes 1024 | tf_op jit(solution)/shard_map/pallas_call | solution.py:179
  118.5 5.9 %all-to-all-start.2 = ((bf16[16,2,32,128]{3,2,1,0:T(8,128)(2,1)}), bf16[16,2,32,128]{3,2,1,0:T(8,128)(2,1)S(1)}, u32[]{:S(2)}, u32[]{:S(2)}) async-start(bf16[16,2,32,128]{3,2,1,0:T(8,128)(2,1)} %get-tuple-element.56), calls=%async_computation.3 | async-start | bytes 524288 | tf_op jit(solution)/shard_map/all_to_all | solution.py:376
  124.4 0.4 collective-permute-start.10
  124.8 4.4 %collective-permute-done.10.after = f32[2,8,512]{2,1,0:T(8,128)S(1)} collective-permute-done((f32[2,8,512]{2,1,0:T(8,128)}, f32[2,8,512]{2,1,0:T(8,128)S(1)}, u32[]{:S(2)}, u32[]{:S(2)}) %collective-permute-start.10) | collective-permute-done | bytes 32800 | tf_op jit(solution)/shard_map/ppermute | solution.py:467
  129.2 0.6 copy-done.9
  129.8 1.9 shard_map.164
  131.7 0.7 copy-done.4
  132.4 5.5 %shard_map.166 = (bf16[1024,128]{1,0:T(8,128)(2,1)}, f32[1024,256]{1,0:T(8,128)}) custom-call(bf16[16,2,32,128]{3,2,1,0:T(8,128)(2,1)} %copy-done.4, f32[1024,256]{1,0:T(8,128)} %shard_map.156.filter_spec, bf16[64,96]{1,0:T(8,128)(2,1)} %constant.10.clone.first_in, bf16[32,192]{1,0:T(8,128)(2,1)} %constant.11.clone.first_out, ...), custom_call_target="tpu_custom_call" | custom-call | flops 34359738368 | bytes 1024 | tf_op jit(solution)/shard_map/pallas_call | solution.py:179
  137.9 18.3 %all-to-all-start.3 = ((bf16[32,32,128]{2,1,0:T(8,128)(2,1)}), bf16[32,32,128]{2,1,0:T(8,128)(2,1)S(1)}, u32[]{:S(2)}, u32[]{:S(2)}) async-start(bf16[32,32,128]{2,1,0:T(8,128)(2,1)} %bitcast.17), calls=%async_computation.4 | async-start | bytes 524288 | tf_op jit(solution)/shard_map/all_to_all | solution.py:479
  156.2 5.5 %collective-permute-start.11 = (bf16[128,512]{1,0:T(8,128)(2,1)S(1)}, bf16[128,512]{1,0:T(8,128)(2,1)S(1)}, u32[]{:S(2)}, u32[]{:S(2)}) collective-permute-start(bf16[128,512]{1,0:T(8,128)(2,1)S(1)} %copy-done.12), channel_id=1, source_target_pairs={{0,128},{128,0},{1,129},{129,1},{2,130},{130,2},{3,131},{131,3},{4... | collective-permute-start | bytes 393224 | tf_op jit(solution)/shard_map/ppermute | solution.py:372
  161.7 1.6 collective-permute-start.8
  163.3 6.1 %all-to-all-done.3 = bf16[32,32,128]{2,1,0:T(8,128)(2,1)S(1)} async-done(((bf16[32,32,128]{2,1,0:T(8,128)(2,1)}), bf16[32,32,128]{2,1,0:T(8,128)(2,1)S(1)}, u32[]{:S(2)}, u32[]{:S(2)}) %all-to-all-start.3) | async-done | bytes 262176 | tf_op jit(solution)/shard_map/all_to_all | solution.py:479
  169.4 0.7 copy-done.5
  170.1 2.6 %shard_map.167 = (f32[128,1024]{1,0:T(8,128)}, f32[128,1024]{1,0:T(8,128)}, f32[16,1024]{1,0:T(8,128)}) custom-call(bf16[128,1024]{1,0:T(8,128)(2,1)} %key.5, bf16[128,1024]{1,0:T(8,128)(2,1)} %value.5, bf16[48,1024]{1,0:T(8,128)(2,1)} %copy-done.3, f32[3,3,1024]{2,1,0:T(4,128)} %short_filter.11, bf16[1024,128]{1,0:T(8,128)(2,1)} %bitcast.16), custom_call_target="tpu_custom_call" | custom-call | flops 8589934592 | bytes 1024 | tf_op jit(solution)/shard_map/pallas_call | solution.py:179
  172.7 3.7 %collective-permute-start.12 = (f32[16,1024]{1,0:T(8,128)}, f32[16,1024]{1,0:T(8,128)S(1)}, u32[]{:S(2)}, u32[]{:S(2)}) collective-permute-start(f32[16,1024]{1,0:T(8,128)} %get-tuple-element.61), channel_id=1, source_target_pairs={{8,0},{16,8},{24,16},{32,24},{40,32},{48,40},{56,48},{64,56},{72,6... | collective-permute-start | bytes 196616 | tf_op jit(solution)/shard_map/ppermute | solution.py:493
  176.4 0.6 copy-done.7
  177.1 1.7 shard_map.165
  178.8 4.1 %shard_map.168 = f32[32,4096]{1,0:T(8,128)} custom-call(f32[1024,256]{1,0:T(8,128)} %get-tuple-element.62.first_spec, f32[1024,256]{1,0:T(8,128)} %get-tuple-element.63.second_spec, bf16[32,192]{1,0:T(8,128)(2,1)} %constant.11.clone.first_out, f32[2,32,128]{2,1,0:T(8,128)} %constant.12.clone.twist, bf16[2,256,256]{2,1,0:T(8,128)(2,1)} %constant.14.clone.second_out), custom_call_target="tpu_custom_call" | custom-call | flops 1024 | bytes 1024 | tf_op jit(solution)/shard_map/pallas_call | solution.py:179
  182.9 0.6 copy-done.8
  183.5 2.3 %shard_map.169 = (bf16[128,1024]{1,0:T(8,128)(2,1)}, bf16[128,1024]{1,0:T(8,128)(2,1)}) custom-call(f32[128,1024]{1,0:T(8,128)} %get-tuple-element.59.key_conv_grad, f32[128,1024]{1,0:T(8,128)} %get-tuple-element.60.value_conv_grad, f32[16,1024]{1,0:T(8,128)} %copy-done.8, f32[3,3,1024]{2,1,0:T(4,128)} %short_filter.11), custom_call_target="tpu_custom_call" | custom-call | flops 1024 | bytes 1024 | tf_op jit(solution)/shard_map/pallas_call | solution.py:179
  185.8 0.7 copy.18
  (34 shorter events, 0.3 us)
Async XLA Ops:
  7.2 86.8 %all-gather.3.cloned.1.call-start = ((), (), s32[]{:S(2)}) async-start(), calls=%async_computation.6 | async-start | bytes 8912896 | tf_op jit(solution)/shard_map/all_gather | solution.py:399
  9.3 6.7 %collective-permute-start = (bf16[48,1024]{1,0:T(8,128)(2,1)}, bf16[48,1024]{1,0:T(8,128)(2,1)S(1)}, u32[]{:S(2)}, u32[]{:S(2)}) collective-permute-start(bf16[48,1024]{1,0:T(8,128)(2,1)} %shard_map.155), channel_id=1, source_target_pairs={{0,8},{8,16},{16,24},{24,32},{32,40},{40,48},{48,56},{56,64},{64,7... | collective-permute-start | bytes 294920 | tf_op jit(solution)/shard_map/ppermute | solution.py:416
  16.0 0.6 copy-start.3
  18.9 32.0 %all-to-all-start = ((bf16[32,32,128]{2,1,0:T(8,128)(2,1)}), bf16[32,32,128]{2,1,0:T(8,128)(2,1)S(1)}, u32[]{:S(2)}, u32[]{:S(2)}) async-start(bf16[32,32,128]{2,1,0:T(8,128)(2,1)} %bitcast.14), calls=%async_computation | async-start | bytes 524288 | tf_op jit(solution)/shard_map/all_to_all | solution.py:420
  36.3 125.4 %reduce-scatter.2.cloned.1.call-start = ((), (), s32[]{:S(2)}) async-start(), calls=%async_computation.5 | async-start | bytes 2359296 | tf_op jit(solution)/shard_map/reduce_scatter | solution.py:460
  38.0 20.6 %collective-permute-start.1 = (bf16[144,512]{1,0:T(8,128)(2,1)}, bf16[144,512]{1,0:T(8,128)(2,1)S(1)}, u32[]{:S(2)}, u32[]{:S(2)}) collective-permute-start(bf16[144,512]{1,0:T(8,128)(2,1)} %get-tuple-element.38), channel_id=1, source_target_pairs={{0,128},{128,0},{1,129},{129,1},{2,130},{130,2},{3,131},{131,3},{4... | collective-permute-start | bytes 442376 | tf_op jit(solution)/shard_map/ppermute | solution.py:372
  50.9 7.7 %copy-start.2 = (bf16[32,32,128]{2,1,0:T(8,128)(2,1)}, bf16[32,32,128]{2,1,0:T(8,128)(2,1)S(1)}, u32[]{:S(2)}) copy-start(bf16[32,32,128]{2,1,0:T(8,128)(2,1)S(1)} %all-to-all-done) | copy-start | bytes 786436
  50.9 31.1 %collective-permute-start.6 = (bf16[128,1024]{1,0:T(8,128)(2,1)}, bf16[128,1024]{1,0:T(8,128)(2,1)S(1)}, u32[]{:S(2)}, u32[]{:S(2)}) collective-permute-start(bf16[128,1024]{1,0:T(8,128)(2,1)} %param.18), channel_id=1, source_target_pairs={{130,0},{128,2},{2,4},{0,6},{134,128},{132,130},{6,132},{4,134},{1... | collective-permute-start | bytes 786440 | tf_op jit(solution)/shard_map/ppermute | solution.py:430
  52.8 29.2 %collective-permute-start.5 = (bf16[128,1024]{1,0:T(8,128)(2,1)}, bf16[128,1024]{1,0:T(8,128)(2,1)S(1)}, u32[]{:S(2)}, u32[]{:S(2)}) collective-permute-start(bf16[128,1024]{1,0:T(8,128)(2,1)} %param.18), channel_id=1, source_target_pairs={{128,0},{130,2},{0,4},{2,6},{132,128},{134,130},{4,132},{6,134},{1... | collective-permute-start | bytes 786440 | tf_op jit(solution)/shard_map/ppermute | solution.py:430
  56.5 25.6 %collective-permute-start.4 = (bf16[128,1024]{1,0:T(8,128)(2,1)}, bf16[128,1024]{1,0:T(8,128)(2,1)S(1)}, u32[]{:S(2)}, u32[]{:S(2)}) collective-permute-start(bf16[128,1024]{1,0:T(8,128)(2,1)} %param.18), channel_id=1, source_target_pairs={{2,0},{0,2},{130,4},{128,6},{6,128},{4,130},{134,132},{132,134},{3... | collective-permute-start | bytes 786440 | tf_op jit(solution)/shard_map/ppermute | solution.py:430
  57.1 25.0 %collective-permute-start.3 = (bf16[128,1024]{1,0:T(8,128)(2,1)}, bf16[128,1024]{1,0:T(8,128)(2,1)S(1)}, u32[]{:S(2)}, u32[]{:S(2)}) collective-permute-start(bf16[128,1024]{1,0:T(8,128)(2,1)} %param.18), channel_id=1, source_target_pairs={{0,0},{2,2},{128,4},{130,6},{4,128},{6,130},{132,132},{134,134},{1... | collective-permute-start | bytes 786440 | tf_op jit(solution)/shard_map/ppermute | solution.py:430
  58.7 21.2 %copy-start.6 = (bf16[144,512]{1,0:T(8,128)(2,1)}, bf16[144,512]{1,0:T(8,128)(2,1)S(1)}, u32[]{:S(2)}) copy-start(bf16[144,512]{1,0:T(8,128)(2,1)S(1)} %collective-permute-done.1.other) | copy-start | bytes 442372
  82.2 11.8 %copy-start = (bf16[4,128,1024]{2,1,0:T(8,128)(2,1)}, bf16[4,128,1024]{2,1,0:T(8,128)(2,1)S(1)}, u32[]{:S(2)}) copy-start(bf16[4,128,1024]{2,1,0:T(8,128)(2,1)S(1)} %pad_maximum_fusion.cot) | copy-start | bytes 3145732
  82.2 10.1 %collective-permute-start.7 = (bf16[4,128,1024]{2,1,0:T(8,128)(2,1)S(1)}, bf16[4,128,1024]{2,1,0:T(8,128)(2,1)S(1)}, u32[]{:S(2)}, u32[]{:S(2)}) collective-permute-start(bf16[4,128,1024]{2,1,0:T(8,128)(2,1)S(1)} %pad_maximum_fusion.cot), channel_id=1, source_target_pairs={{0,1},{1,0},{2,3},{3,2},{4,5},{5,4},{6,7},{7,6},{8,9},{9,8},{10,11... | collective-permute-start | bytes 3145736 | tf_op jit(solution)/shard_map/ppermute | solution.py:372
  82.3 24.7 %collective-permute-start.2 = (bf16[2,128,512]{2,1,0:T(8,128)(2,1)}, bf16[2,128,512]{2,1,0:T(8,128)(2,1)S(1)}, u32[]{:S(2)}, u32[]{:S(2)}) collective-permute-start(bf16[2,128,512]{2,1,0:T(8,128)(2,1)} %get-tuple-element.41.product), channel_id=1, source_target_pairs={{0,128},{128,0},{1,129},{129,1},{2,130},{130,2},{3,131},{131,3},{4... | collective-permute-start | bytes 786440 | tf_op jit(solution)/shard_map/ppermute | solution.py:372
  92.4 1.7 copy-start.1
  101.3 14.0 %collective-permute-start.9 = (bf16[2,128,512]{2,1,0:T(8,128)(2,1)}, bf16[2,128,512]{2,1,0:T(8,128)(2,1)S(1)}, u32[]{:S(2)}, u32[]{:S(2)}) collective-permute-start(bf16[2,128,512]{2,1,0:T(8,128)(2,1)} %get-tuple-element.47), channel_id=1, source_target_pairs={{0,128},{128,0},{1,129},{129,1},{2,130},{130,2},{3,131},{131,3},{4... | collective-permute-start | bytes 786440 | tf_op jit(solution)/shard_map/ppermute | solution.py:372
  107.0 0.7 copy-start.11
  115.3 0.7 copy-start.10
  118.5 13.2 %all-to-all-start.2 = ((bf16[16,2,32,128]{3,2,1,0:T(8,128)(2,1)}), bf16[16,2,32,128]{3,2,1,0:T(8,128)(2,1)S(1)}, u32[]{:S(2)}, u32[]{:S(2)}) async-start(bf16[16,2,32,128]{3,2,1,0:T(8,128)(2,1)} %get-tuple-element.56), calls=%async_computation.3 | async-start | bytes 524288 | tf_op jit(solution)/shard_map/all_to_all | solution.py:376
  124.4 4.8 %collective-permute-start.10 = (f32[2,8,512]{2,1,0:T(8,128)}, f32[2,8,512]{2,1,0:T(8,128)S(1)}, u32[]{:S(2)}, u32[]{:S(2)}) collective-permute-start(f32[2,8,512]{2,1,0:T(8,128)} %get-tuple-element.53), channel_id=1, source_target_pairs={{8,0},{16,8},{24,16},{32,24},{40,32},{48,40},{56,48},{64,56},{72,6... | collective-permute-start | bytes 98312 | tf_op jit(solution)/shard_map/ppermute | solution.py:467
  129.2 0.6 copy-start.9
  131.7 0.7 copy-start.4
  132.4 23.8 %copy-start.12 = (bf16[128,512]{1,0:T(8,128)(2,1)S(1)}, bf16[128,512]{1,0:T(8,128)(2,1)}, u32[]{:S(2)}) copy-start(bf16[128,512]{1,0:T(8,128)(2,1)} %get-tuple-element.55) | copy-start | bytes 393220
  137.9 31.5 %all-to-all-start.3 = ((bf16[32,32,128]{2,1,0:T(8,128)(2,1)}), bf16[32,32,128]{2,1,0:T(8,128)(2,1)S(1)}, u32[]{:S(2)}, u32[]{:S(2)}) async-start(bf16[32,32,128]{2,1,0:T(8,128)(2,1)} %bitcast.17), calls=%async_computation.4 | async-start | bytes 524288 | tf_op jit(solution)/shard_map/all_to_all | solution.py:479
  156.2 20.2 %collective-permute-start.11 = (bf16[128,512]{1,0:T(8,128)(2,1)S(1)}, bf16[128,512]{1,0:T(8,128)(2,1)S(1)}, u32[]{:S(2)}, u32[]{:S(2)}) collective-permute-start(bf16[128,512]{1,0:T(8,128)(2,1)S(1)} %copy-done.12), channel_id=1, source_target_pairs={{0,128},{128,0},{1,129},{129,1},{2,130},{130,2},{3,131},{131,3},{4... | collective-permute-start | bytes 393224 | tf_op jit(solution)/shard_map/ppermute | solution.py:372
  161.7 24.1 %collective-permute-start.8 = (bf16[128,1024]{1,0:T(8,128)(2,1)}, bf16[128,1024]{1,0:T(8,128)(2,1)S(1)}, u32[]{:S(2)}, u32[]{:S(2)}) collective-permute-start(bf16[128,1024]{1,0:T(8,128)(2,1)} %bitcast.22), channel_id=1, source_target_pairs={{0,0},{2,2},{4,128},{6,130},{128,4},{130,6},{132,132},{134,134},{1... | collective-permute-start | bytes 786440 | tf_op jit(solution)/shard_map/ppermute | solution.py:461
  169.4 0.7 copy-start.5
  172.7 10.1 %collective-permute-start.12 = (f32[16,1024]{1,0:T(8,128)}, f32[16,1024]{1,0:T(8,128)S(1)}, u32[]{:S(2)}, u32[]{:S(2)}) collective-permute-start(f32[16,1024]{1,0:T(8,128)} %get-tuple-element.61), channel_id=1, source_target_pairs={{8,0},{16,8},{24,16},{32,24},{40,32},{48,40},{56,48},{64,56},{72,6... | collective-permute-start | bytes 196616 | tf_op jit(solution)/shard_map/ppermute | solution.py:493
  176.4 0.7 copy-start.7
  182.9 0.6 copy-start.8
Sparse Core Ops, SparseCore 0:
  10.4 83.5 all-gather.2
  114.5 37.3 reduce-scatter.1

commit v3 on v2

--- a/solution.py
+++ b/solution.py
@@ -16,7 +16,7 @@
 F32 = jnp.float32
 FAST = 128
 GROUP = 8
-VMEM = 60 * 1024 * 1024
+VMEM = 65408 * 1024
 
 
 def halves(value):
@@ -150,11 +150,24 @@
         spectrum[here, :] = spec
         both = product_of(spec, filter_spec[here, :], conjugate)
         group_inverse(both, group, first_out, twist, second_out, out)
-    if len(result.shape) == 2:
-        result[...] = out[...].astype(result.dtype)
-    else:
+    if len(result.shape) == 4:
         for n1 in range(rows):
             result[n1 % result.shape[0], n1 // result.shape[0]] = out[line(n1), :].astype(result.dtype)
+        return
+    count = FAST // channels
+    place = lax.axis_index("x")
+    column = lax.broadcasted_iota(jnp.int32, (8, FAST), 1)
+    mine = (column >= place * channels) & (column < (place + 1) * channels)
+    empty = jnp.zeros((PAD - 8, FAST), F32)
+    for n1 in range(rows):
+        result[n1, :channels] = out[line(n1), :].astype(result.dtype)
+        if n1 % count == 0:
+            ahead = out[n1 * channels : (n1 + count) * channels, :].T[:8]
+        if n1 > 0:
+            moved = pltpu.roll(ahead, (place + 4 - n1 % count) % 4 * channels, 1)
+            strip = jnp.concatenate([jnp.where(mine, moved, 0.0), empty], axis=0)
+            result[n1 - 1, channels:] = strip.astype(result.dtype)
+    result[rows - 1, channels:] = jnp.zeros((PAD, FAST), result.dtype)
 
 
 def filter_grad_kernel(first_spec, second_spec, first_out, twist, second_out, result, out):
@@ -281,7 +294,7 @@
 
 
 def mixed_grad_kernel(
-    keep, beside, own, other, short_filter, mixed, result, conv_grad, edge
+    keep, beside, own, other, short_filter, mixed, result, conv_keep, conv_give, edge
 ):
     channels = result.shape[2]
     for half, query in enumerate((own, other)):
@@ -290,39 +303,49 @@
         for s in range(result.shape[0]):
             result[s, lax.axis_index("zh") ^ half] = rows[s * channels : (s + 1) * channels]
         query_grad = out_grad * mixed[half].astype(F32)
-        conv_grad[half] = query_grad
-        edge[half] = query_grad[:8]
-
-
-def query_grad_kernel(conv_grad, after, short_filter, keep, give):
-    taps = taps_of(short_filter, 0, columns_of(0, keep.shape[1]))
-    zh, y, x = position("zh", "y", "x")
-    last = (y == 3) & (x == 3)
-    for half, result in ((0, keep), (1, give)):
-        beyond = jnp.where((zh ^ half) == 0, after[1 - half], 0.0)
-        rows = jnp.where(last, beyond, after[half])
-        result[...] = adjoint(conv_grad[half], rows, taps).astype(BF)
-
-
-def query_join_kernel(keep, beside, result):
-    width = keep.shape[1]
-    result[:, columns_of(0, width)] = keep[...]
-    result[:, columns_of(1, width)] = beside[...]
-
-
-def edge_kernel(key, value, halo, short_filter, gated_grad_rows, key_grad, value_grad, edge):
-    gated_grad = turned_back(gated_grad_rows[...])
-    key_here = gated_grad * causal(value, halo, short_filter, 2)
-    value_here = gated_grad * causal(key, halo, short_filter, 1)
-    key_grad[...] = key_here
-    value_grad[...] = value_here
-    edge[:8] = key_here[:8]
-    edge[8:] = value_here[:8]
-
-
-def last_kernel(key_conv_grad, value_conv_grad, after, short_filter, key_grad, value_grad):
-    key_grad[...] = adjoint(key_conv_grad[...], after[:8], taps_of(short_filter, 1)).astype(BF)
-    value_grad[...] = adjoint(value_conv_grad[...], after[8:], taps_of(short_filter, 2)).astype(BF)
+        if half == 0:
+            conv_keep[...] = query_grad
+        else:
+            conv_give[...] = query_grad.astype(BF)
+        edge[half] = query_grad[:PAD].astype(BF)
+
+
+def last_kernel(
+    key, value, halo, beyond, short_filter, gated_grad_rows, query_own, query_other, edge_own,
+    query_grad, key_grad, value_grad,
+):
+    tokens = query_own.shape[0]
+    for which, grad, after in (
+        (0, query_own[...], edge_own[:8, :]),
+        (1, query_other[:tokens, :], query_other[tokens : tokens + 8, :]),
+    ):
+        columns = columns_of(which, grad.shape[1])
+        taps = taps_of(short_filter, 0, columns)
+        query_grad[:, columns] = adjoint(grad.astype(F32), after.astype(F32), taps).astype(BF)
+    devices, rows, _ = gated_grad_rows.shape
+    channels = rows - PAD
+    count = FAST // channels
+    body = turned_back(
+        jnp.concatenate([gated_grad_rows[d, :channels] for d in range(devices)], axis=0)
+    )
+    strips = []
+    for first in range(0, devices, count):
+        strip = sum(gated_grad_rows[first + i, channels:].astype(F32) for i in range(count))
+        strips.append(strip[:8])
+    gated_grad = jnp.concatenate([body, jnp.concatenate(strips, axis=1)], axis=0)
+
+    def conv(signal, number, branch):
+        before = halo[branch * PAD : (branch + 1) * PAD, :].astype(F32)[PAD - 8 :]
+        after = beyond[number * PAD : (number + 1) * PAD, :].astype(F32)[:8]
+        joined = jnp.concatenate([before, signal[...].astype(F32), after], axis=0)
+        return causal_rows(joined, taps_of(short_filter, branch))
+
+    extent = key.shape[0]
+    for result, grad, branch in (
+        (key_grad, gated_grad * conv(value, 1, 2), 1),
+        (value_grad, gated_grad * conv(key, 0, 1), 2),
+    ):
+        result[...] = adjoint(grad[:extent], grad[extent:], taps_of(short_filter, branch)).astype(BF)
 
 
 def backward_kernel(cot, beside, weight, keep, give, both, total):
@@ -414,6 +437,7 @@
         grid=(1,), specs={i: last_rows for i in range(3)},
     )
     halo = lax.ppermute(halo, SEQ, [(i, i + 1) for i in range(seq_count - 1)])
+    back = [(i + 1, i) for i in range(seq_count - 1)]
     filter_spec = call(filter_kernel, spec_type, [held], long_filter, first_in, twist, second_in)
     halo = once(halo, filter_spec)
     gated_rows = call(gated_kernel, rows_type, [], key, value, halo, short_filter)
@@ -424,6 +448,8 @@
         query_split_kernel, (query_type, query_type), [], query, halo
     )
     query_other = swap(query_other, "zh")
+
+    beyond = lax.ppermute(jnp.concatenate([key[:PAD], value[:PAD]], axis=0), SEQ, back)
 
     cot_there = once(cotangent, gated_rows)
     blocks = [
@@ -437,7 +463,7 @@
     mixed_rows = exchange(mixed_rows)
     product, mixed = call(
         product_kernel, (halves_bf, halves_bf), [],
-        query_own, query_other, short_filter, mixed_rows,
+        query_own, query_other, short_filter, once(mixed_rows, beyond),
     )
     product_beside = swap(product, "zh")
     got = jnp.stack(once(tuple(blocks), product))
@@ -458,41 +484,35 @@
         out_specs=pl.BlockSpec((2, 1, tokens, width), lambda row: (0, row, 0, 0)),
     )
     summed = lax.psum_scatter(partial.reshape(8, tokens, width), CHAN, scatter_dimension=0)
+
+    mixed_grad_rows, query_conv_own, query_conv_other, query_edge = call(
+        mixed_grad_kernel, (split_type, shape_of((tokens, half), F32), shape_of((tokens, half), BF), shape_of((2, PAD, half), BF)), [],
+        grads, once(grads_beside, partial), query_own, query_other, short_filter, mixed, flops=1 << 33,
+    )
+    query_edge = lax.ppermute(query_edge, ("y", "x"), [((i + 1) % 16, i) for i in range(16)])
+    zh, y, x = position("zh", "y", "x")
+    last = (y == 3) & (x == 3)
+    zero = jnp.zeros_like(query_edge[0])
+    edge_own = jnp.where(last, jnp.where(zh == 0, query_edge[1], zero), query_edge[0])
+    edge_other = jnp.where(last, jnp.where(zh == 0, zero, query_edge[0]), query_edge[1])
+    query_conv_other = swap(jnp.concatenate([query_conv_other, edge_other], axis=0), "zh")
+    mixed_grad_rows = exchange(mixed_grad_rows)
+    gated_grad_rows, mixed_spec = call(
+        functools.partial(convolve_kernel, True), (shape_of((seq_count, channels + PAD, FAST), BF), spec_type), [held, held],
+        mixed_grad_rows, filter_spec, first_in, first_out, twist, second_in, second_out,
+        flops=1 << 35,
+    )
+    gated_grad_rows = lax.all_to_all(
+        once(gated_grad_rows, query_conv_other), SEQ, split_axis=0, concat_axis=0, tiled=True
+    )
     block_output = lax.ppermute(summed, ("zh", "zl"), links(0, 0, True))
-
-    mixed_grad_rows, query_conv_grad, query_edge = call(
-        mixed_grad_kernel, (split_type, halves_f32, shape_of((2, 8, half), F32)), [],
-        grads, once(grads_beside, partial), query_own, query_other, short_filter, mixed, flops=1 << 33,
-    )
-    query_after = lax.ppermute(query_edge, ("y", "x"), [((i + 1) % 16, i) for i in range(16)])
-    mixed_grad_rows = exchange(mixed_grad_rows)
-    half_type = shape_of((tokens, half), BF)
-    query_grad, query_grad_other = call(
-        query_grad_kernel, (half_type, half_type), [],
-        query_conv_grad, query_after, short_filter,
-    )
-    gated_grad_rows, mixed_spec = call(
-        functools.partial(convolve_kernel, True), (rows_type, spec_type), [held, held],
-        once(mixed_grad_rows, query_grad_other), filter_spec, first_in, first_out, twist, second_in, second_out,
-        flops=1 << 35,
-    )
-    gated_grad_rows = lax.all_to_all(gated_grad_rows, SEQ, split_axis=0, concat_axis=0, tiled=True)
+    query_grad, key_grad, value_grad = call(
+        last_kernel, (tokens_bf, tokens_bf, tokens_bf), [], key, value, halo, beyond, short_filter,
+        gated_grad_rows, query_conv_own, query_conv_other, edge_own,
+    )
     filter_grad = call(
         filter_grad_kernel, shape_of((channels, length), F32), [held],
-        mixed_spec, gated_spec, first_out, twist, second_out,
-    )
-    back = [(i + 1, i) for i in range(seq_count - 1)]
-    query_grad_other = swap(query_grad_other, "zh")
-    query_grad = call(
-        query_join_kernel, tokens_bf, [], query_grad, query_grad_other
-    )
-    key_conv_grad, value_conv_grad, edge = call(
-        edge_kernel, (tokens_f32, tokens_f32, shape_of((16, width), F32)), [],
-        key, value, halo, short_filter, gated_grad_rows, flops=1 << 33,
-    )
-    after = lax.ppermute(edge, SEQ, back)
-    key_grad, value_grad = call(
-        last_kernel, (tokens_bf, tokens_bf), [], key_conv_grad, value_conv_grad, once(after, filter_grad), short_filter
+        once(mixed_spec, key_grad), gated_spec, first_out, twist, second_out,
     )
     return (block_output, query_grad, key_grad, value_grad, filter_grad)
 

time: 197 us -> 194 us (0.985); the launches traced: 193 us -> 193 us
  blocking collectives: 15.7 us -> 0 us
  waiting for transfers between devices: 21.6 us -> 36.8 us
  Pallas kernels: 50.7 us -> 45.6 us
  starting transfers between devices: 85 us -> 88.6 us
  other arithmetic: 0.13 us -> 3.52 us
    all_to_all x1 -> x0, blocking collectives: 15.7 us -> none  [exchange(): lax.all_to_all(value, ('y', 'x'), split_axis=0, concat_axis=0, tiled=True)]
    ppermute x5, waiting for transfers between devices: 0.96 us -> 11.4 us  [swap(): return lax.ppermute(value, axis, [(0, 1), (1, 0)])]
    all_to_all x1 -> x2, starting transfers between devices: 5.9 us -> 15.4 us  [exchange(): lax.all_to_all(value, ('y', 'x'), split_axis=0, concat_axis=0, tiled=True)]
    all_to_all x1, starting transfers between devices: 18.3 us -> 11.8 us  [shards(): lax.all_to_all(once(gated_grad_rows, query_conv_other), SEQ, split_axis=0...]
    ppermute x1, waiting for transfers between devices: 0.01 us -> 5.5 us  [shards(): lax.ppermute(jnp.concatenate([key[:PAD], value[:PAD]], axis=0), SEQ, back)]
    ppermute x5, starting transfers between devices: 26.7 us -> 21.3 us  [swap(): return lax.ppermute(value, axis, [(0, 1), (1, 0)])]
    pallas_call x15 -> x12, Pallas kernels: 50.7 us -> 45.6 us  [call(): pl.pallas_call(kernel, out_shape=out_shape, grid=grid, in_specs=[specs.ge...]
    ppermute x1, waiting for transfers between devices: 4.43 us -> 0.01 us  [shards(): lax.ppermute(query_edge, ('y', 'x'), [((i + 1) % 16, i) for i in range(16)])]
  transfers between devices with their start and end apart: 18 -> 19, of which waited for: 6 -> 9; matrix products, arithmetic and copies ran while one was open for 0% -> 3% of each run, Pallas kernels for 26% -> 24%
where the time goes in v3:
time: 194 us; the launch traced here: 193 us
  starting transfers between devices  88.6 us (46%)
  Pallas kernels  45.6 us (24%)
  waiting for transfers between devices  36.8 us (19%)
  between operations  14.1 us (7%)
  local copies, waits for them, and re-layouts  4.22 us (2%)
  other arithmetic  3.52 us (2%)
    pallas_call x12, Pallas kernels, call(): pl.pallas_call(kernel, out_shape=out_shape, grid=grid, in_specs=[specs.ge...  45.6 us
    ppermute x5, starting transfers between devices, swap(): return lax.ppermute(value, axis, [(0, 1), (1, 0)])  21.3 us
    all_to_all x1, starting transfers between devices, shards(): lax.all_to_all(gated_rows, SEQ, split_axis=0, concat_axis=0, tiled=True)  17.4 us
    all_to_all x2, starting transfers between devices, exchange(): lax.all_to_all(value, ('y', 'x'), split_axis=0, concat_axis=0, tiled=True)  15.4 us
    all_to_all x1, starting transfers between devices, shards(): lax.all_to_all(once(gated_grad_rows, query_conv_other), SEQ, split_axis=0...  11.8 us
    ppermute x5, waiting for transfers between devices, swap(): return lax.ppermute(value, axis, [(0, 1), (1, 0)])  11.4 us
    ppermute x4, starting transfers between devices, shards(): lax.ppermute(cot_there, ('zh', 'zl'), links(k1, k2, False))  11.4 us
    all_to_all x1, waiting for transfers between devices, shards(): lax.all_to_all(once(gated_grad_rows, query_conv_other), SEQ, split_axis=0...  9.16 us
  transfers between devices with their start and end apart: 19, of which 9 were waited for; matrix products, arithmetic and copies ran while one was open for 3% of the time, Pallas kernels for 24%

profile of v3, /device:TPU:2, one launch (start us, length us, event | category | flops | bytes accessed | tf_op | source)
XLA Modules:
  0.0 192.9 jit_solution(7419417383793823596)
XLA Ops:
  7.2 0.0 all-gather.3.cloned.1.call-start
  7.2 0.7 all-gather.3.cloned.1.call-update
  7.9 1.4 shard_map.155
  9.3 3.4 %collective-permute-start = (bf16[48,1024]{1,0:T(8,128)(2,1)}, bf16[48,1024]{1,0:T(8,128)(2,1)}, u32[]{:S(2)}, u32[]{:S(2)}) collective-permute-start(bf16[48,1024]{1,0:T(8,128)(2,1)} %shard_map.155), channel_id=1, source_target_pairs={{0,8},{8,16},{16,24},{24,32},{32,40},{40,48},{48,56},{56,64},{64,7... | collective-permute-start | bytes 294920 | tf_op jit(solution)/shard_map/ppermute | solution.py:439
  12.7 3.1 %shard_map.156.filter_spec = f32[1024,256]{1,0:T(8,128)} custom-call(f32[32,4096]{1,0:T(8,128)} %signal.1, bf16[64,96]{1,0:T(8,128)(2,1)} %constant.31.clone.first_in, f32[2,32,128]{2,1,0:T(8,128)} %constant.33.clone.twist, bf16[2,256,256]{2,1,0:T(8,128)(2,1)} %constant.34.clone.second_in), custom_call_target="tpu_custom_call" | custom-call | flops 1024 | bytes 1024 | tf_op jit(solution)/shard_map/pallas_call | solution.py:192
  15.8 0.3 collective-permute-done.halo
  16.2 2.3 %shard_map.158 = bf16[1024,128]{1,0:T(8,128)(2,1)} custom-call(bf16[128,1024]{1,0:T(8,128)(2,1)} %key.5, bf16[128,1024]{1,0:T(8,128)(2,1)} %value.5, bf16[48,1024]{1,0:T(8,128)(2,1)} %collective-permute-done.halo, f32[3,3,1024]{2,1,0:T(4,128)} %short_filter.7), custom_call_target="tpu_custom_call" | custom-call | flops 1024 | bytes 1024 | tf_op jit(solution)/shard_map/pallas_call | solution.py:192
  18.4 17.4 %all-to-all-start = ((bf16[32,32,128]{2,1,0:T(8,128)(2,1)}), bf16[32,32,128]{2,1,0:T(8,128)(2,1)}, u32[]{:S(2)}, u32[]{:S(2)}) async-start(bf16[32,32,128]{2,1,0:T(8,128)(2,1)} %bitcast.24), calls=%async_computation | async-start | bytes 524288 | tf_op jit(solution)/shard_map/all_to_all | solution.py:444
  35.8 1.7 shard_map.157
  37.5 5.4 %collective-permute-start.1 = (bf16[144,512]{1,0:T(8,128)(2,1)}, bf16[144,512]{1,0:T(8,128)(2,1)}, u32[]{:S(2)}, u32[]{:S(2)}) collective-permute-start(bf16[144,512]{1,0:T(8,128)(2,1)} %get-tuple-element.36), channel_id=1, source_target_pairs={{0,128},{128,0},{1,129},{129,1},{2,130},{130,2},{3,131},{131,3},{4... | collective-permute-start | bytes 442376 | tf_op jit(solution)/shard_map/ppermute | solution.py:395
  42.9 7.6 %all-to-all-done = bf16[32,32,128]{2,1,0:T(8,128)(2,1)} async-done(((bf16[32,32,128]{2,1,0:T(8,128)(2,1)}), bf16[32,32,128]{2,1,0:T(8,128)(2,1)}, u32[]{:S(2)}, u32[]{:S(2)}) %all-to-all-start) | async-done | bytes 262176 | tf_op jit(solution)/shard_map/all_to_all | solution.py:444
  50.5 3.6 %collective-permute-start.4 = (bf16[128,1024]{1,0:T(8,128)(2,1)}, bf16[128,1024]{1,0:T(8,128)(2,1)}, u32[]{:S(2)}, u32[]{:S(2)}) collective-permute-start(bf16[128,1024]{1,0:T(8,128)(2,1)} %param.18), channel_id=1, source_target_pairs={{0,0},{2,2},{128,4},{130,6},{4,128},{6,130},{132,132},{134,134},{1... | collective-permute-start | bytes 786440 | tf_op jit(solution)/shard_map/ppermute | solution.py:456
  54.1 4.9 %collective-permute-start.5 = (bf16[128,1024]{1,0:T(8,128)(2,1)}, bf16[128,1024]{1,0:T(8,128)(2,1)}, u32[]{:S(2)}, u32[]{:S(2)}) collective-permute-start(bf16[128,1024]{1,0:T(8,128)(2,1)} %param.18), channel_id=1, source_target_pairs={{2,0},{0,2},{130,4},{128,6},{6,128},{4,130},{134,132},{132,134},{3... | collective-permute-start | bytes 786440 | tf_op jit(solution)/shard_map/ppermute | solution.py:456
  59.0 2.9 %collective-permute-start.7 = (bf16[128,1024]{1,0:T(8,128)(2,1)}, bf16[128,1024]{1,0:T(8,128)(2,1)}, u32[]{:S(2)}, u32[]{:S(2)}) collective-permute-start(bf16[128,1024]{1,0:T(8,128)(2,1)} %param.18), channel_id=1, source_target_pairs={{130,0},{128,2},{2,4},{0,6},{134,128},{132,130},{6,132},{4,134},{1... | collective-permute-start | bytes 786440 | tf_op jit(solution)/shard_map/ppermute | solution.py:456
  61.9 5.4 %shard_map.159 = (bf16[16,2,32,128]{3,2,1,0:T(8,128)(2,1)}, f32[1024,256]{1,0:T(8,128)}) custom-call(bf16[1024,128]{1,0:T(8,128)(2,1)} %bitcast.1.signal, f32[1024,256]{1,0:T(8,128)} %shard_map.156.filter_spec, bf16[64,96]{1,0:T(8,128)(2,1)} %constant.31.clone.first_in, bf16[32,192]{1,0:T(8,128)(2,1)} %constant.32.clone.first_out, ...), custom_call_target="tpu_custom_call" | custom-call | flops 1024 | bytes 1024 | tf_op jit(solution)/shard_map/pallas_call | solution.py:192
  67.4 5.5 %all-to-all-start.1 = ((bf16[16,2,32,128]{3,2,1,0:T(8,128)(2,1)}), bf16[16,2,32,128]{3,2,1,0:T(8,128)(2,1)}, u32[]{:S(2)}, u32[]{:S(2)}) async-start(bf16[16,2,32,128]{3,2,1,0:T(8,128)(2,1)} %get-tuple-element.38), calls=%async_computation.1 | async-start | bytes 524288 | tf_op jit(solution)/shard_map/all_to_all | solution.py:399
  72.9 0.0 reduce-scatter.2.cloned.1.call-start
  72.9 0.8 slice.14
  73.7 0.8 slice.15
  74.5 2.2 %collective-permute-start.2 = (bf16[32,1024]{1,0:T(8,128)(2,1)S(1)}, bf16[32,1024]{1,0:T(8,128)(2,1)S(1)}, u32[]{:S(2)}, u32[]{:S(2)}) collective-permute-start(bf16[32,1024]{1,0:T(8,128)(2,1)S(1)} %pad_maximum_fusion.2), channel_id=1, source_target_pairs={{8,0},{16,8},{24,16},{32,24},{40,32},{48,40},{56,48},{64,56},{72,6... | collective-permute-start | bytes 196616 | tf_op jit(solution)/shard_map/ppermute | solution.py:452
  76.7 5.5 %collective-permute-done.2.beyond = bf16[32,1024]{1,0:T(8,128)(2,1)S(1)} collective-permute-done((bf16[32,1024]{1,0:T(8,128)(2,1)S(1)}, bf16[32,1024]{1,0:T(8,128)(2,1)S(1)}, u32[]{:S(2)}, u32[]{:S(2)}) %collective-permute-start.2) | collective-permute-done | bytes 65568 | tf_op jit(solution)/shard_map/ppermute | solution.py:452
  82.2 1.0 all-to-all-done.1.mixed_rows
  83.2 2.2 %shard_map.160 = (bf16[2,128,512]{2,1,0:T(8,128)(2,1)}, bf16[2,128,512]{2,1,0:T(8,128)(2,1)}) custom-call(bf16[144,512]{1,0:T(8,128)(2,1)} %get-tuple-element.35.own, bf16[144,512]{1,0:T(8,128)(2,1)} %collective-permute-done.1.other, f32[3,3,1024]{2,1,0:T(4,128)} %short_filter.7, bf16[16,2,32,128]{3,2,1,0:T(8,128)(2,1)} %all-to-all-done.1.mixed_rows), custom_call_target="tpu_custom_call" | custom-call | flops 1024 | bytes 1024 | tf_op jit(solution)/shard_map/pallas_call | solution.py:192
  85.4 1.3 pad_maximum_fusion.cot
  86.8 1.0 copy-done
  87.8 4.9 %collective-permute-start.3 = (bf16[2,128,512]{2,1,0:T(8,128)(2,1)}, bf16[2,128,512]{2,1,0:T(8,128)(2,1)}, u32[]{:S(2)}, u32[]{:S(2)}) collective-permute-start(bf16[2,128,512]{2,1,0:T(8,128)(2,1)} %get-tuple-element.40.product), channel_id=1, source_target_pairs={{0,128},{128,0},{1,129},{129,1},{2,130},{130,2},{3,131},{131,3},{4... | collective-permute-start | bytes 786440 | tf_op jit(solution)/shard_map/ppermute | solution.py:395
  92.7 1.0 all-gather.3.cloned.1.call-done
  93.7 7.3 %shard_map.161 = (f32[2,128,512]{2,1,0:T(8,128)}, bf16[2,128,512]{2,1,0:T(8,128)(2,1)}) custom-call(bf16[4,128,1024]{2,1,0:T(8,128)(2,1)} %copy-done, bf16[4,128,1024]{2,1,0:T(8,128)(2,1)} %collective-permute-done.8.beside, bf16[16,1024,256]{2,1,0:T(8,128)(2,1)} %bitcast.21), custom_call_target="tpu_custom_call" | custom-call | flops 1024 | bytes 1024 | tf_op jit(solution)/shard_map/pallas_call | solution.py:192
  101.0 5.7 %collective-permute-start.10 = (bf16[2,128,512]{2,1,0:T(8,128)(2,1)}, bf16[2,128,512]{2,1,0:T(8,128)(2,1)}, u32[]{:S(2)}, u32[]{:S(2)}) collective-permute-start(bf16[2,128,512]{2,1,0:T(8,128)(2,1)} %get-tuple-element.46), channel_id=1, source_target_pairs={{0,128},{128,0},{1,129},{129,1},{2,130},{130,2},{3,131},{131,3},{4... | collective-permute-start | bytes 786440 | tf_op jit(solution)/shard_map/ppermute | solution.py:395
  106.8 6.6 %shard_map.162 = bf16[2,4,128,1024]{3,2,1,0:T(8,128)(2,1)} custom-call(bf16[2,128,512]{2,1,0:T(8,128)(2,1)} %get-tuple-element.40.product, bf16[2,128,512]{2,1,0:T(8,128)(2,1)} %collective-permute-done.3.beside, bf16[16,1024,256]{2,1,0:T(8,128)(2,1)} %bitcast.22), custom_call_target="tpu_custom_call" | custom-call | flops 17179869184 | bytes 1024 | tf_op jit(solution)/shard_map/pallas_call | solution.py:192
  113.4 0.0 reduce-scatter.2.cloned.1.call-update
  113.4 7.4 %collective-permute-done.10.beside = bf16[2,128,512]{2,1,0:T(8,128)(2,1)} collective-permute-done((bf16[2,128,512]{2,1,0:T(8,128)(2,1)}, bf16[2,128,512]{2,1,0:T(8,128)(2,1)}, u32[]{:S(2)}, u32[]{:S(2)}) %collective-permute-start.10) | collective-permute-done | bytes 262176 | tf_op jit(solution)/shard_map/ppermute | solution.py:395
  120.8 2.4 %shard_map.163 = (bf16[16,2,32,128]{3,2,1,0:T(8,128)(2,1)}, f32[128,512]{1,0:T(8,128)}, bf16[128,512]{1,0:T(8,128)(2,1)}, bf16[2,16,512]{2,1,0:T(8,128)(2,1)}) custom-call(f32[2,128,512]{2,1,0:T(8,128)} %get-tuple-element.48.keep, bf16[2,128,512]{2,1,0:T(8,128)(2,1)} %collective-permute-done.10.beside, bf16[144,512]{1,0:T(8,128)(2,1)} %get-tuple-element.35.own, ...), custom_call_target="tpu_custom_call" | custom-call | flops 8589934592 | bytes 1024 | tf_op jit(solution)/shard_map/pallas_call | solution.py:192
  123.2 2.0 %collective-permute-start.11 = (bf16[2,16,512]{2,1,0:T(8,128)(2,1)}, bf16[2,16,512]{2,1,0:T(8,128)(2,1)S(1)}, u32[]{:S(2)}, u32[]{:S(2)}) collective-permute-start(bf16[2,16,512]{2,1,0:T(8,128)(2,1)} %get-tuple-element.54), channel_id=1, source_target_pairs={{8,0},{16,8},{24,16},{32,24},{40,32},{48,40},{56,48},{64,56},{72,6... | collective-permute-start | bytes 98312 | tf_op jit(solution)/shard_map/ppermute | solution.py:492
  125.2 9.9 %all-to-all-start.2 = ((bf16[16,2,32,128]{3,2,1,0:T(8,128)(2,1)}), bf16[16,2,32,128]{3,2,1,0:T(8,128)(2,1)}, u32[]{:S(2)}, u32[]{:S(2)}) async-start(bf16[16,2,32,128]{3,2,1,0:T(8,128)(2,1)} %get-tuple-element.51), calls=%async_computation.3 | async-start | bytes 524288 | tf_op jit(solution)/shard_map/all_to_all | solution.py:399
  135.1 0.6 select_select_fusion
  135.7 1.6 pad_maximum_fusion.1
  137.3 5.3 %collective-permute-start.12 = (bf16[144,512]{1,0:T(8,128)(2,1)}, bf16[144,512]{1,0:T(8,128)(2,1)}, u32[]{:S(2)}, u32[]{:S(2)}) collective-permute-start(bf16[144,512]{1,0:T(8,128)(2,1)} %pad_maximum_fusion.1), channel_id=1, source_target_pairs={{0,128},{128,0},{1,129},{129,1},{2,130},{130,2},{3,131},{131,3},{4... | collective-permute-start | bytes 442376 | tf_op jit(solution)/shard_map/ppermute | solution.py:395
  142.6 0.1 all-to-all-done.2.signal
  142.6 5.7 %shard_map.164 = (bf16[32,48,128]{2,1,0:T(8,128)(2,1)}, f32[1024,256]{1,0:T(8,128)}) custom-call(bf16[16,2,32,128]{3,2,1,0:T(8,128)(2,1)} %all-to-all-done.2.signal, f32[1024,256]{1,0:T(8,128)} %shard_map.156.filter_spec, bf16[64,96]{1,0:T(8,128)(2,1)} %constant.31.clone.first_in, bf16[32,192]{1,0:T(8,128)(2,1)} %constant.32.clone.first_out, ...), custom_call_target="tpu_custom_call" | custom-call | flops 34359738368 | bytes 1024 | tf_op jit(solution)/shard_map/pallas_call | solution.py:192
  148.4 4.0 %collective-permute-done.12.query_other = bf16[144,512]{1,0:T(8,128)(2,1)} collective-permute-done((bf16[144,512]{1,0:T(8,128)(2,1)}, bf16[144,512]{1,0:T(8,128)(2,1)}, u32[]{:S(2)}, u32[]{:S(2)}) %collective-permute-start.12) | collective-permute-done | bytes 147488 | tf_op jit(solution)/shard_map/ppermute | solution.py:395
  152.4 11.8 %all-to-all-start.3 = ((bf16[32,48,128]{2,1,0:T(8,128)(2,1)}), bf16[32,48,128]{2,1,0:T(8,128)(2,1)}, u32[]{:S(2)}, u32[]{:S(2)}) async-start(bf16[32,48,128]{2,1,0:T(8,128)(2,1)} %get-tuple-element.55), calls=%async_computation.4 | async-start | bytes 786432 | tf_op jit(solution)/shard_map/all_to_all | solution.py:505
  164.2 0.0 reduce-scatter.2.cloned.1.call-done
  164.2 3.6 %collective-permute-start.9 = (bf16[128,1024]{1,0:T(8,128)(2,1)}, bf16[128,1024]{1,0:T(8,128)(2,1)}, u32[]{:S(2)}, u32[]{:S(2)}) collective-permute-start(bf16[128,1024]{1,0:T(8,128)(2,1)} %bitcast.25), channel_id=1, source_target_pairs={{0,0},{2,2},{4,128},{6,130},{128,4},{130,6},{132,132},{134,134},{1... | collective-permute-start | bytes 786440 | tf_op jit(solution)/shard_map/ppermute | solution.py:508
  167.8 9.2 %all-to-all-done.3.gated_grad_rows = bf16[32,48,128]{2,1,0:T(8,128)(2,1)} async-done(((bf16[32,48,128]{2,1,0:T(8,128)(2,1)}), bf16[32,48,128]{2,1,0:T(8,128)(2,1)}, u32[]{:S(2)}, u32[]{:S(2)}) %all-to-all-start.3) | async-done | bytes 393248 | tf_op jit(solution)/shard_map/all_to_all | solution.py:505
  177.0 3.3 %shard_map.165 = (bf16[128,1024]{1,0:T(8,128)(2,1)}, bf16[128,1024]{1,0:T(8,128)(2,1)}, bf16[128,1024]{1,0:T(8,128)(2,1)}) custom-call(bf16[128,1024]{1,0:T(8,128)(2,1)} %key.5, bf16[128,1024]{1,0:T(8,128)(2,1)} %value.5, bf16[48,1024]{1,0:T(8,128)(2,1)} %collective-permute-done.halo, bf16[32,1024]{1,0:T(8,128)(2,1)} %copy-done.1, ...), custom_call_target="tpu_custom_call" | custom-call | flops 1024 | bytes 1024 | tf_op jit(solution)/shard_map/pallas_call | solution.py:192
  180.3 4.1 %shard_map.166 = f32[32,4096]{1,0:T(8,128)} custom-call(f32[1024,256]{1,0:T(8,128)} %get-tuple-element.61.first_spec, f32[1024,256]{1,0:T(8,128)} %get-tuple-element.62.second_spec, bf16[32,192]{1,0:T(8,128)(2,1)} %constant.32.clone.first_out, f32[2,32,128]{2,1,0:T(8,128)} %constant.33.clone.twist, bf16[2,256,256]{2,1,0:T(8,128)(2,1)} %constant.35.clone.second_out), custom_call_target="tpu_custom_call" | custom-call | flops 1024 | bytes 1024 | tf_op jit(solution)/shard_map/pallas_call | solution.py:192
  184.4 1.7 copy.18
  (15 shorter events, 0.0 us)
Async XLA Ops:
  7.2 86.5 %all-gather.3.cloned.1.call-start = ((), (), s32[]{:S(2)}) async-start(), calls=%async_computation.6 | async-start | bytes 8912896 | tf_op jit(solution)/shard_map/all_gather | solution.py:422
  9.3 6.8 %collective-permute-start = (bf16[48,1024]{1,0:T(8,128)(2,1)}, bf16[48,1024]{1,0:T(8,128)(2,1)}, u32[]{:S(2)}, u32[]{:S(2)}) collective-permute-start(bf16[48,1024]{1,0:T(8,128)(2,1)} %shard_map.155), channel_id=1, source_target_pairs={{0,8},{8,16},{16,24},{24,32},{32,40},{40,48},{48,56},{56,64},{64,7... | collective-permute-start | bytes 294920 | tf_op jit(solution)/shard_map/ppermute | solution.py:439
  18.4 32.1 %all-to-all-start = ((bf16[32,32,128]{2,1,0:T(8,128)(2,1)}), bf16[32,32,128]{2,1,0:T(8,128)(2,1)}, u32[]{:S(2)}, u32[]{:S(2)}) async-start(bf16[32,32,128]{2,1,0:T(8,128)(2,1)} %bitcast.24), calls=%async_computation | async-start | bytes 524288 | tf_op jit(solution)/shard_map/all_to_all | solution.py:444
  37.5 24.4 %collective-permute-start.1 = (bf16[144,512]{1,0:T(8,128)(2,1)}, bf16[144,512]{1,0:T(8,128)(2,1)}, u32[]{:S(2)}, u32[]{:S(2)}) collective-permute-start(bf16[144,512]{1,0:T(8,128)(2,1)} %get-tuple-element.36), channel_id=1, source_target_pairs={{0,128},{128,0},{1,129},{129,1},{2,130},{130,2},{3,131},{131,3},{4... | collective-permute-start | bytes 442376 | tf_op jit(solution)/shard_map/ppermute | solution.py:395
  50.5 34.9 %collective-permute-start.4 = (bf16[128,1024]{1,0:T(8,128)(2,1)}, bf16[128,1024]{1,0:T(8,128)(2,1)}, u32[]{:S(2)}, u32[]{:S(2)}) collective-permute-start(bf16[128,1024]{1,0:T(8,128)(2,1)} %param.18), channel_id=1, source_target_pairs={{0,0},{2,2},{128,4},{130,6},{4,128},{6,130},{132,132},{134,134},{1... | collective-permute-start | bytes 786440 | tf_op jit(solution)/shard_map/ppermute | solution.py:456
  54.1 31.3 %collective-permute-start.5 = (bf16[128,1024]{1,0:T(8,128)(2,1)}, bf16[128,1024]{1,0:T(8,128)(2,1)}, u32[]{:S(2)}, u32[]{:S(2)}) collective-permute-start(bf16[128,1024]{1,0:T(8,128)(2,1)} %param.18), channel_id=1, source_target_pairs={{2,0},{0,2},{130,4},{128,6},{6,128},{4,130},{134,132},{132,134},{3... | collective-permute-start | bytes 786440 | tf_op jit(solution)/shard_map/ppermute | solution.py:456
  59.0 26.4 %collective-permute-start.6 = (bf16[128,1024]{1,0:T(8,128)(2,1)}, bf16[128,1024]{1,0:T(8,128)(2,1)}, u32[]{:S(2)}, u32[]{:S(2)}) collective-permute-start(bf16[128,1024]{1,0:T(8,128)(2,1)} %param.18), channel_id=1, source_target_pairs={{128,0},{130,2},{0,4},{2,6},{132,128},{134,130},{4,132},{6,134},{1... | collective-permute-start | bytes 786440 | tf_op jit(solution)/shard_map/ppermute | solution.py:456
  59.0 26.4 %collective-permute-start.7 = (bf16[128,1024]{1,0:T(8,128)(2,1)}, bf16[128,1024]{1,0:T(8,128)(2,1)}, u32[]{:S(2)}, u32[]{:S(2)}) collective-permute-start(bf16[128,1024]{1,0:T(8,128)(2,1)} %param.18), channel_id=1, source_target_pairs={{130,0},{128,2},{2,4},{0,6},{134,128},{132,130},{6,132},{4,134},{1... | collective-permute-start | bytes 786440 | tf_op jit(solution)/shard_map/ppermute | solution.py:456
  67.4 15.8 %all-to-all-start.1 = ((bf16[16,2,32,128]{3,2,1,0:T(8,128)(2,1)}), bf16[16,2,32,128]{3,2,1,0:T(8,128)(2,1)}, u32[]{:S(2)}, u32[]{:S(2)}) async-start(bf16[16,2,32,128]{3,2,1,0:T(8,128)(2,1)} %get-tuple-element.38), calls=%async_computation.1 | async-start | bytes 524288 | tf_op jit(solution)/shard_map/all_to_all | solution.py:399
  72.9 91.3 %reduce-scatter.2.cloned.1.call-start = ((), (), s32[]{:S(2)}) async-start(), calls=%async_computation.5 | async-start | bytes 2359296 | tf_op jit(solution)/shard_map/reduce_scatter | solution.py:486
  74.5 7.7 %collective-permute-start.2 = (bf16[32,1024]{1,0:T(8,128)(2,1)S(1)}, bf16[32,1024]{1,0:T(8,128)(2,1)S(1)}, u32[]{:S(2)}, u32[]{:S(2)}) collective-permute-start(bf16[32,1024]{1,0:T(8,128)(2,1)S(1)} %pad_maximum_fusion.2), channel_id=1, source_target_pairs={{8,0},{16,8},{24,16},{32,24},{40,32},{48,40},{56,48},{64,56},{72,6... | collective-permute-start | bytes 196616 | tf_op jit(solution)/shard_map/ppermute | solution.py:452
  82.2 31.2 %copy-start.1 = (bf16[32,1024]{1,0:T(8,128)(2,1)}, bf16[32,1024]{1,0:T(8,128)(2,1)S(1)}, u32[]{:S(2)}) copy-start(bf16[32,1024]{1,0:T(8,128)(2,1)S(1)} %collective-permute-done.2.beyond) | copy-start | bytes 196612
  86.8 1.0 copy-start
  87.8 4.9 %collective-permute-start.8 = (bf16[4,128,1024]{2,1,0:T(8,128)(2,1)S(1)}, bf16[4,128,1024]{2,1,0:T(8,128)(2,1)}, u32[]{:S(2)}, u32[]{:S(2)}) collective-permute-start(bf16[4,128,1024]{2,1,0:T(8,128)(2,1)S(1)} %pad_maximum_fusion.cot), channel_id=1, source_target_pairs={{0,1},{1,0},{2,3},{3,2},{4,5},{5,4},{6,7},{7,6},{8,9},{9,8},{10,11... | collective-permute-start | bytes 3145736 | tf_op jit(solution)/shard_map/ppermute | solution.py:395
  87.8 19.0 %collective-permute-start.3 = (bf16[2,128,512]{2,1,0:T(8,128)(2,1)}, bf16[2,128,512]{2,1,0:T(8,128)(2,1)}, u32[]{:S(2)}, u32[]{:S(2)}) collective-permute-start(bf16[2,128,512]{2,1,0:T(8,128)(2,1)} %get-tuple-element.40.product), channel_id=1, source_target_pairs={{0,128},{128,0},{1,129},{129,1},{2,130},{130,2},{3,131},{131,3},{4... | collective-permute-start | bytes 786440 | tf_op jit(solution)/shard_map/ppermute | solution.py:395
  101.0 19.8 %collective-permute-start.10 = (bf16[2,128,512]{2,1,0:T(8,128)(2,1)}, bf16[2,128,512]{2,1,0:T(8,128)(2,1)}, u32[]{:S(2)}, u32[]{:S(2)}) collective-permute-start(bf16[2,128,512]{2,1,0:T(8,128)(2,1)} %get-tuple-element.46), channel_id=1, source_target_pairs={{0,128},{128,0},{1,129},{129,1},{2,130},{130,2},{3,131},{131,3},{4... | collective-permute-start | bytes 786440 | tf_op jit(solution)/shard_map/ppermute | solution.py:395
  123.2 11.9 %collective-permute-start.11 = (bf16[2,16,512]{2,1,0:T(8,128)(2,1)}, bf16[2,16,512]{2,1,0:T(8,128)(2,1)S(1)}, u32[]{:S(2)}, u32[]{:S(2)}) collective-permute-start(bf16[2,16,512]{2,1,0:T(8,128)(2,1)} %get-tuple-element.54), channel_id=1, source_target_pairs={{8,0},{16,8},{24,16},{32,24},{40,32},{48,40},{56,48},{64,56},{72,6... | collective-permute-start | bytes 98312 | tf_op jit(solution)/shard_map/ppermute | solution.py:492
  125.2 17.4 %all-to-all-start.2 = ((bf16[16,2,32,128]{3,2,1,0:T(8,128)(2,1)}), bf16[16,2,32,128]{3,2,1,0:T(8,128)(2,1)}, u32[]{:S(2)}, u32[]{:S(2)}) async-start(bf16[16,2,32,128]{3,2,1,0:T(8,128)(2,1)} %get-tuple-element.51), calls=%async_computation.3 | async-start | bytes 524288 | tf_op jit(solution)/shard_map/all_to_all | solution.py:399
  137.3 15.1 %collective-permute-start.12 = (bf16[144,512]{1,0:T(8,128)(2,1)}, bf16[144,512]{1,0:T(8,128)(2,1)}, u32[]{:S(2)}, u32[]{:S(2)}) collective-permute-start(bf16[144,512]{1,0:T(8,128)(2,1)} %pad_maximum_fusion.1), channel_id=1, source_target_pairs={{0,128},{128,0},{1,129},{129,1},{2,130},{130,2},{3,131},{131,3},{4... | collective-permute-start | bytes 442376 | tf_op jit(solution)/shard_map/ppermute | solution.py:395
  152.4 24.6 %all-to-all-start.3 = ((bf16[32,48,128]{2,1,0:T(8,128)(2,1)}), bf16[32,48,128]{2,1,0:T(8,128)(2,1)}, u32[]{:S(2)}, u32[]{:S(2)}) async-start(bf16[32,48,128]{2,1,0:T(8,128)(2,1)} %get-tuple-element.55), calls=%async_computation.4 | async-start | bytes 786432 | tf_op jit(solution)/shard_map/all_to_all | solution.py:505
  164.2 20.1 %collective-permute-start.9 = (bf16[128,1024]{1,0:T(8,128)(2,1)}, bf16[128,1024]{1,0:T(8,128)(2,1)}, u32[]{:S(2)}, u32[]{:S(2)}) collective-permute-start(bf16[128,1024]{1,0:T(8,128)(2,1)} %bitcast.25), channel_id=1, source_target_pairs={{0,0},{2,2},{4,128},{6,130},{128,4},{130,6},{132,132},{134,134},{1... | collective-permute-start | bytes 786440 | tf_op jit(solution)/shard_map/ppermute | solution.py:508
Sparse Core Ops, SparseCore 0:
  10.4 83.2 all-gather.2
  113.6 49.9 reduce-scatter.1

commit v4 on v3

--- a/solution.py
+++ b/solution.py
@@ -506,13 +506,13 @@
         once(gated_grad_rows, query_conv_other), SEQ, split_axis=0, concat_axis=0, tiled=True
     )
     block_output = lax.ppermute(summed, ("zh", "zl"), links(0, 0, True))
+    filter_grad = call(
+        filter_grad_kernel, shape_of((channels, length), F32), [held],
+        mixed_spec, gated_spec, first_out, twist, second_out,
+    )
     query_grad, key_grad, value_grad = call(
         last_kernel, (tokens_bf, tokens_bf, tokens_bf), [], key, value, halo, beyond, short_filter,
-        gated_grad_rows, query_conv_own, query_conv_other, edge_own,
-    )
-    filter_grad = call(
-        filter_grad_kernel, shape_of((channels, length), F32), [held],
-        once(mixed_spec, key_grad), gated_spec, first_out, twist, second_out,
+        once(gated_grad_rows, filter_grad), query_conv_own, query_conv_other, edge_own,
     )
     return (block_output, query_grad, key_grad, value_grad, filter_grad)
 

time: 194 us -> 192 us (0.990); the launches traced: 193 us -> 189 us
  waiting for transfers between devices: 36.8 us -> 32.5 us
    all_to_all x1, waiting for transfers between devices: 9.16 us -> 4.85 us  [shards(): lax.all_to_all(once(gated_grad_rows, query_conv_other), SEQ, split_axis=0...]
where the time goes in v4:
time: 192 us; the launch traced here: 189 us
  starting transfers between devices  88.6 us (46%)
  Pallas kernels  45.6 us (24%)
  waiting for transfers between devices  32.5 us (17%)
  between operations  14.1 us (7%)
  local copies, waits for them, and re-layouts  4.22 us (2%)
  other arithmetic  3.52 us (2%)
    pallas_call x12, Pallas kernels, call(): pl.pallas_call(kernel, out_shape=out_shape, grid=grid, in_specs=[specs.ge...  45.6 us
    ppermute x5, starting transfers between devices, swap(): return lax.ppermute(value, axis, [(0, 1), (1, 0)])  21.3 us
    all_to_all x1, starting transfers between devices, shards(): lax.all_to_all(gated_rows, SEQ, split_axis=0, concat_axis=0, tiled=True)  17.4 us
    all_to_all x2, starting transfers between devices, exchange(): lax.all_to_all(value, ('y', 'x'), split_axis=0, concat_axis=0, tiled=True)  15.4 us
    all_to_all x1, starting transfers between devices, shards(): lax.all_to_all(once(gated_grad_rows, query_conv_other), SEQ, split_axis=0...  11.8 us
    ppermute x5, waiting for transfers between devices, swap(): return lax.ppermute(value, axis, [(0, 1), (1, 0)])  11.4 us
    ppermute x4, starting transfers between devices, shards(): lax.ppermute(cot_there, ('zh', 'zl'), links(k1, k2, False))  11.4 us
    all_to_all x1, waiting for transfers between devices, shards(): lax.all_to_all(gated_rows, SEQ, split_axis=0, concat_axis=0, tiled=True)  7.58 us
  transfers between devices with their start and end apart: 19, of which 9 were waited for; matrix products, arithmetic and copies ran while one was open for 3% of the time, Pallas kernels for 24%

profile of v4, /device:TPU:2, one launch (start us, length us, event | category | flops | bytes accessed | tf_op | source)
XLA Modules:
  0.0 188.6 jit_solution(14423710792293818913)
XLA Ops:
  7.2 0.0 all-gather.3.cloned.1.call-start
  7.2 0.7 all-gather.3.cloned.1.call-update
  7.9 1.4 shard_map.155
  9.3 3.4 %collective-permute-start = (bf16[48,1024]{1,0:T(8,128)(2,1)}, bf16[48,1024]{1,0:T(8,128)(2,1)}, u32[]{:S(2)}, u32[]{:S(2)}) collective-permute-start(bf16[48,1024]{1,0:T(8,128)(2,1)} %shard_map.155), channel_id=1, source_target_pairs={{0,8},{8,16},{16,24},{24,32},{32,40},{40,48},{48,56},{56,64},{64,7... | collective-permute-start | bytes 294920 | tf_op jit(solution)/shard_map/ppermute | solution.py:439
  12.7 3.1 %shard_map.156.filter_spec = f32[1024,256]{1,0:T(8,128)} custom-call(f32[32,4096]{1,0:T(8,128)} %signal.1, bf16[64,96]{1,0:T(8,128)(2,1)} %constant.31.clone.first_in, f32[2,32,128]{2,1,0:T(8,128)} %constant.33.clone.twist, bf16[2,256,256]{2,1,0:T(8,128)(2,1)} %constant.34.clone.second_in), custom_call_target="tpu_custom_call" | custom-call | flops 1024 | bytes 1024 | tf_op jit(solution)/shard_map/pallas_call | solution.py:192
  15.8 0.4 collective-permute-done.halo
  16.2 2.3 %shard_map.158 = bf16[1024,128]{1,0:T(8,128)(2,1)} custom-call(bf16[128,1024]{1,0:T(8,128)(2,1)} %key.5, bf16[128,1024]{1,0:T(8,128)(2,1)} %value.5, bf16[48,1024]{1,0:T(8,128)(2,1)} %collective-permute-done.halo, f32[3,3,1024]{2,1,0:T(4,128)} %short_filter.7), custom_call_target="tpu_custom_call" | custom-call | flops 1024 | bytes 1024 | tf_op jit(solution)/shard_map/pallas_call | solution.py:192
  18.4 17.4 %all-to-all-start = ((bf16[32,32,128]{2,1,0:T(8,128)(2,1)}), bf16[32,32,128]{2,1,0:T(8,128)(2,1)}, u32[]{:S(2)}, u32[]{:S(2)}) async-start(bf16[32,32,128]{2,1,0:T(8,128)(2,1)} %bitcast.24), calls=%async_computation | async-start | bytes 524288 | tf_op jit(solution)/shard_map/all_to_all | solution.py:444
  35.8 1.7 shard_map.157
  37.5 5.4 %collective-permute-start.1 = (bf16[144,512]{1,0:T(8,128)(2,1)}, bf16[144,512]{1,0:T(8,128)(2,1)}, u32[]{:S(2)}, u32[]{:S(2)}) collective-permute-start(bf16[144,512]{1,0:T(8,128)(2,1)} %get-tuple-element.36), channel_id=1, source_target_pairs={{0,128},{128,0},{1,129},{129,1},{2,130},{130,2},{3,131},{131,3},{4... | collective-permute-start | bytes 442376 | tf_op jit(solution)/shard_map/ppermute | solution.py:395
  42.9 7.6 %all-to-all-done = bf16[32,32,128]{2,1,0:T(8,128)(2,1)} async-done(((bf16[32,32,128]{2,1,0:T(8,128)(2,1)}), bf16[32,32,128]{2,1,0:T(8,128)(2,1)}, u32[]{:S(2)}, u32[]{:S(2)}) %all-to-all-start) | async-done | bytes 262176 | tf_op jit(solution)/shard_map/all_to_all | solution.py:444
  50.5 3.6 %collective-permute-start.4 = (bf16[128,1024]{1,0:T(8,128)(2,1)}, bf16[128,1024]{1,0:T(8,128)(2,1)}, u32[]{:S(2)}, u32[]{:S(2)}) collective-permute-start(bf16[128,1024]{1,0:T(8,128)(2,1)} %param.18), channel_id=1, source_target_pairs={{0,0},{2,2},{128,4},{130,6},{4,128},{6,130},{132,132},{134,134},{1... | collective-permute-start | bytes 786440 | tf_op jit(solution)/shard_map/ppermute | solution.py:456
  54.1 4.9 %collective-permute-start.5 = (bf16[128,1024]{1,0:T(8,128)(2,1)}, bf16[128,1024]{1,0:T(8,128)(2,1)}, u32[]{:S(2)}, u32[]{:S(2)}) collective-permute-start(bf16[128,1024]{1,0:T(8,128)(2,1)} %param.18), channel_id=1, source_target_pairs={{2,0},{0,2},{130,4},{128,6},{6,128},{4,130},{134,132},{132,134},{3... | collective-permute-start | bytes 786440 | tf_op jit(solution)/shard_map/ppermute | solution.py:456
  59.0 2.9 %collective-permute-start.7 = (bf16[128,1024]{1,0:T(8,128)(2,1)}, bf16[128,1024]{1,0:T(8,128)(2,1)}, u32[]{:S(2)}, u32[]{:S(2)}) collective-permute-start(bf16[128,1024]{1,0:T(8,128)(2,1)} %param.18), channel_id=1, source_target_pairs={{130,0},{128,2},{2,4},{0,6},{134,128},{132,130},{6,132},{4,134},{1... | collective-permute-start | bytes 786440 | tf_op jit(solution)/shard_map/ppermute | solution.py:456
  61.9 5.4 %shard_map.159 = (bf16[16,2,32,128]{3,2,1,0:T(8,128)(2,1)}, f32[1024,256]{1,0:T(8,128)}) custom-call(bf16[1024,128]{1,0:T(8,128)(2,1)} %bitcast.1.signal, f32[1024,256]{1,0:T(8,128)} %shard_map.156.filter_spec, bf16[64,96]{1,0:T(8,128)(2,1)} %constant.31.clone.first_in, bf16[32,192]{1,0:T(8,128)(2,1)} %constant.32.clone.first_out, ...), custom_call_target="tpu_custom_call" | custom-call | flops 1024 | bytes 1024 | tf_op jit(solution)/shard_map/pallas_call | solution.py:192
  67.4 5.5 %all-to-all-start.1 = ((bf16[16,2,32,128]{3,2,1,0:T(8,128)(2,1)}), bf16[16,2,32,128]{3,2,1,0:T(8,128)(2,1)}, u32[]{:S(2)}, u32[]{:S(2)}) async-start(bf16[16,2,32,128]{3,2,1,0:T(8,128)(2,1)} %get-tuple-element.38), calls=%async_computation.1 | async-start | bytes 524288 | tf_op jit(solution)/shard_map/all_to_all | solution.py:399
  72.9 0.0 reduce-scatter.2.cloned.1.call-start
  72.9 0.8 slice.14
  73.7 0.8 slice.15
  74.5 2.2 %collective-permute-start.2 = (bf16[32,1024]{1,0:T(8,128)(2,1)S(1)}, bf16[32,1024]{1,0:T(8,128)(2,1)S(1)}, u32[]{:S(2)}, u32[]{:S(2)}) collective-permute-start(bf16[32,1024]{1,0:T(8,128)(2,1)S(1)} %pad_maximum_fusion.2), channel_id=1, source_target_pairs={{8,0},{16,8},{24,16},{32,24},{40,32},{48,40},{56,48},{64,56},{72,6... | collective-permute-start | bytes 196616 | tf_op jit(solution)/shard_map/ppermute | solution.py:452
  76.7 5.5 %collective-permute-done.2.beyond = bf16[32,1024]{1,0:T(8,128)(2,1)S(1)} collective-permute-done((bf16[32,1024]{1,0:T(8,128)(2,1)S(1)}, bf16[32,1024]{1,0:T(8,128)(2,1)S(1)}, u32[]{:S(2)}, u32[]{:S(2)}) %collective-permute-start.2) | collective-permute-done | bytes 65568 | tf_op jit(solution)/shard_map/ppermute | solution.py:452
  82.2 1.0 all-to-all-done.1.mixed_rows
  83.2 2.2 %shard_map.160 = (bf16[2,128,512]{2,1,0:T(8,128)(2,1)}, bf16[2,128,512]{2,1,0:T(8,128)(2,1)}) custom-call(bf16[144,512]{1,0:T(8,128)(2,1)} %get-tuple-element.35.own, bf16[144,512]{1,0:T(8,128)(2,1)} %collective-permute-done.1.other, f32[3,3,1024]{2,1,0:T(4,128)} %short_filter.7, bf16[16,2,32,128]{3,2,1,0:T(8,128)(2,1)} %all-to-all-done.1.mixed_rows), custom_call_target="tpu_custom_call" | custom-call | flops 1024 | bytes 1024 | tf_op jit(solution)/shard_map/pallas_call | solution.py:192
  85.4 1.3 pad_maximum_fusion.cot
  86.8 1.0 copy-done
  87.8 4.9 %collective-permute-start.3 = (bf16[2,128,512]{2,1,0:T(8,128)(2,1)}, bf16[2,128,512]{2,1,0:T(8,128)(2,1)}, u32[]{:S(2)}, u32[]{:S(2)}) collective-permute-start(bf16[2,128,512]{2,1,0:T(8,128)(2,1)} %get-tuple-element.40.product), channel_id=1, source_target_pairs={{0,128},{128,0},{1,129},{129,1},{2,130},{130,2},{3,131},{131,3},{4... | collective-permute-start | bytes 786440 | tf_op jit(solution)/shard_map/ppermute | solution.py:395
  92.7 1.0 all-gather.3.cloned.1.call-done
  93.7 7.3 %shard_map.161 = (f32[2,128,512]{2,1,0:T(8,128)}, bf16[2,128,512]{2,1,0:T(8,128)(2,1)}) custom-call(bf16[4,128,1024]{2,1,0:T(8,128)(2,1)} %copy-done, bf16[4,128,1024]{2,1,0:T(8,128)(2,1)} %collective-permute-done.8.beside, bf16[16,1024,256]{2,1,0:T(8,128)(2,1)} %bitcast.21), custom_call_target="tpu_custom_call" | custom-call | flops 1024 | bytes 1024 | tf_op jit(solution)/shard_map/pallas_call | solution.py:192
  101.0 5.7 %collective-permute-start.10 = (bf16[2,128,512]{2,1,0:T(8,128)(2,1)}, bf16[2,128,512]{2,1,0:T(8,128)(2,1)}, u32[]{:S(2)}, u32[]{:S(2)}) collective-permute-start(bf16[2,128,512]{2,1,0:T(8,128)(2,1)} %get-tuple-element.46), channel_id=1, source_target_pairs={{0,128},{128,0},{1,129},{129,1},{2,130},{130,2},{3,131},{131,3},{4... | collective-permute-start | bytes 786440 | tf_op jit(solution)/shard_map/ppermute | solution.py:395
  106.8 6.6 %shard_map.162 = bf16[2,4,128,1024]{3,2,1,0:T(8,128)(2,1)} custom-call(bf16[2,128,512]{2,1,0:T(8,128)(2,1)} %get-tuple-element.40.product, bf16[2,128,512]{2,1,0:T(8,128)(2,1)} %collective-permute-done.3.beside, bf16[16,1024,256]{2,1,0:T(8,128)(2,1)} %bitcast.22), custom_call_target="tpu_custom_call" | custom-call | flops 17179869184 | bytes 1024 | tf_op jit(solution)/shard_map/pallas_call | solution.py:192
  113.4 0.0 reduce-scatter.2.cloned.1.call-update
  113.4 7.4 %collective-permute-done.10.beside = bf16[2,128,512]{2,1,0:T(8,128)(2,1)} collective-permute-done((bf16[2,128,512]{2,1,0:T(8,128)(2,1)}, bf16[2,128,512]{2,1,0:T(8,128)(2,1)}, u32[]{:S(2)}, u32[]{:S(2)}) %collective-permute-start.10) | collective-permute-done | bytes 262176 | tf_op jit(solution)/shard_map/ppermute | solution.py:395
  120.8 2.4 %shard_map.163 = (bf16[16,2,32,128]{3,2,1,0:T(8,128)(2,1)}, f32[128,512]{1,0:T(8,128)}, bf16[128,512]{1,0:T(8,128)(2,1)}, bf16[2,16,512]{2,1,0:T(8,128)(2,1)}) custom-call(f32[2,128,512]{2,1,0:T(8,128)} %get-tuple-element.48.keep, bf16[2,128,512]{2,1,0:T(8,128)(2,1)} %collective-permute-done.10.beside, bf16[144,512]{1,0:T(8,128)(2,1)} %get-tuple-element.35.own, ...), custom_call_target="tpu_custom_call" | custom-call | flops 8589934592 | bytes 1024 | tf_op jit(solution)/shard_map/pallas_call | solution.py:192
  123.2 2.0 %collective-permute-start.11 = (bf16[2,16,512]{2,1,0:T(8,128)(2,1)}, bf16[2,16,512]{2,1,0:T(8,128)(2,1)S(1)}, u32[]{:S(2)}, u32[]{:S(2)}) collective-permute-start(bf16[2,16,512]{2,1,0:T(8,128)(2,1)} %get-tuple-element.54), channel_id=1, source_target_pairs={{8,0},{16,8},{24,16},{32,24},{40,32},{48,40},{56,48},{64,56},{72,6... | collective-permute-start | bytes 98312 | tf_op jit(solution)/shard_map/ppermute | solution.py:492
  125.2 9.9 %all-to-all-start.2 = ((bf16[16,2,32,128]{3,2,1,0:T(8,128)(2,1)}), bf16[16,2,32,128]{3,2,1,0:T(8,128)(2,1)}, u32[]{:S(2)}, u32[]{:S(2)}) async-start(bf16[16,2,32,128]{3,2,1,0:T(8,128)(2,1)} %get-tuple-element.51), calls=%async_computation.3 | async-start | bytes 524288 | tf_op jit(solution)/shard_map/all_to_all | solution.py:399
  135.1 0.6 select_select_fusion
  135.7 1.6 pad_maximum_fusion.1
  137.3 5.3 %collective-permute-start.12 = (bf16[144,512]{1,0:T(8,128)(2,1)}, bf16[144,512]{1,0:T(8,128)(2,1)}, u32[]{:S(2)}, u32[]{:S(2)}) collective-permute-start(bf16[144,512]{1,0:T(8,128)(2,1)} %pad_maximum_fusion.1), channel_id=1, source_target_pairs={{0,128},{128,0},{1,129},{129,1},{2,130},{130,2},{3,131},{131,3},{4... | collective-permute-start | bytes 442376 | tf_op jit(solution)/shard_map/ppermute | solution.py:395
  142.6 0.1 all-to-all-done.2.signal
  142.6 5.8 %shard_map.164 = (bf16[32,48,128]{2,1,0:T(8,128)(2,1)}, f32[1024,256]{1,0:T(8,128)}) custom-call(bf16[16,2,32,128]{3,2,1,0:T(8,128)(2,1)} %all-to-all-done.2.signal, f32[1024,256]{1,0:T(8,128)} %shard_map.156.filter_spec, bf16[64,96]{1,0:T(8,128)(2,1)} %constant.31.clone.first_in, bf16[32,192]{1,0:T(8,128)(2,1)} %constant.32.clone.first_out, ...), custom_call_target="tpu_custom_call" | custom-call | flops 34359738368 | bytes 1024 | tf_op jit(solution)/shard_map/pallas_call | solution.py:192
  148.4 4.0 %collective-permute-done.12.query_other = bf16[144,512]{1,0:T(8,128)(2,1)} collective-permute-done((bf16[144,512]{1,0:T(8,128)(2,1)}, bf16[144,512]{1,0:T(8,128)(2,1)}, u32[]{:S(2)}, u32[]{:S(2)}) %collective-permute-start.12) | collective-permute-done | bytes 147488 | tf_op jit(solution)/shard_map/ppermute | solution.py:395
  152.4 11.8 %all-to-all-start.3 = ((bf16[32,48,128]{2,1,0:T(8,128)(2,1)}), bf16[32,48,128]{2,1,0:T(8,128)(2,1)}, u32[]{:S(2)}, u32[]{:S(2)}) async-start(bf16[32,48,128]{2,1,0:T(8,128)(2,1)} %get-tuple-element.55), calls=%async_computation.4 | async-start | bytes 786432 | tf_op jit(solution)/shard_map/all_to_all | solution.py:505
  164.2 0.0 reduce-scatter.2.cloned.1.call-done
  164.2 3.6 %collective-permute-start.9 = (bf16[128,1024]{1,0:T(8,128)(2,1)}, bf16[128,1024]{1,0:T(8,128)(2,1)}, u32[]{:S(2)}, u32[]{:S(2)}) collective-permute-start(bf16[128,1024]{1,0:T(8,128)(2,1)} %bitcast.25), channel_id=1, source_target_pairs={{0,0},{2,2},{4,128},{6,130},{128,4},{130,6},{132,132},{134,134},{1... | collective-permute-start | bytes 786440 | tf_op jit(solution)/shard_map/ppermute | solution.py:508
  167.8 4.1 %shard_map.165 = f32[32,4096]{1,0:T(8,128)} custom-call(f32[1024,256]{1,0:T(8,128)} %get-tuple-element.56.first_spec, f32[1024,256]{1,0:T(8,128)} %get-tuple-element.57.second_spec, bf16[32,192]{1,0:T(8,128)(2,1)} %constant.32.clone.first_out, f32[2,32,128]{2,1,0:T(8,128)} %constant.33.clone.twist, bf16[2,256,256]{2,1,0:T(8,128)(2,1)} %constant.35.clone.second_out), custom_call_target="tpu_custom_call" | custom-call | flops 1024 | bytes 1024 | tf_op jit(solution)/shard_map/pallas_call | solution.py:192
  171.9 4.8 %all-to-all-done.3.gated_grad_rows = bf16[32,48,128]{2,1,0:T(8,128)(2,1)} async-done(((bf16[32,48,128]{2,1,0:T(8,128)(2,1)}), bf16[32,48,128]{2,1,0:T(8,128)(2,1)}, u32[]{:S(2)}, u32[]{:S(2)}) %all-to-all-start.3) | async-done | bytes 393248 | tf_op jit(solution)/shard_map/all_to_all | solution.py:505
  176.8 3.3 %shard_map.166 = (bf16[128,1024]{1,0:T(8,128)(2,1)}, bf16[128,1024]{1,0:T(8,128)(2,1)}, bf16[128,1024]{1,0:T(8,128)(2,1)}) custom-call(bf16[128,1024]{1,0:T(8,128)(2,1)} %key.5, bf16[128,1024]{1,0:T(8,128)(2,1)} %value.5, bf16[48,1024]{1,0:T(8,128)(2,1)} %collective-permute-done.halo, bf16[32,1024]{1,0:T(8,128)(2,1)} %copy-done.1, ...), custom_call_target="tpu_custom_call" | custom-call | flops 1024 | bytes 1024 | tf_op jit(solution)/shard_map/pallas_call | solution.py:192
  180.0 1.7 copy.18
  (15 shorter events, 0.0 us)
Async XLA Ops:
  7.2 86.5 %all-gather.3.cloned.1.call-start = ((), (), s32[]{:S(2)}) async-start(), calls=%async_computation.6 | async-start | bytes 8912896 | tf_op jit(solution)/shard_map/all_gather | solution.py:422
  9.3 6.8 %collective-permute-start = (bf16[48,1024]{1,0:T(8,128)(2,1)}, bf16[48,1024]{1,0:T(8,128)(2,1)}, u32[]{:S(2)}, u32[]{:S(2)}) collective-permute-start(bf16[48,1024]{1,0:T(8,128)(2,1)} %shard_map.155), channel_id=1, source_target_pairs={{0,8},{8,16},{16,24},{24,32},{32,40},{40,48},{48,56},{56,64},{64,7... | collective-permute-start | bytes 294920 | tf_op jit(solution)/shard_map/ppermute | solution.py:439
  18.4 32.1 %all-to-all-start = ((bf16[32,32,128]{2,1,0:T(8,128)(2,1)}), bf16[32,32,128]{2,1,0:T(8,128)(2,1)}, u32[]{:S(2)}, u32[]{:S(2)}) async-start(bf16[32,32,128]{2,1,0:T(8,128)(2,1)} %bitcast.24), calls=%async_computation | async-start | bytes 524288 | tf_op jit(solution)/shard_map/all_to_all | solution.py:444
  37.5 24.4 %collective-permute-start.1 = (bf16[144,512]{1,0:T(8,128)(2,1)}, bf16[144,512]{1,0:T(8,128)(2,1)}, u32[]{:S(2)}, u32[]{:S(2)}) collective-permute-start(bf16[144,512]{1,0:T(8,128)(2,1)} %get-tuple-element.36), channel_id=1, source_target_pairs={{0,128},{128,0},{1,129},{129,1},{2,130},{130,2},{3,131},{131,3},{4... | collective-permute-start | bytes 442376 | tf_op jit(solution)/shard_map/ppermute | solution.py:395
  50.5 34.9 %collective-permute-start.4 = (bf16[128,1024]{1,0:T(8,128)(2,1)}, bf16[128,1024]{1,0:T(8,128)(2,1)}, u32[]{:S(2)}, u32[]{:S(2)}) collective-permute-start(bf16[128,1024]{1,0:T(8,128)(2,1)} %param.18), channel_id=1, source_target_pairs={{0,0},{2,2},{128,4},{130,6},{4,128},{6,130},{132,132},{134,134},{1... | collective-permute-start | bytes 786440 | tf_op jit(solution)/shard_map/ppermute | solution.py:456
  54.1 31.3 %collective-permute-start.5 = (bf16[128,1024]{1,0:T(8,128)(2,1)}, bf16[128,1024]{1,0:T(8,128)(2,1)}, u32[]{:S(2)}, u32[]{:S(2)}) collective-permute-start(bf16[128,1024]{1,0:T(8,128)(2,1)} %param.18), channel_id=1, source_target_pairs={{2,0},{0,2},{130,4},{128,6},{6,128},{4,130},{134,132},{132,134},{3... | collective-permute-start | bytes 786440 | tf_op jit(solution)/shard_map/ppermute | solution.py:456
  59.0 26.4 %collective-permute-start.6 = (bf16[128,1024]{1,0:T(8,128)(2,1)}, bf16[128,1024]{1,0:T(8,128)(2,1)}, u32[]{:S(2)}, u32[]{:S(2)}) collective-permute-start(bf16[128,1024]{1,0:T(8,128)(2,1)} %param.18), channel_id=1, source_target_pairs={{128,0},{130,2},{0,4},{2,6},{132,128},{134,130},{4,132},{6,134},{1... | collective-permute-start | bytes 786440 | tf_op jit(solution)/shard_map/ppermute | solution.py:456
  59.0 26.4 %collective-permute-start.7 = (bf16[128,1024]{1,0:T(8,128)(2,1)}, bf16[128,1024]{1,0:T(8,128)(2,1)}, u32[]{:S(2)}, u32[]{:S(2)}) collective-permute-start(bf16[128,1024]{1,0:T(8,128)(2,1)} %param.18), channel_id=1, source_target_pairs={{130,0},{128,2},{2,4},{0,6},{134,128},{132,130},{6,132},{4,134},{1... | collective-permute-start | bytes 786440 | tf_op jit(solution)/shard_map/ppermute | solution.py:456
  67.4 15.8 %all-to-all-start.1 = ((bf16[16,2,32,128]{3,2,1,0:T(8,128)(2,1)}), bf16[16,2,32,128]{3,2,1,0:T(8,128)(2,1)}, u32[]{:S(2)}, u32[]{:S(2)}) async-start(bf16[16,2,32,128]{3,2,1,0:T(8,128)(2,1)} %get-tuple-element.38), calls=%async_computation.1 | async-start | bytes 524288 | tf_op jit(solution)/shard_map/all_to_all | solution.py:399
  72.9 91.3 %reduce-scatter.2.cloned.1.call-start = ((), (), s32[]{:S(2)}) async-start(), calls=%async_computation.5 | async-start | bytes 2359296 | tf_op jit(solution)/shard_map/reduce_scatter | solution.py:486
  74.5 7.7 %collective-permute-start.2 = (bf16[32,1024]{1,0:T(8,128)(2,1)S(1)}, bf16[32,1024]{1,0:T(8,128)(2,1)S(1)}, u32[]{:S(2)}, u32[]{:S(2)}) collective-permute-start(bf16[32,1024]{1,0:T(8,128)(2,1)S(1)} %pad_maximum_fusion.2), channel_id=1, source_target_pairs={{8,0},{16,8},{24,16},{32,24},{40,32},{48,40},{56,48},{64,56},{72,6... | collective-permute-start | bytes 196616 | tf_op jit(solution)/shard_map/ppermute | solution.py:452
  82.2 31.2 %copy-start.1 = (bf16[32,1024]{1,0:T(8,128)(2,1)}, bf16[32,1024]{1,0:T(8,128)(2,1)S(1)}, u32[]{:S(2)}) copy-start(bf16[32,1024]{1,0:T(8,128)(2,1)S(1)} %collective-permute-done.2.beyond) | copy-start | bytes 196612
  86.8 1.0 copy-start
  87.8 4.9 %collective-permute-start.8 = (bf16[4,128,1024]{2,1,0:T(8,128)(2,1)S(1)}, bf16[4,128,1024]{2,1,0:T(8,128)(2,1)}, u32[]{:S(2)}, u32[]{:S(2)}) collective-permute-start(bf16[4,128,1024]{2,1,0:T(8,128)(2,1)S(1)} %pad_maximum_fusion.cot), channel_id=1, source_target_pairs={{0,1},{1,0},{2,3},{3,2},{4,5},{5,4},{6,7},{7,6},{8,9},{9,8},{10,11... | collective-permute-start | bytes 3145736 | tf_op jit(solution)/shard_map/ppermute | solution.py:395
  87.8 19.0 %collective-permute-start.3 = (bf16[2,128,512]{2,1,0:T(8,128)(2,1)}, bf16[2,128,512]{2,1,0:T(8,128)(2,1)}, u32[]{:S(2)}, u32[]{:S(2)}) collective-permute-start(bf16[2,128,512]{2,1,0:T(8,128)(2,1)} %get-tuple-element.40.product), channel_id=1, source_target_pairs={{0,128},{128,0},{1,129},{129,1},{2,130},{130,2},{3,131},{131,3},{4... | collective-permute-start | bytes 786440 | tf_op jit(solution)/shard_map/ppermute | solution.py:395
  101.0 19.8 %collective-permute-start.10 = (bf16[2,128,512]{2,1,0:T(8,128)(2,1)}, bf16[2,128,512]{2,1,0:T(8,128)(2,1)}, u32[]{:S(2)}, u32[]{:S(2)}) collective-permute-start(bf16[2,128,512]{2,1,0:T(8,128)(2,1)} %get-tuple-element.46), channel_id=1, source_target_pairs={{0,128},{128,0},{1,129},{129,1},{2,130},{130,2},{3,131},{131,3},{4... | collective-permute-start | bytes 786440 | tf_op jit(solution)/shard_map/ppermute | solution.py:395
  123.2 11.9 %collective-permute-start.11 = (bf16[2,16,512]{2,1,0:T(8,128)(2,1)}, bf16[2,16,512]{2,1,0:T(8,128)(2,1)S(1)}, u32[]{:S(2)}, u32[]{:S(2)}) collective-permute-start(bf16[2,16,512]{2,1,0:T(8,128)(2,1)} %get-tuple-element.54), channel_id=1, source_target_pairs={{8,0},{16,8},{24,16},{32,24},{40,32},{48,40},{56,48},{64,56},{72,6... | collective-permute-start | bytes 98312 | tf_op jit(solution)/shard_map/ppermute | solution.py:492
  125.2 17.4 %all-to-all-start.2 = ((bf16[16,2,32,128]{3,2,1,0:T(8,128)(2,1)}), bf16[16,2,32,128]{3,2,1,0:T(8,128)(2,1)}, u32[]{:S(2)}, u32[]{:S(2)}) async-start(bf16[16,2,32,128]{3,2,1,0:T(8,128)(2,1)} %get-tuple-element.51), calls=%async_computation.3 | async-start | bytes 524288 | tf_op jit(solution)/shard_map/all_to_all | solution.py:399
  137.3 15.1 %collective-permute-start.12 = (bf16[144,512]{1,0:T(8,128)(2,1)}, bf16[144,512]{1,0:T(8,128)(2,1)}, u32[]{:S(2)}, u32[]{:S(2)}) collective-permute-start(bf16[144,512]{1,0:T(8,128)(2,1)} %pad_maximum_fusion.1), channel_id=1, source_target_pairs={{0,128},{128,0},{1,129},{129,1},{2,130},{130,2},{3,131},{131,3},{4... | collective-permute-start | bytes 442376 | tf_op jit(solution)/shard_map/ppermute | solution.py:395
  152.4 24.3 %all-to-all-start.3 = ((bf16[32,48,128]{2,1,0:T(8,128)(2,1)}), bf16[32,48,128]{2,1,0:T(8,128)(2,1)}, u32[]{:S(2)}, u32[]{:S(2)}) async-start(bf16[32,48,128]{2,1,0:T(8,128)(2,1)} %get-tuple-element.55), calls=%async_computation.4 | async-start | bytes 786432 | tf_op jit(solution)/shard_map/all_to_all | solution.py:505
  164.2 15.8 %collective-permute-start.9 = (bf16[128,1024]{1,0:T(8,128)(2,1)}, bf16[128,1024]{1,0:T(8,128)(2,1)}, u32[]{:S(2)}, u32[]{:S(2)}) collective-permute-start(bf16[128,1024]{1,0:T(8,128)(2,1)} %bitcast.25), channel_id=1, source_target_pairs={{0,0},{2,2},{4,128},{6,130},{128,4},{130,6},{132,132},{134,134},{1... | collective-permute-start | bytes 786440 | tf_op jit(solution)/shard_map/ppermute | solution.py:508
Sparse Core Ops, SparseCore 0:
  10.4 83.2 all-gather.2
  113.6 49.8 reduce-scatter.1

commit v5 on v4

--- a/solution.py
+++ b/solution.py
@@ -316,8 +316,8 @@
 ):
     tokens = query_own.shape[0]
     for which, grad, after in (
-        (0, query_own[...], edge_own[:8, :]),
-        (1, query_other[:tokens, :], query_other[tokens : tokens + 8, :]),
+        (0, query_own[...], edge_own[...]),
+        (1, query_other[:tokens, :], query_other[tokens:, :]),
     ):
         columns = columns_of(which, grad.shape[1])
         taps = taps_of(short_filter, 0, columns)

time: 192 us -> 192 us (level)
  no operation moved by 1% of the time
where the time goes in v5:
time: 192 us; the launch traced here: 189 us
  starting transfers between devices  88.6 us (46%)
  Pallas kernels  45.6 us (24%)
  waiting for transfers between devices  32.5 us (17%)
  between operations  14.1 us (7%)
  local copies, waits for them, and re-layouts  4.22 us (2%)
  other arithmetic  3.52 us (2%)
    pallas_call x12, Pallas kernels, call(): pl.pallas_call(kernel, out_shape=out_shape, grid=grid, in_specs=[specs.ge...  45.6 us
    ppermute x5, starting transfers between devices, swap(): return lax.ppermute(value, axis, [(0, 1), (1, 0)])  21.3 us
    all_to_all x1, starting transfers between devices, shards(): lax.all_to_all(gated_rows, SEQ, split_axis=0, concat_axis=0, tiled=True)  17.4 us
    all_to_all x2, starting transfers between devices, exchange(): lax.all_to_all(value, ('y', 'x'), split_axis=0, concat_axis=0, tiled=True)  15.4 us
    all_to_all x1, starting transfers between devices, shards(): lax.all_to_all(once(gated_grad_rows, query_conv_other), SEQ, split_axis=0...  11.8 us
    ppermute x5, waiting for transfers between devices, swap(): return lax.ppermute(value, axis, [(0, 1), (1, 0)])  11.4 us
    ppermute x4, starting transfers between devices, shards(): lax.ppermute(cot_there, ('zh', 'zl'), links(k1, k2, False))  11.4 us
    all_to_all x1, waiting for transfers between devices, shards(): lax.all_to_all(gated_rows, SEQ, split_axis=0, concat_axis=0, tiled=True)  7.58 us
  transfers between devices with their start and end apart: 19, of which 9 were waited for; matrix products, arithmetic and copies ran while one was open for 3% of the time, Pallas kernels for 24%

profile of v5, /device:TPU:2, one launch (start us, length us, event | category | flops | bytes accessed | tf_op | source)
XLA Modules:
  0.0 188.6 jit_solution(14423710792293818913)
XLA Ops:
  7.2 0.0 all-gather.3.cloned.1.call-start
  7.2 0.7 all-gather.3.cloned.1.call-update
  7.9 1.4 shard_map.155
  9.3 3.4 %collective-permute-start = (bf16[48,1024]{1,0:T(8,128)(2,1)}, bf16[48,1024]{1,0:T(8,128)(2,1)}, u32[]{:S(2)}, u32[]{:S(2)}) collective-permute-start(bf16[48,1024]{1,0:T(8,128)(2,1)} %shard_map.155), channel_id=1, source_target_pairs={{0,8},{8,16},{16,24},{24,32},{32,40},{40,48},{48,56},{56,64},{64,7... | collective-permute-start | bytes 294920 | tf_op jit(solution)/shard_map/ppermute | solution.py:439
  12.7 3.1 %shard_map.156.filter_spec = f32[1024,256]{1,0:T(8,128)} custom-call(f32[32,4096]{1,0:T(8,128)} %signal.1, bf16[64,96]{1,0:T(8,128)(2,1)} %constant.31.clone.first_in, f32[2,32,128]{2,1,0:T(8,128)} %constant.33.clone.twist, bf16[2,256,256]{2,1,0:T(8,128)(2,1)} %constant.34.clone.second_in), custom_call_target="tpu_custom_call" | custom-call | flops 1024 | bytes 1024 | tf_op jit(solution)/shard_map/pallas_call | solution.py:192
  15.8 0.4 collective-permute-done.halo
  16.2 2.3 %shard_map.158 = bf16[1024,128]{1,0:T(8,128)(2,1)} custom-call(bf16[128,1024]{1,0:T(8,128)(2,1)} %key.5, bf16[128,1024]{1,0:T(8,128)(2,1)} %value.5, bf16[48,1024]{1,0:T(8,128)(2,1)} %collective-permute-done.halo, f32[3,3,1024]{2,1,0:T(4,128)} %short_filter.7), custom_call_target="tpu_custom_call" | custom-call | flops 1024 | bytes 1024 | tf_op jit(solution)/shard_map/pallas_call | solution.py:192
  18.4 17.4 %all-to-all-start = ((bf16[32,32,128]{2,1,0:T(8,128)(2,1)}), bf16[32,32,128]{2,1,0:T(8,128)(2,1)}, u32[]{:S(2)}, u32[]{:S(2)}) async-start(bf16[32,32,128]{2,1,0:T(8,128)(2,1)} %bitcast.24), calls=%async_computation | async-start | bytes 524288 | tf_op jit(solution)/shard_map/all_to_all | solution.py:444
  35.8 1.7 shard_map.157
  37.5 5.4 %collective-permute-start.1 = (bf16[144,512]{1,0:T(8,128)(2,1)}, bf16[144,512]{1,0:T(8,128)(2,1)}, u32[]{:S(2)}, u32[]{:S(2)}) collective-permute-start(bf16[144,512]{1,0:T(8,128)(2,1)} %get-tuple-element.36), channel_id=1, source_target_pairs={{0,128},{128,0},{1,129},{129,1},{2,130},{130,2},{3,131},{131,3},{4... | collective-permute-start | bytes 442376 | tf_op jit(solution)/shard_map/ppermute | solution.py:395
  42.9 7.6 %all-to-all-done = bf16[32,32,128]{2,1,0:T(8,128)(2,1)} async-done(((bf16[32,32,128]{2,1,0:T(8,128)(2,1)}), bf16[32,32,128]{2,1,0:T(8,128)(2,1)}, u32[]{:S(2)}, u32[]{:S(2)}) %all-to-all-start) | async-done | bytes 262176 | tf_op jit(solution)/shard_map/all_to_all | solution.py:444
  50.5 3.6 %collective-permute-start.4 = (bf16[128,1024]{1,0:T(8,128)(2,1)}, bf16[128,1024]{1,0:T(8,128)(2,1)}, u32[]{:S(2)}, u32[]{:S(2)}) collective-permute-start(bf16[128,1024]{1,0:T(8,128)(2,1)} %param.18), channel_id=1, source_target_pairs={{0,0},{2,2},{128,4},{130,6},{4,128},{6,130},{132,132},{134,134},{1... | collective-permute-start | bytes 786440 | tf_op jit(solution)/shard_map/ppermute | solution.py:456
  54.1 4.9 %collective-permute-start.5 = (bf16[128,1024]{1,0:T(8,128)(2,1)}, bf16[128,1024]{1,0:T(8,128)(2,1)}, u32[]{:S(2)}, u32[]{:S(2)}) collective-permute-start(bf16[128,1024]{1,0:T(8,128)(2,1)} %param.18), channel_id=1, source_target_pairs={{2,0},{0,2},{130,4},{128,6},{6,128},{4,130},{134,132},{132,134},{3... | collective-permute-start | bytes 786440 | tf_op jit(solution)/shard_map/ppermute | solution.py:456
  59.0 2.9 %collective-permute-start.7 = (bf16[128,1024]{1,0:T(8,128)(2,1)}, bf16[128,1024]{1,0:T(8,128)(2,1)}, u32[]{:S(2)}, u32[]{:S(2)}) collective-permute-start(bf16[128,1024]{1,0:T(8,128)(2,1)} %param.18), channel_id=1, source_target_pairs={{130,0},{128,2},{2,4},{0,6},{134,128},{132,130},{6,132},{4,134},{1... | collective-permute-start | bytes 786440 | tf_op jit(solution)/shard_map/ppermute | solution.py:456
  61.9 5.4 %shard_map.159 = (bf16[16,2,32,128]{3,2,1,0:T(8,128)(2,1)}, f32[1024,256]{1,0:T(8,128)}) custom-call(bf16[1024,128]{1,0:T(8,128)(2,1)} %bitcast.1.signal, f32[1024,256]{1,0:T(8,128)} %shard_map.156.filter_spec, bf16[64,96]{1,0:T(8,128)(2,1)} %constant.31.clone.first_in, bf16[32,192]{1,0:T(8,128)(2,1)} %constant.32.clone.first_out, ...), custom_call_target="tpu_custom_call" | custom-call | flops 1024 | bytes 1024 | tf_op jit(solution)/shard_map/pallas_call | solution.py:192
  67.4 5.5 %all-to-all-start.1 = ((bf16[16,2,32,128]{3,2,1,0:T(8,128)(2,1)}), bf16[16,2,32,128]{3,2,1,0:T(8,128)(2,1)}, u32[]{:S(2)}, u32[]{:S(2)}) async-start(bf16[16,2,32,128]{3,2,1,0:T(8,128)(2,1)} %get-tuple-element.38), calls=%async_computation.1 | async-start | bytes 524288 | tf_op jit(solution)/shard_map/all_to_all | solution.py:399
  72.9 0.0 reduce-scatter.2.cloned.1.call-start
  72.9 0.8 slice.14
  73.7 0.8 slice.15
  74.5 2.2 %collective-permute-start.2 = (bf16[32,1024]{1,0:T(8,128)(2,1)S(1)}, bf16[32,1024]{1,0:T(8,128)(2,1)S(1)}, u32[]{:S(2)}, u32[]{:S(2)}) collective-permute-start(bf16[32,1024]{1,0:T(8,128)(2,1)S(1)} %pad_maximum_fusion.2), channel_id=1, source_target_pairs={{8,0},{16,8},{24,16},{32,24},{40,32},{48,40},{56,48},{64,56},{72,6... | collective-permute-start | bytes 196616 | tf_op jit(solution)/shard_map/ppermute | solution.py:452
  76.7 5.5 %collective-permute-done.2.beyond = bf16[32,1024]{1,0:T(8,128)(2,1)S(1)} collective-permute-done((bf16[32,1024]{1,0:T(8,128)(2,1)S(1)}, bf16[32,1024]{1,0:T(8,128)(2,1)S(1)}, u32[]{:S(2)}, u32[]{:S(2)}) %collective-permute-start.2) | collective-permute-done | bytes 65568 | tf_op jit(solution)/shard_map/ppermute | solution.py:452
  82.2 1.0 all-to-all-done.1.mixed_rows
  83.2 2.2 %shard_map.160 = (bf16[2,128,512]{2,1,0:T(8,128)(2,1)}, bf16[2,128,512]{2,1,0:T(8,128)(2,1)}) custom-call(bf16[144,512]{1,0:T(8,128)(2,1)} %get-tuple-element.35.own, bf16[144,512]{1,0:T(8,128)(2,1)} %collective-permute-done.1.other, f32[3,3,1024]{2,1,0:T(4,128)} %short_filter.7, bf16[16,2,32,128]{3,2,1,0:T(8,128)(2,1)} %all-to-all-done.1.mixed_rows), custom_call_target="tpu_custom_call" | custom-call | flops 1024 | bytes 1024 | tf_op jit(solution)/shard_map/pallas_call | solution.py:192
  85.4 1.3 pad_maximum_fusion.cot
  86.8 1.0 copy-done
  87.8 4.9 %collective-permute-start.3 = (bf16[2,128,512]{2,1,0:T(8,128)(2,1)}, bf16[2,128,512]{2,1,0:T(8,128)(2,1)}, u32[]{:S(2)}, u32[]{:S(2)}) collective-permute-start(bf16[2,128,512]{2,1,0:T(8,128)(2,1)} %get-tuple-element.40.product), channel_id=1, source_target_pairs={{0,128},{128,0},{1,129},{129,1},{2,130},{130,2},{3,131},{131,3},{4... | collective-permute-start | bytes 786440 | tf_op jit(solution)/shard_map/ppermute | solution.py:395
  92.7 1.0 all-gather.3.cloned.1.call-done
  93.7 7.3 %shard_map.161 = (f32[2,128,512]{2,1,0:T(8,128)}, bf16[2,128,512]{2,1,0:T(8,128)(2,1)}) custom-call(bf16[4,128,1024]{2,1,0:T(8,128)(2,1)} %copy-done, bf16[4,128,1024]{2,1,0:T(8,128)(2,1)} %collective-permute-done.8.beside, bf16[16,1024,256]{2,1,0:T(8,128)(2,1)} %bitcast.21), custom_call_target="tpu_custom_call" | custom-call | flops 1024 | bytes 1024 | tf_op jit(solution)/shard_map/pallas_call | solution.py:192
  101.0 5.7 %collective-permute-start.10 = (bf16[2,128,512]{2,1,0:T(8,128)(2,1)}, bf16[2,128,512]{2,1,0:T(8,128)(2,1)}, u32[]{:S(2)}, u32[]{:S(2)}) collective-permute-start(bf16[2,128,512]{2,1,0:T(8,128)(2,1)} %get-tuple-element.46), channel_id=1, source_target_pairs={{0,128},{128,0},{1,129},{129,1},{2,130},{130,2},{3,131},{131,3},{4... | collective-permute-start | bytes 786440 | tf_op jit(solution)/shard_map/ppermute | solution.py:395
  106.8 6.6 %shard_map.162 = bf16[2,4,128,1024]{3,2,1,0:T(8,128)(2,1)} custom-call(bf16[2,128,512]{2,1,0:T(8,128)(2,1)} %get-tuple-element.40.product, bf16[2,128,512]{2,1,0:T(8,128)(2,1)} %collective-permute-done.3.beside, bf16[16,1024,256]{2,1,0:T(8,128)(2,1)} %bitcast.22), custom_call_target="tpu_custom_call" | custom-call | flops 17179869184 | bytes 1024 | tf_op jit(solution)/shard_map/pallas_call | solution.py:192
  113.4 0.0 reduce-scatter.2.cloned.1.call-update
  113.4 7.4 %collective-permute-done.10.beside = bf16[2,128,512]{2,1,0:T(8,128)(2,1)} collective-permute-done((bf16[2,128,512]{2,1,0:T(8,128)(2,1)}, bf16[2,128,512]{2,1,0:T(8,128)(2,1)}, u32[]{:S(2)}, u32[]{:S(2)}) %collective-permute-start.10) | collective-permute-done | bytes 262176 | tf_op jit(solution)/shard_map/ppermute | solution.py:395
  120.8 2.4 %shard_map.163 = (bf16[16,2,32,128]{3,2,1,0:T(8,128)(2,1)}, f32[128,512]{1,0:T(8,128)}, bf16[128,512]{1,0:T(8,128)(2,1)}, bf16[2,16,512]{2,1,0:T(8,128)(2,1)}) custom-call(f32[2,128,512]{2,1,0:T(8,128)} %get-tuple-element.48.keep, bf16[2,128,512]{2,1,0:T(8,128)(2,1)} %collective-permute-done.10.beside, bf16[144,512]{1,0:T(8,128)(2,1)} %get-tuple-element.35.own, ...), custom_call_target="tpu_custom_call" | custom-call | flops 8589934592 | bytes 1024 | tf_op jit(solution)/shard_map/pallas_call | solution.py:192
  123.2 2.0 %collective-permute-start.11 = (bf16[2,16,512]{2,1,0:T(8,128)(2,1)}, bf16[2,16,512]{2,1,0:T(8,128)(2,1)S(1)}, u32[]{:S(2)}, u32[]{:S(2)}) collective-permute-start(bf16[2,16,512]{2,1,0:T(8,128)(2,1)} %get-tuple-element.54), channel_id=1, source_target_pairs={{8,0},{16,8},{24,16},{32,24},{40,32},{48,40},{56,48},{64,56},{72,6... | collective-permute-start | bytes 98312 | tf_op jit(solution)/shard_map/ppermute | solution.py:492
  125.2 9.9 %all-to-all-start.2 = ((bf16[16,2,32,128]{3,2,1,0:T(8,128)(2,1)}), bf16[16,2,32,128]{3,2,1,0:T(8,128)(2,1)}, u32[]{:S(2)}, u32[]{:S(2)}) async-start(bf16[16,2,32,128]{3,2,1,0:T(8,128)(2,1)} %get-tuple-element.51), calls=%async_computation.3 | async-start | bytes 524288 | tf_op jit(solution)/shard_map/all_to_all | solution.py:399
  135.1 0.6 select_select_fusion
  135.7 1.6 pad_maximum_fusion.1
  137.3 5.3 %collective-permute-start.12 = (bf16[144,512]{1,0:T(8,128)(2,1)}, bf16[144,512]{1,0:T(8,128)(2,1)}, u32[]{:S(2)}, u32[]{:S(2)}) collective-permute-start(bf16[144,512]{1,0:T(8,128)(2,1)} %pad_maximum_fusion.1), channel_id=1, source_target_pairs={{0,128},{128,0},{1,129},{129,1},{2,130},{130,2},{3,131},{131,3},{4... | collective-permute-start | bytes 442376 | tf_op jit(solution)/shard_map/ppermute | solution.py:395
  142.6 0.1 all-to-all-done.2.signal
  142.6 5.8 %shard_map.164 = (bf16[32,48,128]{2,1,0:T(8,128)(2,1)}, f32[1024,256]{1,0:T(8,128)}) custom-call(bf16[16,2,32,128]{3,2,1,0:T(8,128)(2,1)} %all-to-all-done.2.signal, f32[1024,256]{1,0:T(8,128)} %shard_map.156.filter_spec, bf16[64,96]{1,0:T(8,128)(2,1)} %constant.31.clone.first_in, bf16[32,192]{1,0:T(8,128)(2,1)} %constant.32.clone.first_out, ...), custom_call_target="tpu_custom_call" | custom-call | flops 34359738368 | bytes 1024 | tf_op jit(solution)/shard_map/pallas_call | solution.py:192
  148.4 4.0 %collective-permute-done.12.query_other = bf16[144,512]{1,0:T(8,128)(2,1)} collective-permute-done((bf16[144,512]{1,0:T(8,128)(2,1)}, bf16[144,512]{1,0:T(8,128)(2,1)}, u32[]{:S(2)}, u32[]{:S(2)}) %collective-permute-start.12) | collective-permute-done | bytes 147488 | tf_op jit(solution)/shard_map/ppermute | solution.py:395
  152.4 11.8 %all-to-all-start.3 = ((bf16[32,48,128]{2,1,0:T(8,128)(2,1)}), bf16[32,48,128]{2,1,0:T(8,128)(2,1)}, u32[]{:S(2)}, u32[]{:S(2)}) async-start(bf16[32,48,128]{2,1,0:T(8,128)(2,1)} %get-tuple-element.55), calls=%async_computation.4 | async-start | bytes 786432 | tf_op jit(solution)/shard_map/all_to_all | solution.py:505
  164.2 0.0 reduce-scatter.2.cloned.1.call-done
  164.2 3.6 %collective-permute-start.9 = (bf16[128,1024]{1,0:T(8,128)(2,1)}, bf16[128,1024]{1,0:T(8,128)(2,1)}, u32[]{:S(2)}, u32[]{:S(2)}) collective-permute-start(bf16[128,1024]{1,0:T(8,128)(2,1)} %bitcast.25), channel_id=1, source_target_pairs={{0,0},{2,2},{4,128},{6,130},{128,4},{130,6},{132,132},{134,134},{1... | collective-permute-start | bytes 786440 | tf_op jit(solution)/shard_map/ppermute | solution.py:508
  167.8 4.1 %shard_map.165 = f32[32,4096]{1,0:T(8,128)} custom-call(f32[1024,256]{1,0:T(8,128)} %get-tuple-element.56.first_spec, f32[1024,256]{1,0:T(8,128)} %get-tuple-element.57.second_spec, bf16[32,192]{1,0:T(8,128)(2,1)} %constant.32.clone.first_out, f32[2,32,128]{2,1,0:T(8,128)} %constant.33.clone.twist, bf16[2,256,256]{2,1,0:T(8,128)(2,1)} %constant.35.clone.second_out), custom_call_target="tpu_custom_call" | custom-call | flops 1024 | bytes 1024 | tf_op jit(solution)/shard_map/pallas_call | solution.py:192
  171.9 4.8 %all-to-all-done.3.gated_grad_rows = bf16[32,48,128]{2,1,0:T(8,128)(2,1)} async-done(((bf16[32,48,128]{2,1,0:T(8,128)(2,1)}), bf16[32,48,128]{2,1,0:T(8,128)(2,1)}, u32[]{:S(2)}, u32[]{:S(2)}) %all-to-all-start.3) | async-done | bytes 393248 | tf_op jit(solution)/shard_map/all_to_all | solution.py:505
  176.8 3.3 %shard_map.166 = (bf16[128,1024]{1,0:T(8,128)(2,1)}, bf16[128,1024]{1,0:T(8,128)(2,1)}, bf16[128,1024]{1,0:T(8,128)(2,1)}) custom-call(bf16[128,1024]{1,0:T(8,128)(2,1)} %key.5, bf16[128,1024]{1,0:T(8,128)(2,1)} %value.5, bf16[48,1024]{1,0:T(8,128)(2,1)} %collective-permute-done.halo, bf16[32,1024]{1,0:T(8,128)(2,1)} %copy-done.1, ...), custom_call_target="tpu_custom_call" | custom-call | flops 1024 | bytes 1024 | tf_op jit(solution)/shard_map/pallas_call | solution.py:192
  180.0 1.7 copy.18
  (15 shorter events, 0.0 us)
Async XLA Ops:
  7.2 86.5 %all-gather.3.cloned.1.call-start = ((), (), s32[]{:S(2)}) async-start(), calls=%async_computation.6 | async-start | bytes 8912896 | tf_op jit(solution)/shard_map/all_gather | solution.py:422
  9.3 6.8 %collective-permute-start = (bf16[48,1024]{1,0:T(8,128)(2,1)}, bf16[48,1024]{1,0:T(8,128)(2,1)}, u32[]{:S(2)}, u32[]{:S(2)}) collective-permute-start(bf16[48,1024]{1,0:T(8,128)(2,1)} %shard_map.155), channel_id=1, source_target_pairs={{0,8},{8,16},{16,24},{24,32},{32,40},{40,48},{48,56},{56,64},{64,7... | collective-permute-start | bytes 294920 | tf_op jit(solution)/shard_map/ppermute | solution.py:439
  18.4 32.1 %all-to-all-start = ((bf16[32,32,128]{2,1,0:T(8,128)(2,1)}), bf16[32,32,128]{2,1,0:T(8,128)(2,1)}, u32[]{:S(2)}, u32[]{:S(2)}) async-start(bf16[32,32,128]{2,1,0:T(8,128)(2,1)} %bitcast.24), calls=%async_computation | async-start | bytes 524288 | tf_op jit(solution)/shard_map/all_to_all | solution.py:444
  37.5 24.4 %collective-permute-start.1 = (bf16[144,512]{1,0:T(8,128)(2,1)}, bf16[144,512]{1,0:T(8,128)(2,1)}, u32[]{:S(2)}, u32[]{:S(2)}) collective-permute-start(bf16[144,512]{1,0:T(8,128)(2,1)} %get-tuple-element.36), channel_id=1, source_target_pairs={{0,128},{128,0},{1,129},{129,1},{2,130},{130,2},{3,131},{131,3},{4... | collective-permute-start | bytes 442376 | tf_op jit(solution)/shard_map/ppermute | solution.py:395
  50.5 34.9 %collective-permute-start.4 = (bf16[128,1024]{1,0:T(8,128)(2,1)}, bf16[128,1024]{1,0:T(8,128)(2,1)}, u32[]{:S(2)}, u32[]{:S(2)}) collective-permute-start(bf16[128,1024]{1,0:T(8,128)(2,1)} %param.18), channel_id=1, source_target_pairs={{0,0},{2,2},{128,4},{130,6},{4,128},{6,130},{132,132},{134,134},{1... | collective-permute-start | bytes 786440 | tf_op jit(solution)/shard_map/ppermute | solution.py:456
  54.1 31.3 %collective-permute-start.5 = (bf16[128,1024]{1,0:T(8,128)(2,1)}, bf16[128,1024]{1,0:T(8,128)(2,1)}, u32[]{:S(2)}, u32[]{:S(2)}) collective-permute-start(bf16[128,1024]{1,0:T(8,128)(2,1)} %param.18), channel_id=1, source_target_pairs={{2,0},{0,2},{130,4},{128,6},{6,128},{4,130},{134,132},{132,134},{3... | collective-permute-start | bytes 786440 | tf_op jit(solution)/shard_map/ppermute | solution.py:456
  59.0 26.4 %collective-permute-start.6 = (bf16[128,1024]{1,0:T(8,128)(2,1)}, bf16[128,1024]{1,0:T(8,128)(2,1)}, u32[]{:S(2)}, u32[]{:S(2)}) collective-permute-start(bf16[128,1024]{1,0:T(8,128)(2,1)} %param.18), channel_id=1, source_target_pairs={{128,0},{130,2},{0,4},{2,6},{132,128},{134,130},{4,132},{6,134},{1... | collective-permute-start | bytes 786440 | tf_op jit(solution)/shard_map/ppermute | solution.py:456
  59.0 26.4 %collective-permute-start.7 = (bf16[128,1024]{1,0:T(8,128)(2,1)}, bf16[128,1024]{1,0:T(8,128)(2,1)}, u32[]{:S(2)}, u32[]{:S(2)}) collective-permute-start(bf16[128,1024]{1,0:T(8,128)(2,1)} %param.18), channel_id=1, source_target_pairs={{130,0},{128,2},{2,4},{0,6},{134,128},{132,130},{6,132},{4,134},{1... | collective-permute-start | bytes 786440 | tf_op jit(solution)/shard_map/ppermute | solution.py:456
  67.4 15.8 %all-to-all-start.1 = ((bf16[16,2,32,128]{3,2,1,0:T(8,128)(2,1)}), bf16[16,2,32,128]{3,2,1,0:T(8,128)(2,1)}, u32[]{:S(2)}, u32[]{:S(2)}) async-start(bf16[16,2,32,128]{3,2,1,0:T(8,128)(2,1)} %get-tuple-element.38), calls=%async_computation.1 | async-start | bytes 524288 | tf_op jit(solution)/shard_map/all_to_all | solution.py:399
  72.9 91.3 %reduce-scatter.2.cloned.1.call-start = ((), (), s32[]{:S(2)}) async-start(), calls=%async_computation.5 | async-start | bytes 2359296 | tf_op jit(solution)/shard_map/reduce_scatter | solution.py:486
  74.5 7.7 %collective-permute-start.2 = (bf16[32,1024]{1,0:T(8,128)(2,1)S(1)}, bf16[32,1024]{1,0:T(8,128)(2,1)S(1)}, u32[]{:S(2)}, u32[]{:S(2)}) collective-permute-start(bf16[32,1024]{1,0:T(8,128)(2,1)S(1)} %pad_maximum_fusion.2), channel_id=1, source_target_pairs={{8,0},{16,8},{24,16},{32,24},{40,32},{48,40},{56,48},{64,56},{72,6... | collective-permute-start | bytes 196616 | tf_op jit(solution)/shard_map/ppermute | solution.py:452
  82.2 31.2 %copy-start.1 = (bf16[32,1024]{1,0:T(8,128)(2,1)}, bf16[32,1024]{1,0:T(8,128)(2,1)S(1)}, u32[]{:S(2)}) copy-start(bf16[32,1024]{1,0:T(8,128)(2,1)S(1)} %collective-permute-done.2.beyond) | copy-start | bytes 196612
  86.8 1.0 copy-start
  87.8 4.9 %collective-permute-start.8 = (bf16[4,128,1024]{2,1,0:T(8,128)(2,1)S(1)}, bf16[4,128,1024]{2,1,0:T(8,128)(2,1)}, u32[]{:S(2)}, u32[]{:S(2)}) collective-permute-start(bf16[4,128,1024]{2,1,0:T(8,128)(2,1)S(1)} %pad_maximum_fusion.cot), channel_id=1, source_target_pairs={{0,1},{1,0},{2,3},{3,2},{4,5},{5,4},{6,7},{7,6},{8,9},{9,8},{10,11... | collective-permute-start | bytes 3145736 | tf_op jit(solution)/shard_map/ppermute | solution.py:395
  87.8 19.0 %collective-permute-start.3 = (bf16[2,128,512]{2,1,0:T(8,128)(2,1)}, bf16[2,128,512]{2,1,0:T(8,128)(2,1)}, u32[]{:S(2)}, u32[]{:S(2)}) collective-permute-start(bf16[2,128,512]{2,1,0:T(8,128)(2,1)} %get-tuple-element.40.product), channel_id=1, source_target_pairs={{0,128},{128,0},{1,129},{129,1},{2,130},{130,2},{3,131},{131,3},{4... | collective-permute-start | bytes 786440 | tf_op jit(solution)/shard_map/ppermute | solution.py:395
  101.0 19.8 %collective-permute-start.10 = (bf16[2,128,512]{2,1,0:T(8,128)(2,1)}, bf16[2,128,512]{2,1,0:T(8,128)(2,1)}, u32[]{:S(2)}, u32[]{:S(2)}) collective-permute-start(bf16[2,128,512]{2,1,0:T(8,128)(2,1)} %get-tuple-element.46), channel_id=1, source_target_pairs={{0,128},{128,0},{1,129},{129,1},{2,130},{130,2},{3,131},{131,3},{4... | collective-permute-start | bytes 786440 | tf_op jit(solution)/shard_map/ppermute | solution.py:395
  123.2 11.9 %collective-permute-start.11 = (bf16[2,16,512]{2,1,0:T(8,128)(2,1)}, bf16[2,16,512]{2,1,0:T(8,128)(2,1)S(1)}, u32[]{:S(2)}, u32[]{:S(2)}) collective-permute-start(bf16[2,16,512]{2,1,0:T(8,128)(2,1)} %get-tuple-element.54), channel_id=1, source_target_pairs={{8,0},{16,8},{24,16},{32,24},{40,32},{48,40},{56,48},{64,56},{72,6... | collective-permute-start | bytes 98312 | tf_op jit(solution)/shard_map/ppermute | solution.py:492
  125.2 17.4 %all-to-all-start.2 = ((bf16[16,2,32,128]{3,2,1,0:T(8,128)(2,1)}), bf16[16,2,32,128]{3,2,1,0:T(8,128)(2,1)}, u32[]{:S(2)}, u32[]{:S(2)}) async-start(bf16[16,2,32,128]{3,2,1,0:T(8,128)(2,1)} %get-tuple-element.51), calls=%async_computation.3 | async-start | bytes 524288 | tf_op jit(solution)/shard_map/all_to_all | solution.py:399
  137.3 15.1 %collective-permute-start.12 = (bf16[144,512]{1,0:T(8,128)(2,1)}, bf16[144,512]{1,0:T(8,128)(2,1)}, u32[]{:S(2)}, u32[]{:S(2)}) collective-permute-start(bf16[144,512]{1,0:T(8,128)(2,1)} %pad_maximum_fusion.1), channel_id=1, source_target_pairs={{0,128},{128,0},{1,129},{129,1},{2,130},{130,2},{3,131},{131,3},{4... | collective-permute-start | bytes 442376 | tf_op jit(solution)/shard_map/ppermute | solution.py:395
  152.4 24.3 %all-to-all-start.3 = ((bf16[32,48,128]{2,1,0:T(8,128)(2,1)}), bf16[32,48,128]{2,1,0:T(8,128)(2,1)}, u32[]{:S(2)}, u32[]{:S(2)}) async-start(bf16[32,48,128]{2,1,0:T(8,128)(2,1)} %get-tuple-element.55), calls=%async_computation.4 | async-start | bytes 786432 | tf_op jit(solution)/shard_map/all_to_all | solution.py:505
  164.2 15.8 %collective-permute-start.9 = (bf16[128,1024]{1,0:T(8,128)(2,1)}, bf16[128,1024]{1,0:T(8,128)(2,1)}, u32[]{:S(2)}, u32[]{:S(2)}) collective-permute-start(bf16[128,1024]{1,0:T(8,128)(2,1)} %bitcast.25), channel_id=1, source_target_pairs={{0,0},{2,2},{4,128},{6,130},{128,4},{130,6},{132,132},{134,134},{1... | collective-permute-start | bytes 786440 | tf_op jit(solution)/shard_map/ppermute | solution.py:508
Sparse Core Ops, SparseCore 0:
  10.4 83.2 all-gather.2
  113.6 49.8 reduce-scatter.1
